TPU v7x, 32 devices: a whole 2x2x4 slice. The times are simulated.
32 devices in a mesh: sample: 2 (over x), stretch: 4 (over z), band: 4 (over y, core).
Axes of the slice: x: 2, y: 2, z: 4, core: 2. Of those that a mesh axis runs over, the one named last changes fastest.
Arguments:
- latents: bfloat16 [32, 8, 16, 128], P('sample', 'stretch', 'band'), may hold values from -6 to 6
- lengths: int32 [32], replicated, may hold values from 1 to 8, as said below
- dest_slot: int32 [32], replicated, may hold values from 0 to 31, as said below
- w_in: bfloat16 [432, 384], replicated, may hold values from -0.3125 to 0.3125
- b_in: float32 [384], replicated, may hold values from -3 to 3
- gain_mid: float32 [384], replicated, may hold values from 0.25 to 1.75
- w_mid: bfloat16 [10368, 384], replicated, may hold values from -0.0625 to 0.0625
- b_mid: float32 [384], replicated, may hold values from -3 to 3
- w_proj: bfloat16 [384, 1536], replicated, may hold values from -0.3125 to 0.3125
- gain_tok: float32 [1536], replicated, may hold values from 0.25 to 1.75
- w_gate: bfloat16 [1536, 8960], P('sample', ('stretch', 'band')), may hold values from -0.15625 to 0.15625
- w_up: bfloat16 [1536, 8960], P('sample', ('stretch', 'band')), may hold values from -0.15625 to 0.15625
- w_down: bfloat16 [8960, 1536], P(('stretch', 'band'), 'sample'), may hold values from -0.0625 to 0.0625
- w_score: float32 [1536], replicated, may hold values from -0.15625 to 0.15625
Outputs:
- decoded: bfloat16 [32, 8, 16, 3072], P('sample', 'stretch', 'band')
- scores: float32 [32], replicated
Inputs may be any that keep to these rules, and one draw needn't show every extreme that they name: `lengths`: every clip has 1 or more frames; some clip has 8. `dest_slot`: a permutation; slot k belongs to decoder group k // 16; diffusion group g (clips g * 16 onward) sends exactly 8 clips to every decoder group, into that group's slots g * 8 to g * 8 + 7.
All inputs are finite; a program needn't handle non-finite values.
Results may differ from a plain program's by a relative error of at most 0.0085.
Values may be sent and summed in bfloat16 or wider, within the bound.
No kernel may reach another device: no remote copies, remote signals or barrier semaphores. Data moves between devices by JAX's collectives and lax.ppermute only.
A program may use at most 128 MiB of HBM per device.

v0:
```python
import jax
import jax.numpy as jnp
from jax import lax
from jax.sharding import PartitionSpec as P


def with_halo(cells, sides, width):
    for axis, dim in sides:
        count = lax.axis_size(axis)
        ends = count - 1
        head = lax.slice_in_dim(cells, 0, width, axis=dim)
        tail = lax.slice_in_dim(cells, cells.shape[dim] - width, cells.shape[dim], axis=dim)
        cells = jnp.concatenate(
            [
                lax.ppermute(tail, axis, [(i, (i + 1) % count) for i in range(ends)]),
                cells,
                lax.ppermute(head, axis, [((i + 1) % count, i) for i in range(ends)]),
            ],
            axis=dim,
        )
    return cells


def from_behind(block, axis, distance):
    devices = range(lax.axis_size(axis))
    route = [(i - distance, i) for i in devices if i - distance in devices]
    return lax.ppermute(block, axis, route)


def conv_taps(extended, weight, frames_out, rows_out, cols_out):
    clip_total = extended.shape[0]
    chans_in = extended.shape[-1]
    running_sum = jnp.zeros(
        (clip_total * frames_out * rows_out * cols_out, weight.shape[1]), jnp.float32
    )
    for shift_t in range(3):
        windows = []
        for remain in range(9):
            shift_r, shift_c = divmod(remain, 3)
            windows.append(
                extended[
                    :,
                    shift_t : shift_t + frames_out,
                    shift_r : shift_r + rows_out,
                    shift_c : shift_c + cols_out,
                    :,
                ]
            )
        stacked = jnp.concatenate(windows, axis=-1).reshape(-1, 9 * chans_in)
        rows_w = weight[shift_t * 9 * chans_in : (shift_t + 1) * 9 * chans_in]
        running_sum = running_sum + jnp.dot(stacked, rows_w, preferred_element_type=jnp.float32)
    return running_sum.reshape(clip_total, frames_out, rows_out, cols_out, -1)


def activate(first_out, gain_mid):
    values = first_out.astype(jnp.float32)
    scaled = (
        values * lax.rsqrt(jnp.mean(values * values, axis=-1, keepdims=True) + 1e-06) * gain_mid
    )
    return jax.nn.silu(scaled).astype(jnp.bfloat16)


def latent_rim(block_cells):
    padded = with_halo(block_cells, (("band", 2),), 1)
    return jnp.pad(padded, ((0, 0), (0, 0), (0, 0), (1, 1), (0, 0)))


def feature_rim(block_cells):
    padded = with_halo(block_cells, (("band", 2),), 1)
    return jnp.pad(padded, ((0, 0), (0, 0), (0, 0), (1, 1), (0, 0)))


def body(
    latents,
    lengths,
    dest_slot,
    w_in,
    b_in,
    gain_mid,
    w_mid,
    b_mid,
    w_proj,
    gain_tok,
    w_gate,
    w_up,
    w_down,
    w_score,
):
    clip_count = latents.shape[0]
    frames = latents.shape[1]
    row_count = latents.shape[2]
    chans_lat = w_in.shape[0] // 27
    widths = latents.shape[3] // chans_lat
    group_index = lax.axis_index("sample")
    stretch_pos = lax.axis_index("stretch")
    all_clips = dest_slot.shape[0]
    inverse = (
        jnp.zeros((all_clips,), jnp.int32).at[dest_slot].set(jnp.arange(all_clips, dtype=jnp.int32))
    )
    my_clips = lax.dynamic_slice_in_dim(inverse, group_index * clip_count, clip_count)
    my_lengths = lengths[my_clips]
    block_piece = lax.all_gather(latents, "sample", axis=0, tiled=True)
    wanted = jnp.arange(block_piece.shape[0], dtype=jnp.int32)
    select = (my_clips[:, None] == wanted[None, :]).astype(jnp.bfloat16)
    arrived = jnp.dot(
        select, block_piece.reshape(block_piece.shape[0], -1), preferred_element_type=jnp.float32
    )
    arrived = arrived.astype(jnp.bfloat16).reshape(latents.shape)
    frame_ids = stretch_pos * frames + jnp.arange(frames, dtype=jnp.int32)
    valid_frames = frame_ids[None, :] < my_lengths[:, None]
    latent_cells = arrived.reshape(clip_count, frames, row_count, widths, chans_lat)
    latent_cells = jnp.where(
        valid_frames[:, :, None, None, None], latent_cells, jnp.zeros((), jnp.bfloat16)
    )
    earlier = from_behind(latent_cells, "stretch", 1)
    first_in = latent_rim(jnp.concatenate([earlier, latent_cells], axis=1))
    first_out = (conv_taps(first_in, w_in, frames, row_count, widths) + b_in).astype(jnp.bfloat16)
    hidden_in = activate(first_out, gain_mid)
    before = from_behind(hidden_in, "stretch", 1)
    extended = jnp.concatenate([before, hidden_in], axis=1)
    second = conv_taps(feature_rim(extended), w_mid, frames, row_count, widths)
    mixed_out = first_out.astype(jnp.float32) + second + b_mid
    decoded = jnp.where(valid_frames[:, :, None, None, None], mixed_out, 0.0).astype(jnp.bfloat16)
    band_sum = jnp.sum(decoded.astype(jnp.float32), axis=(2, 3))
    pooled = lax.psum(band_sum, "band") / (row_count * lax.axis_size("band") * widths)
    tokens_here = jnp.dot(
        pooled.astype(jnp.bfloat16).reshape(-1, pooled.shape[-1]),
        w_proj,
        preferred_element_type=jnp.float32,
    )
    tokens_here = tokens_here.astype(jnp.bfloat16).reshape(clip_count, frames, -1)
    tokens = lax.all_gather(tokens_here, "stretch", axis=1, tiled=True)
    decoded_out = decoded.reshape(clip_count, frames, row_count, -1)
    all_frames = tokens.shape[1]
    tokens = tokens.reshape(clip_count * all_frames, -1)
    token_f = tokens.astype(jnp.float32)
    normed = (
        token_f * lax.rsqrt(jnp.mean(token_f * token_f, axis=-1, keepdims=True) + 1e-06) * gain_tok
    ).astype(jnp.bfloat16)
    gate_sum = jnp.dot(
        normed,
        lax.all_gather(w_gate, "sample", axis=0, tiled=True),
        preferred_element_type=jnp.float32,
    )
    up_sum = jnp.dot(
        normed,
        lax.all_gather(w_up, "sample", axis=0, tiled=True),
        preferred_element_type=jnp.float32,
    )
    hidden = (jax.nn.silu(gate_sum) * up_sum).astype(jnp.bfloat16)
    partial_down = jnp.dot(
        hidden,
        lax.all_gather(w_down, "sample", axis=1, tiled=True),
        preferred_element_type=jnp.float32,
    )
    branch = jnp.sum(partial_down * w_score, axis=-1)
    branch_total = lax.psum(branch, ("stretch", "band"))
    token_scores = jnp.sum(token_f * w_score, axis=-1) + branch_total
    token_scores = token_scores.reshape(clip_count, all_frames)
    live_frames = jnp.arange(all_frames, dtype=jnp.int32)[None, :] < my_lengths[:, None]
    clip_scores = jnp.sum(jnp.where(live_frames, token_scores, 0.0), axis=1) / my_lengths.astype(
        jnp.float32
    )
    every_score = lax.all_gather(clip_scores, "sample", axis=0, tiled=True)
    scores = every_score[dest_slot]
    return (decoded_out, scores)


def solution(mesh):
    in_specs = (
        P("sample", "stretch", "band", None),
        P(),
        P(),
        P(),
        P(),
        P(),
        P(),
        P(),
        P(),
        P(),
        P("sample", ("stretch", "band")),
        P("sample", ("stretch", "band")),
        P(("stretch", "band"), "sample"),
        P(),
    )
    out_specs = (P("sample", "stretch", "band", None), P())
    return jax.shard_map(body, mesh=mesh, in_specs=in_specs, out_specs=out_specs, check_vma=False)
```

profile of v0, /device:TPU:0, one launch (start us, length us, event | category | flops | bytes accessed | tf_op | source)
XLA Modules:
  0.0 210.0 jit_solution(8314424271124307847)
XLA Ops:
  8.0 5.8 %all_gather.18 = bf16[32,2,4,128]{3,2,1,0:T(4,128)(2,1)S(1)} all-gather(bf16[16,2,4,128]{3,2,1,0:T(4,128)(2,1)} %param.14), channel_id=1, replica_groups=mesh['sample'=2,'stretch'=4,'band'=4] {'sample'}, dimensions={0}, use_global_device_ids=true | all-gather | bytes 98304 | tf_op jit(solution)/shard_map/all_gather | solution.py:102
  18.2 4.0 %collective-permute-start = (bf16[16,2,4,8,16]{4,3,2,1,0:T(8,128)(2,1)S(1)}, bf16[16,2,4,8,16]{4,3,2,1,0:T(8,128)(2,1)S(1)}, u32[]{:S(2)}, u32[]{:S(2)}) collective-permute-start(bf16[16,2,4,8,16]{4,3,2,1,0:T(8,128)(2,1)S(1)} %broadcast_select_fusion), channel_id=1, source_target_pairs={{0,4},{4,8},{8,12},{1,5},{5,9},{9,13},{2,6},{6,10},{10,14},{3,7},{... | collective-permute-start | bytes 98312 | tf_op jit(solution)/shard_map/ppermute | solution.py:27
  22.2 4.3 %collective-permute-done = bf16[16,2,4,8,16]{4,3,2,1,0:T(8,128)(2,1)S(1)} collective-permute-done((bf16[16,2,4,8,16]{4,3,2,1,0:T(8,128)(2,1)S(1)}, bf16[16,2,4,8,16]{4,3,2,1,0:T(8,128)(2,1)S(1)}, u32[]{:S(2)}, u32[]{:S(2)}) %collective-permute-start) | collective-permute-done | bytes 32800 | tf_op jit(solution)/shard_map/ppermute | solution.py:27
  29.3 3.6 %collective-permute-done.2 = bf16[16,4,1,8,16]{4,3,2,1,0:T(8,128)(2,1)S(1)} collective-permute-done((bf16[16,4,1,8,16]{4,3,2,1,0:T(8,128)(2,1)S(1)}, bf16[16,4,1,8,16]{4,3,2,1,0:T(8,128)(2,1)S(1)}, u32[]{:S(2)}, u32[]{:S(2)}) %collective-permute-start.2) | collective-permute-done | bytes 16416 | tf_op jit(solution)/shard_map/ppermute | solution.py:17
  33.7 2.3 %fusion.56 = (bf16[16,2,4,8,16]{4,3,2,1,0:T(8,128)(2,1)S(1)}, bf16[16,2,4,8,16]{4,3,2,1,0:T(8,128)(2,1)S(1)}, bf16[16,2,4,8,16]{4,3,2,1,0:T(8,128)(2,1)S(1)}, bf...) fusion(bf16[16,4,6,10,16]{4,3,2,1,0:T(8,128)(2,1)S(1)} %select_, ...), kind=kLoop, calls=%fused_computation.127 | loop fusion | bytes 1179648 | tf_op jit(solution)/shard_map/slice | solution.py:41
  37.4 3.3 %concatenate.55 = bf16[16,2,4,8,144]{4,3,2,1,0:T(8,128)(2,1)S(1)} concatenate(bf16[16,2,4,8,16]{4,3,2,1,0:T(8,128)(2,1)} %get-tuple-element.45, bf16[16,2,4,8,16]{4,3,2,1,0:T(8,128)(2,1)} %get-tuple-element.70, bf16[16,2,4,8,16]{4,3,2,1,0:T(8,128)(2,1)} %get-tuple-element.44, bf16[16,2,4,8,16]{4,3,2,1,0:T(8,128)(2,1)} %get-tuple-element.43, ...), dimensions={4} | concatenate | bytes 589824 | tf_op jit(solution)/shard_map/concatenate | solution.py:49
  40.7 2.5 %fusion.44 = f32[1024,384]{1,0:T(8,128)} fusion(bf16[1024,144]{1,0:T(8,128)(2,1)S(1)} %bitcast.37, bf16[432,384]{1,0:T(8,128)(2,1)} %param.17), kind=kOutput, calls=%fused_computation.103 | convolution fusion | flops 113246208 | bytes 1978368 | tf_op jit(solution)/shard_map/dot_general | solution.py:51
  43.2 3.3 %concatenate.54 = bf16[16,2,4,8,144]{4,3,2,1,0:T(8,128)(2,1)S(1)} concatenate(bf16[16,2,4,8,16]{4,3,2,1,0:T(8,128)(2,1)} %get-tuple-element.51, bf16[16,2,4,8,16]{4,3,2,1,0:T(8,128)(2,1)} %get-tuple-element.69, bf16[16,2,4,8,16]{4,3,2,1,0:T(8,128)(2,1)} %get-tuple-element.50, bf16[16,2,4,8,16]{4,3,2,1,0:T(8,128)(2,1)} %get-tuple-element.49, ...), dimensions={4} | concatenate | bytes 589824 | tf_op jit(solution)/shard_map/concatenate | solution.py:49
  46.5 2.5 %fusion.46 = f32[1024,384]{1,0:T(8,128)} fusion(bf16[1024,144]{1,0:T(8,128)(2,1)S(1)} %bitcast.38, bf16[432,384]{1,0:T(8,128)(2,1)} %param.17), kind=kOutput, calls=%fused_computation.105 | convolution fusion | flops 113246208 | bytes 1978368 | tf_op jit(solution)/shard_map/dot_general | solution.py:51
  48.9 3.7 %concatenate.56 = bf16[16,2,4,8,144]{4,3,2,1,0:T(8,128)(2,1)S(1)} concatenate(bf16[16,2,4,8,16]{4,3,2,1,0:T(8,128)(2,1)} %get-tuple-element.39, bf16[16,2,4,8,16]{4,3,2,1,0:T(8,128)(2,1)} %get-tuple-element.71, bf16[16,2,4,8,16]{4,3,2,1,0:T(8,128)(2,1)} %get-tuple-element.38, bf16[16,2,4,8,16]{4,3,2,1,0:T(8,128)(2,1)} %get-tuple-element.37, ...), dimensions={4} | concatenate | bytes 589824 | tf_op jit(solution)/shard_map/concatenate | solution.py:49
  52.6 2.4 %multiply_reduce_fusion = (f32[1024]{0:T(1024)S(1)}, f32[1024,384]{1,0:T(8,128)S(1)}) fusion(f32[384]{0:T(512)S(1)} %copy-done.6, bf16[1024,144]{1,0:T(8,128)(2,1)S(1)} %bitcast.36, bf16[432,384]{1,0:T(8,128)(2,1)} %param.17, f32[1024,384]{1,0:T(8,128)} %fusion.46, f32[1024,384]{1,0:T(8,128)} %fusion.44), kind=kOutput, calls=%fused_computation.44 | convolution fusion | flops 115997696 | bytes 5129728 | tf_op jit(solution)/shard_map/dot_general | solution.py:51
  55.8 1.4 fusion.17
  57.2 4.4 %collective-permute-start.3 = (bf16[16,2,4,8,384]{4,3,2,1,0:T(8,128)(2,1)S(1)}, bf16[16,2,4,8,384]{4,3,2,1,0:T(8,128)(2,1)S(1)}, u32[]{:S(2)}, u32[]{:S(2)}) collective-permute-start(bf16[16,2,4,8,384]{4,3,2,1,0:T(8,128)(2,1)S(1)} %fusion.17), channel_id=1, source_target_pairs={{0,4},{4,8},{8,12},{1,5},{5,9},{9,13},{2,6},{6,10},{10,14},{3,7},{... | collective-permute-start | bytes 2359304 | tf_op jit(solution)/shard_map/ppermute | solution.py:27
  61.6 14.7 %collective-permute-done.3 = bf16[16,2,4,8,384]{4,3,2,1,0:T(8,128)(2,1)S(1)} collective-permute-done((bf16[16,2,4,8,384]{4,3,2,1,0:T(8,128)(2,1)S(1)}, bf16[16,2,4,8,384]{4,3,2,1,0:T(8,128)(2,1)S(1)}, u32[]{:S(2)}, u32[]{:S(2)}) %collective-permute-start.3) | collective-permute-done | bytes 786464 | tf_op jit(solution)/shard_map/ppermute | solution.py:27
  78.2 5.9 %collective-permute-start.4 = (bf16[16,4,1,8,384]{4,3,2,1,0:T(8,128)(2,1)}, bf16[16,4,1,8,384]{4,3,2,1,0:T(8,128)(2,1)}, u32[]{:S(2)}, u32[]{:S(2)}) collective-permute-start(bf16[16,4,1,8,384]{4,3,2,1,0:T(8,128)(2,1)} %get-tuple-element.32), channel_id=1, source_target_pairs={{0,1},{1,2},{2,3},{4,5},{5,6},{6,7},{8,9},{9,10},{10,11},{12,13},{... | collective-permute-start | bytes 1179656 | tf_op jit(solution)/shard_map/ppermute | solution.py:15
  92.4 1.7 reshape.134
  94.1 4.1 %select_maximum_fusion = bf16[16,4,6,10,384]{4,3,2,1,0:T(8,128)(2,1)S(1)} fusion(bf16[16,4,1,8,384]{4,3,2,1,0:T(8,128)(2,1)} %collective-permute-done.5, bf16[16,4,1,8,384]{4,3,2,1,0:T(8,128)(2,1)} %collective-permute-done.4, bf16[16,2,4,8,384]{4,3,2,1,0:T(8,128)(2,1)S(1)} %fusion.17, bf16[16,2,4,8,384]{4,3,2,1,0:T(8,128)(2,1)} %copy-done.1), kind=kLoop, calls=%fused_computation.8 | loop fusion | flops 22118400 | bytes 5308416 | tf_op jit(solution)/shard_map/concatenate | solution.py:13
  99.3 1.7 pad_maximum_fusion
  103.3 2.9 %copy-done.4 = bf16[16,2,4,8,3456]{4,3,2,1,0:T(8,128)(2,1)} copy-done((bf16[16,2,4,8,3456]{4,3,2,1,0:T(8,128)(2,1)}, bf16[16,2,4,8,3456]{4,3,2,1,0:T(8,128)(2,1)S(1)}, u32[]{:S(2)}) %copy-start.4) | copy-done | bytes 7077912
  106.2 1.5 slice_dynamic-update-slice_fusion.3
  110.3 1.5 slice_dynamic-update-slice_fusion
  111.8 3.9 %fusion.7 = f32[1024,384]{1,0:T(8,128)S(1)} fusion(bf16[1024,3456]{1,0:T(8,128)(2,1)S(1)} %bitcast.41, bf16[10368,384]{1,0:T(8,128)(2,1)S(1)} %bitcast.40), kind=kOutput, calls=%fused_computation.16 | convolution fusion | flops 2717908992 | bytes 11304960 | tf_op jit(solution)/shard_map/dot_general | solution.py:51
  115.7 6.1 %fusion.9 = f32[1024,384]{1,0:T(8,128)S(1)} fusion(bf16[1024,3456]{1,0:T(8,128)(2,1)} %bitcast.42, bf16[10368,384]{1,0:T(8,128)(2,1)S(1)} %bitcast.40), kind=kOutput, calls=%fused_computation.18 | convolution fusion | flops 2717908992 | bytes 11304960 | tf_op jit(solution)/shard_map/dot_general | solution.py:51
  121.8 5.4 %convert_reduce_fusion = (f32[16,2,384]{2,1,0:T(2,128)S(1)}, f32[1024,384]{1,0:T(8,128)}) fusion(f32[384]{0:T(512)S(1)} %copy-done.9, pred[16,2]{1,0:T(8,128)(4,1)S(1)} %copy-done.8, f32[384]{0:T(512)S(1)} %copy-done.6, f32[1024,384]{1,0:T(8,128)S(1)} %get-tuple-element.66, bf16[1024,3456]{1,0:T(8,128)(2,1)S(1)} %bitcast.35, ...), kind=kOutput, calls=%fused_computation.41 | convolution fusion | flops 2722222080 | bytes 16078848 | tf_op jit(solution)/shard_map/dot_general | solution.py:51
  127.2 11.9 %psum.14 = f32[16,2,384]{2,1,0:T(2,128)S(1)} all-reduce(f32[16,2,384]{2,1,0:T(2,128)S(1)} %get-tuple-element.67), channel_id=1, replica_groups=mesh['sample'=2,'stretch'=4,'band'=4] {'band'}, use_global_device_ids=true, to_apply=%region_3.4 | all-reduce | flops 12288 | bytes 98304 | tf_op jit(solution)/shard_map/psum | solution.py:125
  139.5 15.3 %all_gather.19 = bf16[16,8,1536]{2,0,1:T(8,128)(2,1)S(1)} all-gather(bf16[16,2,1536]{2,0,1:T(8,128)(2,1)S(1)} %copy.17), channel_id=1, replica_groups=mesh['sample'=2,'stretch'=4,'band'=4] {'stretch'}, dimensions={1}, use_global_device_ids=true | all-gather | bytes 491520 | tf_op jit(solution)/shard_map/all_gather | solution.py:132
  155.5 2.7 %reshape.139 = f32[16,2,4,3072]{3,2,1,0:T(4,128)} reshape(f32[1024,384]{1,0:T(8,128)} %get-tuple-element.68) | data formatting | bytes 3145728 | tf_op jit(solution)/shard_map/reshape | solution.py:52
  158.2 3.0 %select_convert_fusion = bf16[16,2,4,3072]{3,2,1,0:T(4,128)(2,1)} fusion(f32[16,2,4,3072]{3,2,1,0:T(4,128)} %reshape.139, f32[16,2,4,3072]{3,2,1,0:T(4,128)S(1)} %copy-done.3, f32[3072]{0:T(1024)S(1)} %copy-done.5, f32[3072]{0:T(1024)S(1)} %add.128, pred[16,2]{1,0:T(8,128)(4,1)S(1)} %copy-done.8), kind=kLoop, calls=%fused_computation.42 | loop fusion | flops 2752512 | bytes 3956768 | tf_op jit(solution)/shard_map/convert_element_type | solution.py:123
  161.3 2.2 %fusion.50 = f32[128,560]{0,1:T(8,128)S(1)} fusion(bf16[1536,560]{0,1:T(8,128)(2,1)} %all-gather.4.cloned.1.call-done, f32[1536]{0:T(1024)S(1)} %copy-done.15, f32[128]{0:T(128)S(1)} %rsqrt.25, bf16[16,8,1536]{2,0,1:T(8,128)(2,1)S(1)} %all_gather.19), kind=kOutput, calls=%fused_computation.107 | convolution fusion | flops 220987392 | bytes 2406912 | tf_op jit(solution)/shard_map/dot_general | solution.py:140
  163.5 3.8 %fusion.26 = f32[128]{0:T(128)S(1)} fusion(bf16[560,1536]{1,0:T(8,128)(2,1)} %all-gather.8.cloned.1.call-done, bf16[1536,560]{0,1:T(8,128)(2,1)} %all-gather.6.cloned.1.call-done, f32[1536]{0:T(1024)S(1)} %copy-done.10, f32[128,560]{0,1:T(8,128)S(1)} %fusion.50, f32[1536]{0:T(1024)S(1)} %copy-done.15, f32[128]{0:T(128)S(1)} %rsqrt.25, ...), kind=kOutput, calls=%fused_computation.49 | convolution fusion | flops 442011520 | bytes 4133888 | tf_op jit(solution)/shard_map/dot_general | solution.py:151
  167.3 29.5 %psum.15 = f32[128]{0:T(128)S(1)} all-reduce(f32[128]{0:T(128)S(1)} %fusion.26), channel_id=1, replica_groups=mesh['sample'=2,'stretch'=4,'band'=4] {'stretch','band'}, use_global_device_ids=true, to_apply=%region_7.8 | all-reduce | flops 128 | bytes 1024 | tf_op jit(solution)/shard_map/psum | solution.py:157
  197.2 4.9 %all-reduce.2 = f32[32]{0:T(128)S(1)} all-reduce(f32[32]{0:T(128)S(1)} %divide_dynamic-update-slice_fusion), channel_id=1, replica_groups=mesh['sample'=2,'stretch'=4,'band'=4] {'sample'}, use_global_device_ids=true, to_apply=%add.2 | all-reduce | flops 32 | bytes 256
  (99 shorter events, 29.1 us)
Async XLA Ops:
  7.2 132.0 %copy-start = (bf16[384,1536]{1,0:T(8,128)(2,1)S(1)}, bf16[384,1536]{1,0:T(8,128)(2,1)}, u32[]{:S(2)}) copy-start(bf16[384,1536]{1,0:T(8,128)(2,1)} %param.22) | copy-start | bytes 3538948
  7.2 154.1 %all-gather.4.cloned.1.call-start = ((), (), s32[]{:S(2)}) async-start(), calls=%async_computation | async-start | bytes 2580480 | tf_op jit(solution)/shard_map/all_gather | solution.py:142
  7.9 155.5 %all-gather.6.cloned.1.call-start = ((), (), s32[]{:S(2)}) async-start(), calls=%async_computation.1 | async-start | bytes 2580480 | tf_op jit(solution)/shard_map/all_gather | solution.py:147
  14.4 0.8 copy-start.14
  16.9 0.5 copy-start.11
  17.6 0.6 copy-start.7
  18.2 8.4 %collective-permute-start = (bf16[16,2,4,8,16]{4,3,2,1,0:T(8,128)(2,1)S(1)}, bf16[16,2,4,8,16]{4,3,2,1,0:T(8,128)(2,1)S(1)}, u32[]{:S(2)}, u32[]{:S(2)}) collective-permute-start(bf16[16,2,4,8,16]{4,3,2,1,0:T(8,128)(2,1)S(1)} %broadcast_select_fusion), channel_id=1, source_target_pairs={{0,4},{4,8},{8,12},{1,5},{5,9},{9,13},{2,6},{6,10},{10,14},{3,7},{... | collective-permute-start | bytes 98312 | tf_op jit(solution)/shard_map/ppermute | solution.py:27
  22.2 141.3 %all-gather.8.cloned.1.call-start = ((), (), s32[]{:S(2)}) async-start(), calls=%async_computation.2 | async-start | bytes 2580480 | tf_op jit(solution)/shard_map/all_gather | solution.py:153
  26.6 2.7 %collective-permute-start.1 = (bf16[16,4,1,8,16]{4,3,2,1,0:T(8,128)(2,1)S(1)}, bf16[16,4,1,8,16]{4,3,2,1,0:T(8,128)(2,1)S(1)}, u32[]{:S(2)}, u32[]{:S(2)}) collective-permute-start(bf16[16,4,1,8,16]{4,3,2,1,0:T(8,128)(2,1)S(1)} %get-tuple-element.63), channel_id=1, source_target_pairs={{0,1},{1,2},{2,3},{4,5},{5,6},{6,7},{8,9},{9,10},{10,11},{12,13},{... | collective-permute-start | bytes 49160 | tf_op jit(solution)/shard_map/ppermute | solution.py:15
  27.9 5.0 %collective-permute-start.2 = (bf16[16,4,1,8,16]{4,3,2,1,0:T(8,128)(2,1)S(1)}, bf16[16,4,1,8,16]{4,3,2,1,0:T(8,128)(2,1)S(1)}, u32[]{:S(2)}, u32[]{:S(2)}) collective-permute-start(bf16[16,4,1,8,16]{4,3,2,1,0:T(8,128)(2,1)S(1)} %get-tuple-element.64), channel_id=1, source_target_pairs={{1,0},{2,1},{3,2},{5,4},{6,5},{7,6},{9,8},{10,9},{11,10},{13,12},{... | collective-permute-start | bytes 49160 | tf_op jit(solution)/shard_map/ppermute | solution.py:17
  46.4 6.2 %copy-start.6 = (f32[384]{0:T(512)S(1)}, f32[384]{0:T(512)}, u32[]{:S(2)}) copy-start(f32[384]{0:T(512)} %param.18) | copy-start | bytes 4612
  52.6 3.2 %copy-start.13 = (f32[384]{0:T(512)S(1)}, f32[384]{0:T(512)}, u32[]{:S(2)}) copy-start(f32[384]{0:T(512)} %param.19) | copy-start | bytes 4612
  57.2 19.2 %collective-permute-start.3 = (bf16[16,2,4,8,384]{4,3,2,1,0:T(8,128)(2,1)S(1)}, bf16[16,2,4,8,384]{4,3,2,1,0:T(8,128)(2,1)S(1)}, u32[]{:S(2)}, u32[]{:S(2)}) collective-permute-start(bf16[16,2,4,8,384]{4,3,2,1,0:T(8,128)(2,1)S(1)} %fusion.17), channel_id=1, source_target_pairs={{0,4},{4,8},{8,12},{1,5},{5,9},{9,13},{2,6},{6,10},{10,14},{3,7},{... | collective-permute-start | bytes 2359304 | tf_op jit(solution)/shard_map/ppermute | solution.py:27
  76.4 0.9 copy-start.1
  78.2 15.9 %collective-permute-start.4 = (bf16[16,4,1,8,384]{4,3,2,1,0:T(8,128)(2,1)}, bf16[16,4,1,8,384]{4,3,2,1,0:T(8,128)(2,1)}, u32[]{:S(2)}, u32[]{:S(2)}) collective-permute-start(bf16[16,4,1,8,384]{4,3,2,1,0:T(8,128)(2,1)} %get-tuple-element.32), channel_id=1, source_target_pairs={{0,1},{1,2},{2,3},{4,5},{5,6},{6,7},{8,9},{9,10},{10,11},{12,13},{... | collective-permute-start | bytes 1179656 | tf_op jit(solution)/shard_map/ppermute | solution.py:15
  84.1 10.0 %collective-permute-start.5 = (bf16[16,4,1,8,384]{4,3,2,1,0:T(8,128)(2,1)}, bf16[16,4,1,8,384]{4,3,2,1,0:T(8,128)(2,1)}, u32[]{:S(2)}, u32[]{:S(2)}) collective-permute-start(bf16[16,4,1,8,384]{4,3,2,1,0:T(8,128)(2,1)} %get-tuple-element.33), channel_id=1, source_target_pairs={{1,0},{2,1},{3,2},{5,4},{6,5},{7,6},{9,8},{10,9},{11,10},{13,12},{... | collective-permute-start | bytes 1179656 | tf_op jit(solution)/shard_map/ppermute | solution.py:17
  98.2 1.1 copy-start.2
  103.3 2.9 %copy-start.4 = (bf16[16,2,4,8,3456]{4,3,2,1,0:T(8,128)(2,1)}, bf16[16,2,4,8,3456]{4,3,2,1,0:T(8,128)(2,1)S(1)}, u32[]{:S(2)}) copy-start(bf16[16,2,4,8,3456]{4,3,2,1,0:T(8,128)(2,1)S(1)} %get-tuple-element.54) | copy-start | bytes 21233668
  106.2 5.6 %slice-start = ((s8[7962624]{0:T(1024)(128)(4,1)}), s8[4194304]{0:T(1024)(128)(4,1)S(1)}, s32[]{:S(2)}) async-start(s8[7962624]{0:T(1024)(128)(4,1)} %bitcast.39), calls=%async_computation.3 | async-start | bytes 8388608
  109.0 2.8 %slice-start.1 = ((s8[7962624]{0:T(1024)(128)(4,1)}), s8[3768320]{0:T(1024)(128)(4,1)S(1)}, s32[]{:S(2)}) async-start(s8[7962624]{0:T(1024)(128)(4,1)} %bitcast.39), calls=%async_computation.4 | async-start | bytes 7536640
  115.7 6.1 %copy-start.8 = (pred[16,2]{1,0:T(8,128)(4,1)S(1)}, pred[16,2]{1,0:T(8,128)(4,1)}, u32[]{:S(2)}) copy-start(pred[16,2]{1,0:T(8,128)(4,1)} %copy-done.7) | copy-start | bytes 100
  115.7 6.1 %copy-start.9 = (f32[384]{0:T(512)S(1)}, f32[384]{0:T(512)}, u32[]{:S(2)}) copy-start(f32[384]{0:T(512)} %param.21) | copy-start | bytes 4612
  121.8 33.1 %copy-start.10 = (f32[1536]{0:T(1024)S(1)}, f32[1536]{0:T(1024)}, u32[]{:S(2)}) copy-start(f32[1536]{0:T(1024)} %param.27) | copy-start | bytes 18436
  127.2 31.0 %copy-start.3 = (f32[16,2,4,3072]{3,2,1,0:T(4,128)S(1)}, f32[16,2,4,3072]{3,2,1,0:T(4,128)}, u32[]{:S(2)}) copy-start(f32[16,2,4,3072]{3,2,1,0:T(4,128)} %reshape.134) | copy-start | bytes 4718596
  127.2 31.0 %copy-start.5 = (f32[3072]{0:T(1024)S(1)}, f32[3072]{0:T(1024)}, u32[]{:S(2)}) copy-start(f32[3072]{0:T(1024)} %add.142) | copy-start | bytes 36868
  155.5 5.8 %copy-start.15 = (f32[1536]{0:T(1024)S(1)}, f32[1536]{0:T(1024)}, u32[]{:S(2)}) copy-start(f32[1536]{0:T(1024)} %param.23) | copy-start | bytes 18436
  163.4 33.5 %copy-start.12 = (s32[16]{0:T(128)S(1)}, s32[16]{0:T(128)}, u32[]{:S(2)}) copy-start(s32[16]{0:T(128)} %copy-done.11) | copy-start | bytes 196
Sparse Core Ops, SparseCore 0:
  9.6 31.5 all-gather.3
  42.7 28.8 all-gather.5
  85.6 30.7 all-gather.7
where the time goes:
time: 211 us; the launch traced here: 210 us
  blocking collectives  67.4 us (32%)
  local copies, waits for them, and re-layouts  41.3 us (20%)
  matrix products  29.1 us (14%)
  waiting for transfers between devices  23.4 us (11%)
  starting transfers between devices  18.3 us (9%)
  other arithmetic  15.6 us (7%)
  between operations  14.9 us (7%)
    psum x1, blocking collectives, body(): branch_total = lax.psum(branch, ('stretch', 'band'))  29.5 us
    dot_general x6, matrix products, conv_taps(): jnp.dot(stacked, rows_w, preferred_element_type=jnp.float32)  22.6 us
    ppermute x2, waiting for transfers between devices, from_behind(): return lax.ppermute(block, axis, route)  19 us
    all_gather x1, blocking collectives, body(): tokens = lax.all_gather(tokens_here, 'stretch', axis=1, tiled=True)  15.3 us
    unnamed x45, local copies, waits for them, and re-layouts  13.1 us
    psum x1, blocking collectives, body(): lax.psum(band_sum, 'band') / (row_count * lax.axis_size('band') * widths)  11.9 us
    concatenate x4, local copies, waits for them, and re-layouts, conv_taps(): stacked = jnp.concatenate(windows, axis=-1).reshape(-1, 9 * chans_in)  11.8 us
    ppermute x2, starting transfers between devices, from_behind(): return lax.ppermute(block, axis, route)  8.4 us
  transfers between devices with their start and end apart: 9, of which 3 were waited for; matrix products, arithmetic and copies ran while one was open for 36% of the time, Pallas kernels for 0%

commit v1 on v0

v1 whole, which is shorter than its diff:
```python
import functools

import jax
import jax.numpy as jnp
from jax import lax
from jax.experimental import pallas as pl
from jax.experimental.pallas import tpu as pltpu
from jax.sharding import PartitionSpec as P

ALL = ("sample", "stretch", "band")
TAPS = 3
BEHIND = 2 * (TAPS - 1)


def decode_kernel(
    edge_ref,
    len_ref,
    *refs,
    blocks,
    frames,
    rows,
    widths,
    clips,
    chans,
):
    lat_refs = refs[:blocks]
    (w_in_ref, b_in_ref, gain_ref, w_mid_hbm, b_mid_ref, out_ref, pool_ref) = refs[
        blocks : blocks + 7
    ]
    x1_ref, wt_ref, act_ref, first_ref, acc_ref, wm_ref, sem = refs[blocks + 7 :]
    chans_lat = w_in_ref.shape[0] // 27
    lanes = widths * chans_lat
    frames_act = frames + TAPS - 1
    rows_act = rows + TAPS - 1
    per_frame = rows_act * clips
    weights_copy = pltpu.make_async_copy(w_mid_hbm, wm_ref, sem)
    weights_copy.start()

    skip = blocks * frames - (frames_act + TAPS - 1)

    def frame(index):
        return lat_refs[(index + skip) // frames], (index + skip) % frames

    for j in range(9):
        dt, dr = divmod(j, 3)
        for f in range(frames_act):
            ref, at = frame(f + dt)
            x1_ref[f * per_frame : (f + 1) * per_frame, j * lanes : (j + 1) * lanes] = ref[
                at, dr : dr + rows_act
            ].reshape(per_frame, lanes)
    wt_ref[...] = jnp.zeros_like(wt_ref)
    act_ref[:, :, 0] = jnp.zeros((frames_act, rows_act, clips, chans), jnp.bfloat16)
    act_ref[:, :, widths + 1] = jnp.zeros((frames_act, rows_act, clips, chans), jnp.bfloat16)

    def column(q, carry):
        here = pl.multiple_of(q * chans_lat, chans_lat)
        before = pl.multiple_of(jnp.maximum(q - 1, 0) * chans_lat, chans_lat)
        for j in range(9):
            wt_ref[j, pl.ds(before, chans_lat), :] = jnp.zeros((chans_lat, chans), jnp.bfloat16)
            wt_ref[j, pl.ds(here, 3 * chans_lat), :] = w_in_ref[
                j * 3 * chans_lat : (j + 1) * 3 * chans_lat, :
            ]
        weight = wt_ref[:, chans_lat : chans_lat + lanes, :].reshape(9 * lanes, chans)
        total = jnp.dot(x1_ref[...], weight, preferred_element_type=jnp.float32)
        first = (total + b_in_ref[...]).astype(jnp.bfloat16)
        values = first.astype(jnp.float32)
        square = jnp.sum(values * values, axis=-1, keepdims=True) * (1.0 / chans)
        scaled = values * lax.rsqrt(square + 1e-06) * gain_ref[...]
        half = 0.5 * scaled
        act = (half + half * jnp.tanh(half)).astype(jnp.bfloat16)
        act_ref[:, :, q + 1] = act.reshape(frames_act, rows_act, clips, chans)
        first_ref[:, :, q] = first.reshape(frames_act, rows_act, clips, chans)[
            TAPS - 1 :, 1 : 1 + rows
        ]
        return carry

    lax.fori_loop(0, widths, column, 0)

    @pl.when(edge_ref[0] == 1)
    def _():
        act_ref[:, 0] = jnp.zeros((frames_act, widths + 2, clips, chans), jnp.bfloat16)

    @pl.when(edge_ref[1] == 1)
    def _():
        act_ref[:, rows_act - 1] = jnp.zeros((frames_act, widths + 2, clips, chans), jnp.bfloat16)

    @pl.when(edge_ref[2] == 1)
    def _():
        act_ref[0 : TAPS - 1] = jnp.zeros(
            (TAPS - 1, rows_act, widths + 2, clips, chans), jnp.bfloat16
        )

    weights_copy.wait()
    cells = rows * widths * clips

    def window(t, tap):
        dt = tap // 9
        dr = (tap % 9) // 3
        dq = tap % 3
        return act_ref[t + dt, pl.ds(dr, rows), pl.ds(dq, widths)].reshape(cells, chans)

    for t in range(frames):
        acc_ref[...] = jnp.dot(
            window(t, 26), wm_ref[26 * chans : 27 * chans, :], preferred_element_type=jnp.float32
        )

        def pair(p, carry, t=t):
            both = jnp.concatenate([window(t, 2 * p), window(t, 2 * p + 1)], axis=-1)
            at = pl.multiple_of(p * 2 * chans, 2 * chans)
            acc_ref[...] += jnp.dot(
                both, wm_ref[pl.ds(at, 2 * chans), :], preferred_element_type=jnp.float32
            )
            return carry

        lax.fori_loop(0, 13, pair, 0)
        live = (edge_ref[3] + t) < len_ref[:, 0:1]
        pooled = jnp.zeros((clips, chans), jnp.float32)
        for r in range(rows):
            for q in range(widths):
                at = (r * widths + q) * clips
                mixed = (
                    first_ref[t, r, q].astype(jnp.float32)
                    + acc_ref[at : at + clips, :]
                    + b_mid_ref[...]
                )
                done = jnp.where(live, mixed, 0.0).astype(jnp.bfloat16)
                out_ref[t, r, :, q * chans : (q + 1) * chans] = done
                pooled = pooled + done.astype(jnp.float32)
        pool_ref[t] = pooled


def decode(edges, lens, blocks, w_in, b_in, gain_mid, w_mid, b_mid, frames, rows, widths):
    chans = w_in.shape[1]
    clips = blocks[0].shape[2]
    lanes = blocks[0].shape[3]
    chans_lat = lanes // widths
    frames_act = frames + TAPS - 1
    rows_act = rows + TAPS - 1
    vmem = pl.BlockSpec(memory_space=pltpu.VMEM)
    kernel = functools.partial(
        decode_kernel,
        blocks=len(blocks),
        frames=frames,
        rows=rows,
        widths=widths,
        clips=clips,
        chans=chans,
    )
    flops = 2 * frames * rows * widths * clips * chans * 27 * chans
    return pl.pallas_call(
        kernel,
        out_shape=(
            jax.ShapeDtypeStruct((frames, rows, clips, widths * chans), jnp.bfloat16),
            jax.ShapeDtypeStruct((frames, clips, chans), jnp.float32),
        ),
        in_specs=[pl.BlockSpec(memory_space=pltpu.SMEM), vmem]
        + [vmem] * len(blocks)
        + [vmem, vmem, vmem, pl.BlockSpec(memory_space=pl.ANY), vmem],
        out_specs=(vmem, vmem),
        scratch_shapes=[
            pltpu.VMEM((frames_act * rows_act * clips, 9 * lanes), jnp.bfloat16),
            pltpu.VMEM((9, lanes + 2 * chans_lat, chans), jnp.bfloat16),
            pltpu.VMEM((frames_act, rows_act, widths + 2, clips, chans), jnp.bfloat16),
            pltpu.VMEM((frames, rows, widths, clips, chans), jnp.bfloat16),
            pltpu.VMEM((rows * widths * clips, chans), jnp.float32),
            pltpu.VMEM(w_mid.shape, jnp.bfloat16),
            pltpu.SemaphoreType.DMA,
        ],
        compiler_params=pltpu.CompilerParams(vmem_limit_bytes=40 * 1024 * 1024),
        cost_estimate=pl.CostEstimate(
            flops=flops, bytes_accessed=w_mid.size * 2, transcendentals=0
        ),
    )(
        edges,
        lens,
        *blocks,
        w_in,
        b_in.reshape(1, -1),
        gain_mid.reshape(1, -1),
        w_mid,
        b_mid.reshape(1, -1),
    )


def spread(value, axes):
    count = 1
    for axis in axes:
        count *= lax.axis_size(axis)
    return lax.all_to_all(
        jnp.broadcast_to(value[None], (count,) + value.shape), axes, 0, 0, tiled=True
    )


def body(
    latents,
    lengths,
    dest_slot,
    w_in,
    b_in,
    gain_mid,
    w_mid,
    b_mid,
    w_proj,
    gain_tok,
    w_gate,
    w_up,
    w_down,
    w_score,
):
    clips, frames, rows, lanes = latents.shape
    n_sample, n_stretch, n_band = (lax.axis_size(axis) for axis in ALL)
    chans_lat = w_in.shape[0] // 27
    chans = w_in.shape[1]
    widths = lanes // chans_lat
    sends = clips // n_sample
    group = lax.axis_index("sample")
    stretch = lax.axis_index("stretch")
    band = lax.axis_index("band")
    all_clips = dest_slot.shape[0]
    frame0 = stretch * frames

    my_dest = lax.dynamic_slice_in_dim(dest_slot, group * clips, clips)
    my_len = lax.dynamic_slice_in_dim(lengths, group * clips, clips)
    target = jnp.arange(n_sample, dtype=jnp.int32)[:, None] * clips + group * sends
    target = (target + jnp.arange(sends, dtype=jnp.int32)[None, :]).reshape(-1)
    select = (target[:, None] == my_dest[None, :]).astype(jnp.bfloat16)
    frame_ids = frame0 + jnp.arange(frames, dtype=jnp.int32)
    live = frame_ids[None, :] < my_len[:, None]
    masked = jnp.where(live[:, :, None, None], latents, jnp.zeros((), jnp.bfloat16))
    routed = jnp.einsum(
        "kc,ctrl->trkl", select, masked, preferred_element_type=jnp.float32
    ).astype(jnp.bfloat16)
    routed = routed.reshape(frames, rows, n_sample, sends, lanes).transpose(2, 0, 1, 3, 4)
    outgoing = jnp.broadcast_to(
        routed[:, None], (n_sample, n_band, frames, rows, sends, lanes)
    ).reshape(n_sample * n_band, frames, rows, sends, lanes)
    got = lax.all_to_all(outgoing, ("sample", "band"), 0, 0, tiled=True)
    got = got.reshape(n_sample, n_band, frames, rows, sends, lanes)
    got = got.transpose(2, 1, 3, 0, 4, 5).reshape(frames, n_band * rows, clips, lanes)
    got = jnp.pad(got, ((0, 0), (2, 2), (0, 0), (0, 0)))
    own = lax.dynamic_slice_in_dim(got, band * rows, rows + 4, axis=1)
    hops = -(-BEHIND // frames)
    blocks = [
        lax.ppermute(own, "stretch", [(i, i + d) for i in range(n_stretch - d)])
        for d in range(hops, 0, -1)
    ] + [own]

    units = w_gate.shape[1] // n_sample

    def of_units(weight, index, axis):
        return lax.dynamic_slice_in_dim(weight, index * units, units, axis=axis)

    own_v = jnp.sum(
        w_down.astype(jnp.float32)
        * lax.dynamic_slice_in_dim(w_score, group * w_down.shape[1], w_down.shape[1])[None, :],
        axis=-1,
    )
    depth = w_gate.shape[0]
    gate_parts, up_parts, v_unit = [None], [None], of_units(own_v, group, 0)
    for d in range(1, n_sample):
        route = [(i, (i + d) % n_sample) for i in range(n_sample)]
        other = (group + d) % n_sample
        gate_parts.append(lax.ppermute(of_units(w_gate, other, 1), "sample", route))
        up_parts.append(lax.ppermute(of_units(w_up, other, 1), "sample", route))
        v_unit = v_unit + lax.ppermute(of_units(own_v, other, 0), "sample", route)
    gate_parts[0] = of_units(w_gate, group, 1)
    up_parts[0] = of_units(w_up, group, 1)

    slot_is = dest_slot[None, :] == jnp.arange(all_clips, dtype=jnp.int32)[:, None]
    len_slot = jnp.sum(jnp.where(slot_is, lengths[None, :], 0), axis=1)
    my_slots = lax.dynamic_slice_in_dim(len_slot, group * clips, clips)
    edges = jnp.stack(
        [
            (band == 0).astype(jnp.int32),
            (band == n_band - 1).astype(jnp.int32),
            (stretch == 0).astype(jnp.int32),
            frame0.astype(jnp.int32),
        ]
    )
    lens = jnp.broadcast_to(my_slots[:, None], (clips, 128))
    decoded, band_sum = decode(
        edges, lens, blocks, w_in, b_in, gain_mid, w_mid, b_mid, frames, rows, widths
    )
    decoded_out = decoded.transpose(2, 0, 1, 3)

    band_sum = band_sum.reshape(n_band, frames * clips // n_band, chans)
    parts = lax.all_to_all(band_sum, "band", 0, 0, tiled=True)
    pooled = jnp.sum(parts, axis=0) / (rows * n_band * widths)
    pooled = spread(pooled.astype(jnp.bfloat16), ALL).reshape(-1, chans)
    tokens = jnp.dot(pooled, w_proj, preferred_element_type=jnp.float32).astype(jnp.bfloat16)
    token_f = tokens.astype(jnp.float32)
    normed = (
        token_f * lax.rsqrt(jnp.mean(token_f * token_f, axis=-1, keepdims=True) + 1e-06) * gain_tok
    ).astype(jnp.bfloat16)

    def product(parts):
        total = None
        for d in range(n_sample):
            source = (group - d) % n_sample
            rows_here = lax.dynamic_slice_in_dim(normed, source * depth, depth, axis=1)
            term = jnp.dot(rows_here, parts[d], preferred_element_type=jnp.float32)
            total = term if total is None else total + term
        return total

    hidden = (jax.nn.silu(product(gate_parts)) * product(up_parts)).astype(jnp.bfloat16)
    branch = jnp.sum(hidden.astype(jnp.float32) * v_unit[None, :], axis=-1)
    at_home = jnp.sum(token_f * w_score, axis=-1)
    first_device = (group == 0) & (stretch == 0) & (band == 0)
    partial = branch + jnp.where(first_device, at_home, 0.0)
    partial = partial.reshape(n_sample, n_stretch * frames, clips)
    lens_all = len_slot.reshape(n_sample, 1, clips)
    counted = jnp.arange(n_stretch * frames, dtype=jnp.int32)[None, :, None] < lens_all
    slot_part = jnp.sum(jnp.where(counted, partial, 0.0), axis=1).reshape(-1)
    slot_part = slot_part / len_slot.astype(jnp.float32)
    clip_part = jnp.sum(jnp.where(slot_is, slot_part[:, None], 0.0), axis=0)
    scores = jnp.sum(spread(clip_part, ALL), axis=0)
    return (decoded_out, scores)


def solution(mesh):
    in_specs = (
        P("sample", "stretch", "band", None),
        P(),
        P(),
        P(),
        P(),
        P(),
        P(),
        P(),
        P(),
        P(),
        P("sample", ("stretch", "band")),
        P("sample", ("stretch", "band")),
        P(("stretch", "band"), "sample"),
        P(),
    )
    out_specs = (P("sample", "stretch", "band", None), P())
    return jax.shard_map(body, mesh=mesh, in_specs=in_specs, out_specs=out_specs, check_vma=False)
```

time: 211 us -> 90.8 us (0.43)
  blocking collectives: 67.4 us -> 0 us
  local copies, waits for them, and re-layouts: 41.3 us -> 12.6 us
  Pallas kernels: 0 us -> 25.4 us
  matrix products: 29.1 us -> 4.24 us
  between operations: 14.9 us -> 0.92 us
  other arithmetic: 15.6 us -> 3.58 us
  starting transfers between devices: 18.3 us -> 27.1 us
  waiting for transfers between devices: 23.4 us -> 16.2 us
    psum x2 -> x0, blocking collectives: 41.4 us -> none  [the longest x1 29.5 us: body(): branch_total = lax.psum(branch, ('stretch', 'band'))]
    pallas_call x0 -> x1, Pallas kernels: none -> 25.4 us  [decode(): pl.pallas_call(kernel, out_shape=(jax.ShapeDtypeStruct((frames, rows, cli...]
    dot_general x10 -> x6, matrix products: 29.1 us -> 4.24 us  [the longest x4 3.35 us: product(): term = jnp.dot(rows_here, parts[d], preferred_element_type=jnp.float32)]
    all_gather x2 -> x0, blocking collectives: 21.1 us -> none  [the longest x1 15.3 us: body(): tokens = lax.all_gather(tokens_here, 'stretch', axis=1, tiled=True)]
    ppermute x6 -> x5, waiting for transfers between devices: 22.7 us -> 5.7 us  [the longest x1 3.89 us: body(): v_unit = v_unit + lax.ppermute(of_units(own_v, other, 0), 'sample', route)]
    all_to_all x0 -> x4, starting transfers between devices: none -> 14.4 us  [the longest x2 5.98 us: spread(): lax.all_to_all(jnp.broadcast_to(value[None], (count,) + value.shape), axe...]
    concatenate x4 -> x0, local copies, waits for them, and re-layouts: 11.8 us -> none  [conv_taps(): stacked = jnp.concatenate(windows, axis=-1).reshape(-1, 9 * chans_in)]
    all_to_all x0 -> x4, waiting for transfers between devices: none -> 10.5 us  [the longest x2 7.21 us: spread(): lax.all_to_all(jnp.broadcast_to(value[None], (count,) + value.shape), axe...]
  transfers between devices with their start and end apart: 9 -> 9, of which waited for: 3 -> 6; matrix products, arithmetic and copies ran while one was open for 36% -> 11% of each run, Pallas kernels for 0% -> 28%
where the time goes in v1:
time: 90.8 us; the launch traced here: 90.1 us
  starting transfers between devices  27.1 us (30%)
  Pallas kernels  25.4 us (28%)
  waiting for transfers between devices  16.2 us (18%)
  local copies, waits for them, and re-layouts  12.6 us (14%)
  matrix products  4.24 us (5%)
  other arithmetic  3.58 us (4%)
  between operations  0.92 us (1%)
    pallas_call x1, Pallas kernels, decode(): pl.pallas_call(kernel, out_shape=(jax.ShapeDtypeStruct((frames, rows, cli...  25.4 us
    ppermute x2, starting transfers between devices, body(): lax.ppermute(own, 'stretch', [(i, i + d) for i in range(n_stretch - d)])  7.98 us
    all_to_all x2, waiting for transfers between devices, spread(): lax.all_to_all(jnp.broadcast_to(value[None], (count,) + value.shape), axe...  7.21 us
    all_to_all x2, starting transfers between devices, spread(): lax.all_to_all(jnp.broadcast_to(value[None], (count,) + value.shape), axe...  5.98 us
    unnamed x25, local copies, waits for them, and re-layouts  5.73 us
    all_to_all x1, starting transfers between devices, body(): got = lax.all_to_all(outgoing, ('sample', 'band'), 0, 0, tiled=True)  5.17 us
    ppermute x1, waiting for transfers between devices, body(): v_unit = v_unit + lax.ppermute(of_units(own_v, other, 0), 'sample', route)  3.89 us
    dot_general x4, matrix products, product(): term = jnp.dot(rows_here, parts[d], preferred_element_type=jnp.float32)  3.35 us
  transfers between devices with their start and end apart: 9, of which 6 were waited for; matrix products, arithmetic and copies ran while one was open for 11% of the time, Pallas kernels for 28%

profile of v1, /device:TPU:0, one launch (start us, length us, event | category | flops | bytes accessed | tf_op | source)
XLA Modules:
  0.0 90.1 jit_solution(722034206663635987)
XLA Ops:
  0.7 0.9 dynamic_slice.42
  1.6 0.7 dynamic_slice.43
  2.6 0.9 broadcast_select_fusion
  3.6 0.7 broadcast_in_dim.57
  4.3 5.2 %all-to-all-start = ((bf16[8,2,4,8,128]{4,3,2,1,0:T(8,128)(2,1)}), bf16[8,2,4,8,128]{4,3,2,1,0:T(8,128)(2,1)S(1)}, u32[]{:S(2)}, u32[]{:S(2)}) async-start(bf16[8,2,4,8,128]{4,3,2,1,0:T(8,128)(2,1)} %bitcast.9), calls=%async_computation | async-start | bytes 262144 | tf_op jit(solution)/shard_map/all_to_all | solution.py:237
  9.5 1.8 %constant_dynamic-slice_fusion.1 = bf16[768,280]{0,1:T(8,128)(2,1)} fusion(bf16[768,560]{0,1:T(8,128)(2,1)} %param.24, s32[]{:T(128)S(6)} %select_n.84), kind=kLoop, calls=%fused_computation.38 | loop fusion | bytes 860164 | tf_op jit(solution)/shard_map/dynamic_slice | solution.py:251
  11.3 2.0 %collective-permute-start.2 = (bf16[768,280]{0,1:T(8,128)(2,1)}, bf16[768,280]{0,1:T(8,128)(2,1)}, u32[]{:S(2)}, u32[]{:S(2)}) collective-permute-start(bf16[768,280]{0,1:T(8,128)(2,1)} %constant_dynamic-slice_fusion.1), channel_id=1, source_target_pairs={{0,16},{16,0},{1,17},{17,1},{2,18},{18,2},{3,19},{19,3},{4,20},{20... | collective-permute-start | bytes 1290248 | tf_op jit(solution)/shard_map/ppermute | solution.py:263
  13.5 1.1 %all-to-all-done = bf16[8,2,4,8,128]{4,3,2,1,0:T(8,128)(2,1)S(1)} async-done(((bf16[8,2,4,8,128]{4,3,2,1,0:T(8,128)(2,1)}), bf16[8,2,4,8,128]{4,3,2,1,0:T(8,128)(2,1)S(1)}, u32[]{:S(2)}, u32[]{:S(2)}) %all-to-all-start) | async-done | bytes 131104 | tf_op jit(solution)/shard_map/all_to_all | solution.py:237
  14.7 4.5 %collective-permute-start = (bf16[2,8,16,128]{3,2,1,0:T(8,128)(2,1)S(1)}, bf16[2,8,16,128]{3,2,1,0:T(8,128)(2,1)S(1)}, u32[]{:S(2)}, u32[]{:S(2)}) collective-permute-start(bf16[2,8,16,128]{3,2,1,0:T(8,128)(2,1)S(1)} %pad_dynamic-slice_fusion.refs_2_), channel_id=1, source_target_pairs={{0,8},{4,12},{1,9},{5,13},{2,10},{6,14},{3,11},{7,15},{16,24},{20,... | collective-permute-start | bytes 196616 | tf_op jit(solution)/shard_map/ppermute | solution.py:244
  19.2 3.5 %collective-permute-start.1 = (bf16[2,8,16,128]{3,2,1,0:T(8,128)(2,1)S(1)}, bf16[2,8,16,128]{3,2,1,0:T(8,128)(2,1)S(1)}, u32[]{:S(2)}, u32[]{:S(2)}) collective-permute-start(bf16[2,8,16,128]{3,2,1,0:T(8,128)(2,1)S(1)} %pad_dynamic-slice_fusion.refs_2_), channel_id=1, source_target_pairs={{0,4},{4,8},{8,12},{1,5},{5,9},{9,13},{2,6},{6,10},{10,14},{3,7},{... | collective-permute-start | bytes 196616 | tf_op jit(solution)/shard_map/ppermute | solution.py:244
  22.8 1.8 %collective-permute-done.1.refs_1_ = bf16[2,8,16,128]{3,2,1,0:T(8,128)(2,1)S(1)} collective-permute-done((bf16[2,8,16,128]{3,2,1,0:T(8,128)(2,1)S(1)}, bf16[2,8,16,128]{3,2,1,0:T(8,128)(2,1)S(1)}, u32[]{:S(2)}, u32[]{:S(2)}) %collective-permute-start.1) | collective-permute-done | bytes 65568 | tf_op jit(solution)/shard_map/ppermute | solution.py:244
  24.7 3.3 %copy-done.1 = bf16[10368,384]{1,0:T(8,128)(2,1)S(1)} copy-done((bf16[10368,384]{1,0:T(8,128)(2,1)S(1)}, bf16[10368,384]{1,0:T(8,128)(2,1)}, u32[]{:S(2)}) %copy-start.1) | copy-done | bytes 7962648
  27.9 25.4 %shard_map.149 = (bf16[2,4,16,3072]{3,2,1,0:T(8,128)(2,1)S(1)}, f32[2,16,384]{2,1,0:T(8,128)}) custom-call(s32[4]{0:T(128)S(1)} %pad_add_fusion.edge_ref, s32[16,128]{1,0:T(8,128)S(1)} %broadcast_in_dim.50.len_ref, bf16[2,8,16,128]{3,2,1,0:T(8,128)(2,1)S(1)} %collective-permute-done.refs_0_, bf16[2,8,16,128]{3,2,1,0:T(8,128)(2,1)S(1)} %collective-permute-done.1.refs_1_, ...), custom_call_target="tpu_custom_call" | custom-call | flops 8153726976 | bytes 7962624 | tf_op jit(solution)/shard_map/pallas_call | solution.py:150
  53.3 3.3 %all-to-all-start.1 = ((f32[4,8,384]{2,1,0:T(8,128)}), f32[4,8,384]{2,1,0:T(8,128)S(1)}, u32[]{:S(2)}, u32[]{:S(2)}) async-start(f32[4,8,384]{2,1,0:T(8,128)} %bitcast.14), calls=%async_computation.1 | async-start | bytes 98304 | tf_op jit(solution)/shard_map/all_to_all | solution.py:287
  56.6 0.8 constant_dynamic-slice_fusion
  57.4 0.9 %collective-permute-start.3 = (bf16[768,280]{0,1:T(8,128)(2,1)}, bf16[768,280]{0,1:T(8,128)(2,1)}, u32[]{:S(2)}, u32[]{:S(2)}) collective-permute-start(bf16[768,280]{0,1:T(8,128)(2,1)} %constant_dynamic-slice_fusion), channel_id=1, source_target_pairs={{0,16},{16,0},{1,17},{17,1},{2,18},{18,2},{3,19},{19,3},{4,20},{20... | collective-permute-start | bytes 1290248 | tf_op jit(solution)/shard_map/ppermute | solution.py:264
  58.4 2.2 %all-to-all-done.1 = f32[4,8,384]{2,1,0:T(8,128)S(1)} async-done(((f32[4,8,384]{2,1,0:T(8,128)}), f32[4,8,384]{2,1,0:T(8,128)S(1)}, u32[]{:S(2)}, u32[]{:S(2)}) %all-to-all-start.1) | async-done | bytes 49184 | tf_op jit(solution)/shard_map/all_to_all | solution.py:287
  60.6 0.7 broadcast_in_dim.58
  61.3 3.0 %all-to-all-start.2 = ((bf16[32,8,384]{2,1,0:T(8,128)(2,1)}), bf16[32,8,384]{2,1,0:T(8,128)(2,1)S(1)}, u32[]{:S(2)}, u32[]{:S(2)}) async-start(bf16[32,8,384]{2,1,0:T(8,128)(2,1)} %broadcast_in_dim.58), calls=%async_computation.2 | async-start | bytes 393216 | tf_op jit(solution)/shard_map/all_to_all | solution.py:189
  64.3 1.4 %multiply_reduce_fusion = f32[560]{0:T(1024)S(1)} fusion(bf16[560,768]{1,0:T(8,128)(2,1)} %param.26, f32[768]{0:T(1024)S(1)} %dynamic_slice.51), kind=kLoop, calls=%fused_computation.2 | loop fusion | flops 1289680 | bytes 865472 | tf_op jit(solution)/shard_map/reduce_sum | solution.py:253
  65.8 1.8 %collective-permute-start.4 = (f32[280]{0:T(512)S(1)}, f32[280]{0:T(512)S(1)}, u32[]{:S(2)}, u32[]{:S(2)}) collective-permute-start(f32[280]{0:T(512)S(1)} %dynamic_slice.53), channel_id=1, source_target_pairs={{0,16},{16,0},{1,17},{17,1},{2,18},{18,2},{3,19},{19,3},{4,20},{20... | collective-permute-start | bytes 3368 | tf_op jit(solution)/shard_map/ppermute | solution.py:265
  67.6 3.9 %collective-permute-done.4 = f32[280]{0:T(512)S(1)} collective-permute-done((f32[280]{0:T(512)S(1)}, f32[280]{0:T(512)S(1)}, u32[]{:S(2)}, u32[]{:S(2)}) %collective-permute-start.4) | collective-permute-done | bytes 1152 | tf_op jit(solution)/shard_map/ppermute | solution.py:265
  71.6 1.6 %all-to-all-done.2 = bf16[32,8,384]{2,1,0:T(8,128)(2,1)S(1)} async-done(((bf16[32,8,384]{2,1,0:T(8,128)(2,1)}), bf16[32,8,384]{2,1,0:T(8,128)(2,1)S(1)}, u32[]{:S(2)}, u32[]{:S(2)}) %all-to-all-start.2) | async-done | bytes 196640 | tf_op jit(solution)/shard_map/all_to_all | solution.py:189
  73.2 0.7 multiply_reduce_fusion.1
  74.1 0.9 %copy-done.3 = bf16[768,560]{0,1:T(8,128)(2,1)S(1)} copy-done((bf16[768,560]{0,1:T(8,128)(2,1)S(1)}, bf16[768,560]{0,1:T(8,128)(2,1)}, u32[]{:S(2)}) %copy-start.3) | copy-done | bytes 860184
  75.7 1.3 %convolution_add_fusion.1 = f32[256,280]{0,1:T(8,128)S(1)} fusion(f32[256,280]{0,1:T(8,128)S(1)} %fusion.4, bf16[768,280]{0,1:T(8,128)(2,1)} %collective-permute-done.2, bf16[256,1536]{1,0:T(8,128)(2,1)S(1)} %multiply_convert_fusion, s32[]{:T(128)S(6)} %select_n.82), kind=kOutput, calls=%fused_computation.7 | convolution fusion | flops 110172160 | bytes 1396740 | tf_op jit(solution)/shard_map/dot_general | solution.py:301
  77.0 1.4 %multiply_reduce_fusion.3 = f32[256]{0:T(256)S(1)} fusion(f32[280]{0:T(512)S(1)} %dynamic-slice_add_fusion, f32[256,280]{0,1:T(8,128)S(1)} %convolution_add_fusion.1, f32[256,280]{0,1:T(8,128)S(1)} %fusion.2, bf16[768,280]{0,1:T(8,128)(2,1)} %collective-permute-done.3, bf16[256,1536]{1,0:T(8,128)(2,1)S(1)} %multiply_convert_fusion, s32[]{:T(128)S(6)} %select_n.82), kind=kOutput, calls=%fused_computation.18 | convolution fusion | flops 110817024 | bytes 1399812 | tf_op jit(solution)/shard_map/dot_general | solution.py:301
  78.7 0.6 broadcast_in_dim.95
  79.3 3.0 %all-to-all-start.3 = ((f32[32,1,32]{2,1,0:T(1,128)}), f32[32,1,32]{2,1,0:T(1,128)S(1)}, u32[]{:S(2)}, u32[]{:S(2)}) async-start(f32[32,1,32]{2,1,0:T(1,128)} %broadcast_in_dim.95), calls=%async_computation.3 | async-start | bytes 32768 | tf_op jit(solution)/shard_map/all_to_all | solution.py:189
  82.4 1.5 %copy.31 = bf16[16,2,4,3072]{3,2,1,0:T(4,128)(2,1)} copy(bf16[16,2,4,3072]{3,0,2,1:T(8,128)(2,1)S(1)} %bitcast.31) | data formatting | bytes 1572864
  83.9 5.7 %all-to-all-done.3 = f32[32,1,32]{2,1,0:T(1,128)S(1)} async-done(((f32[32,1,32]{2,1,0:T(1,128)}), f32[32,1,32]{2,1,0:T(1,128)S(1)}, u32[]{:S(2)}, u32[]{:S(2)}) %all-to-all-start.3) | async-done | bytes 4128 | tf_op jit(solution)/shard_map/all_to_all | solution.py:189
  89.5 0.5 reduce_sum.89
  (57 shorter events, 2.4 us)
Async XLA Ops:
  0.6 72.5 %copy-start = (bf16[384,1536]{1,0:T(8,128)(2,1)S(1)}, bf16[384,1536]{1,0:T(8,128)(2,1)}, u32[]{:S(2)}) copy-start(bf16[384,1536]{1,0:T(8,128)(2,1)} %param.22) | copy-start | bytes 3538948
  0.6 12.6 %copy-start.10 = (s32[32]{0:T(128)S(1)}, s32[32]{0:T(128)}, u32[]{:S(2)}) copy-start(s32[32]{0:T(128)} %param.15) | copy-start | bytes 388
  0.7 12.6 %copy-start.11 = (s32[32]{0:T(128)S(1)}, s32[32]{0:T(128)}, u32[]{:S(2)}) copy-start(s32[32]{0:T(128)} %param.16) | copy-start | bytes 388
  0.7 12.8 %copy-start.7 = (f32[384]{0:T(512)S(1)}, f32[384]{0:T(512)}, u32[]{:S(2)}) copy-start(f32[384]{0:T(512)} %param.18) | copy-start | bytes 4612
  0.7 12.8 %copy-start.8 = (f32[384]{0:T(512)S(1)}, f32[384]{0:T(512)}, u32[]{:S(2)}) copy-start(f32[384]{0:T(512)} %param.19) | copy-start | bytes 4612
  0.7 12.8 %copy-start.9 = (f32[384]{0:T(512)S(1)}, f32[384]{0:T(512)}, u32[]{:S(2)}) copy-start(f32[384]{0:T(512)} %param.21) | copy-start | bytes 4612
  0.7 24.0 %copy-start.2 = (bf16[432,384]{1,0:T(8,128)(2,1)S(1)}, bf16[432,384]{1,0:T(8,128)(2,1)}, u32[]{:S(2)}) copy-start(bf16[432,384]{1,0:T(8,128)(2,1)} %refs_3_.1) | copy-start | bytes 995332
  4.3 10.4 %all-to-all-start = ((bf16[8,2,4,8,128]{4,3,2,1,0:T(8,128)(2,1)}), bf16[8,2,4,8,128]{4,3,2,1,0:T(8,128)(2,1)S(1)}, u32[]{:S(2)}, u32[]{:S(2)}) async-start(bf16[8,2,4,8,128]{4,3,2,1,0:T(8,128)(2,1)} %bitcast.9), calls=%async_computation | async-start | bytes 262144 | tf_op jit(solution)/shard_map/all_to_all | solution.py:237
  11.3 64.4 %collective-permute-start.2 = (bf16[768,280]{0,1:T(8,128)(2,1)}, bf16[768,280]{0,1:T(8,128)(2,1)}, u32[]{:S(2)}, u32[]{:S(2)}) collective-permute-start(bf16[768,280]{0,1:T(8,128)(2,1)} %constant_dynamic-slice_fusion.1), channel_id=1, source_target_pairs={{0,16},{16,0},{1,17},{17,1},{2,18},{18,2},{3,19},{19,3},{4,20},{20... | collective-permute-start | bytes 1290248 | tf_op jit(solution)/shard_map/ppermute | solution.py:263
  14.7 8.1 %collective-permute-start = (bf16[2,8,16,128]{3,2,1,0:T(8,128)(2,1)S(1)}, bf16[2,8,16,128]{3,2,1,0:T(8,128)(2,1)S(1)}, u32[]{:S(2)}, u32[]{:S(2)}) collective-permute-start(bf16[2,8,16,128]{3,2,1,0:T(8,128)(2,1)S(1)} %pad_dynamic-slice_fusion.refs_2_), channel_id=1, source_target_pairs={{0,8},{4,12},{1,9},{5,13},{2,10},{6,14},{3,11},{7,15},{16,24},{20,... | collective-permute-start | bytes 196616 | tf_op jit(solution)/shard_map/ppermute | solution.py:244
  19.2 5.4 %collective-permute-start.1 = (bf16[2,8,16,128]{3,2,1,0:T(8,128)(2,1)S(1)}, bf16[2,8,16,128]{3,2,1,0:T(8,128)(2,1)S(1)}, u32[]{:S(2)}, u32[]{:S(2)}) collective-permute-start(bf16[2,8,16,128]{3,2,1,0:T(8,128)(2,1)S(1)} %pad_dynamic-slice_fusion.refs_2_), channel_id=1, source_target_pairs={{0,4},{4,8},{8,12},{1,5},{5,9},{9,13},{2,6},{6,10},{10,14},{3,7},{... | collective-permute-start | bytes 196616 | tf_op jit(solution)/shard_map/ppermute | solution.py:244
  24.7 3.3 %copy-start.1 = (bf16[10368,384]{1,0:T(8,128)(2,1)S(1)}, bf16[10368,384]{1,0:T(8,128)(2,1)}, u32[]{:S(2)}) copy-start(bf16[10368,384]{1,0:T(8,128)(2,1)} %refs_6_.1) | copy-start | bytes 23887876
  27.9 28.7 %copy-start.4 = (bf16[768,560]{0,1:T(8,128)(2,1)S(1)}, bf16[768,560]{0,1:T(8,128)(2,1)}, u32[]{:S(2)}) copy-start(bf16[768,560]{0,1:T(8,128)(2,1)} %param.25) | copy-start | bytes 2580484
  27.9 30.4 %copy-start.5 = (f32[1536]{0:T(1024)S(1)}, f32[1536]{0:T(1024)}, u32[]{:S(2)}) copy-start(f32[1536]{0:T(1024)} %param.27) | copy-start | bytes 18436
  53.3 7.3 %all-to-all-start.1 = ((f32[4,8,384]{2,1,0:T(8,128)}), f32[4,8,384]{2,1,0:T(8,128)S(1)}, u32[]{:S(2)}, u32[]{:S(2)}) async-start(f32[4,8,384]{2,1,0:T(8,128)} %bitcast.14), calls=%async_computation.1 | async-start | bytes 98304 | tf_op jit(solution)/shard_map/all_to_all | solution.py:287
  57.4 19.6 %collective-permute-start.3 = (bf16[768,280]{0,1:T(8,128)(2,1)}, bf16[768,280]{0,1:T(8,128)(2,1)}, u32[]{:S(2)}, u32[]{:S(2)}) collective-permute-start(bf16[768,280]{0,1:T(8,128)(2,1)} %constant_dynamic-slice_fusion), channel_id=1, source_target_pairs={{0,16},{16,0},{1,17},{17,1},{2,18},{18,2},{3,19},{19,3},{4,20},{20... | collective-permute-start | bytes 1290248 | tf_op jit(solution)/shard_map/ppermute | solution.py:264
  61.3 11.8 %all-to-all-start.2 = ((bf16[32,8,384]{2,1,0:T(8,128)(2,1)}), bf16[32,8,384]{2,1,0:T(8,128)(2,1)S(1)}, u32[]{:S(2)}, u32[]{:S(2)}) async-start(bf16[32,8,384]{2,1,0:T(8,128)(2,1)} %broadcast_in_dim.58), calls=%async_computation.2 | async-start | bytes 393216 | tf_op jit(solution)/shard_map/all_to_all | solution.py:189
  65.7 8.2 %copy-start.6 = (f32[1536]{0:T(1024)S(1)}, f32[1536]{0:T(1024)}, u32[]{:S(2)}) copy-start(f32[1536]{0:T(1024)} %param.23) | copy-start | bytes 18436
  65.8 5.7 %collective-permute-start.4 = (f32[280]{0:T(512)S(1)}, f32[280]{0:T(512)S(1)}, u32[]{:S(2)}, u32[]{:S(2)}) collective-permute-start(f32[280]{0:T(512)S(1)} %dynamic_slice.53), channel_id=1, source_target_pairs={{0,16},{16,0},{1,17},{17,1},{2,18},{18,2},{3,19},{19,3},{4,20},{20... | collective-permute-start | bytes 3368 | tf_op jit(solution)/shard_map/ppermute | solution.py:265
  73.9 1.2 %copy-start.3 = (bf16[768,560]{0,1:T(8,128)(2,1)S(1)}, bf16[768,560]{0,1:T(8,128)(2,1)}, u32[]{:S(2)}) copy-start(bf16[768,560]{0,1:T(8,128)(2,1)} %param.24) | copy-start | bytes 2580484
  79.3 10.2 %all-to-all-start.3 = ((f32[32,1,32]{2,1,0:T(1,128)}), f32[32,1,32]{2,1,0:T(1,128)S(1)}, u32[]{:S(2)}, u32[]{:S(2)}) async-start(f32[32,1,32]{2,1,0:T(1,128)} %broadcast_in_dim.95), calls=%async_computation.3 | async-start | bytes 32768 | tf_op jit(solution)/shard_map/all_to_all | solution.py:189

commit v2 on v1

--- a/solution.py
+++ b/solution.py
@@ -12,7 +12,7 @@
 BEHIND = 2 * (TAPS - 1)
 
 
-def decode_kernel(
+def first_kernel(
     edge_ref,
     len_ref,
     *refs,
@@ -24,16 +24,15 @@
     chans,
 ):
     lat_refs = refs[:blocks]
-    (w_in_ref, b_in_ref, gain_ref, w_mid_hbm, b_mid_ref, out_ref, pool_ref) = refs[
-        blocks : blocks + 7
-    ]
-    x1_ref, wt_ref, act_ref, first_ref, acc_ref, wm_ref, sem = refs[blocks + 7 :]
+    (w_in_ref, b_in_ref, gain_ref, w_mid_hbm, b_mid_ref) = refs[blocks : blocks + 5]
+    act_hbm, first_hbm, pool_ref = refs[blocks + 5 : blocks + 8]
+    x1_ref, wt_ref, sums_ref, act_ref, first_ref, wm_ref, sem = refs[blocks + 8 :]
     chans_lat = w_in_ref.shape[0] // 27
     lanes = widths * chans_lat
     frames_act = frames + TAPS - 1
     rows_act = rows + TAPS - 1
     per_frame = rows_act * clips
-    weights_copy = pltpu.make_async_copy(w_mid_hbm, wm_ref, sem)
+    weights_copy = pltpu.make_async_copy(w_mid_hbm, wm_ref, sem.at[0])
     weights_copy.start()
 
     skip = blocks * frames - (frames_act + TAPS - 1)
@@ -52,7 +51,7 @@
     act_ref[:, :, 0] = jnp.zeros((frames_act, rows_act, clips, chans), jnp.bfloat16)
     act_ref[:, :, widths + 1] = jnp.zeros((frames_act, rows_act, clips, chans), jnp.bfloat16)
 
-    def column(q, carry):
+    def column(q, total_first):
         here = pl.multiple_of(q * chans_lat, chans_lat)
         before = pl.multiple_of(jnp.maximum(q - 1, 0) * chans_lat, chans_lat)
         for j in range(9):
@@ -69,12 +68,13 @@
         half = 0.5 * scaled
         act = (half + half * jnp.tanh(half)).astype(jnp.bfloat16)
         act_ref[:, :, q + 1] = act.reshape(frames_act, rows_act, clips, chans)
-        first_ref[:, :, q] = first.reshape(frames_act, rows_act, clips, chans)[
-            TAPS - 1 :, 1 : 1 + rows
-        ]
-        return carry
-
-    lax.fori_loop(0, widths, column, 0)
+        inner = first.reshape(frames_act, rows_act, clips, chans)[TAPS - 1 :, 1 : 1 + rows]
+        first_ref[:, :, q] = inner
+        return total_first + jnp.sum(inner.astype(jnp.float32), axis=1)
+
+    total_first = lax.fori_loop(
+        0, widths, column, jnp.zeros((frames, clips, chans), jnp.float32)
+    )
 
     @pl.when(edge_ref[0] == 1)
     def _():
@@ -90,55 +90,128 @@
             (TAPS - 1, rows_act, widths + 2, clips, chans), jnp.bfloat16
         )
 
+    act_copy = pltpu.make_async_copy(act_ref, act_hbm, sem.at[1])
+    first_copy = pltpu.make_async_copy(first_ref, first_hbm, sem.at[2])
+    act_copy.start()
+    first_copy.start()
+
+    half_rows = frames * clips
+    for f in range(frames_act):
+        per_row = []
+        for r in range(rows_act):
+            left = act_ref[f, r, 1].astype(jnp.float32)
+            right = act_ref[f, r, widths].astype(jnp.float32)
+            line = left + right
+            for q in range(2, widths):
+                line = line + act_ref[f, r, q].astype(jnp.float32)
+            per_row.append((line - right, line, line - left))
+        for dr in range(TAPS):
+            for dq in range(TAPS):
+                box = per_row[dr][dq]
+                for r in range(1, rows):
+                    box = box + per_row[dr + r][dq]
+                high = box.astype(jnp.bfloat16)
+                low = (box - high.astype(jnp.float32)).astype(jnp.bfloat16)
+                for t in range(frames):
+                    dt = f - t
+                    if 0 <= dt < TAPS:
+                        at = ((dt * TAPS + dr) * TAPS + dq) * chans
+                        sums_ref[t * clips : (t + 1) * clips, at : at + chans] = high
+                        sums_ref[
+                            half_rows + t * clips : half_rows + (t + 1) * clips, at : at + chans
+                        ] = low
+
     weights_copy.wait()
+    both = jnp.dot(sums_ref[...], wm_ref[...], preferred_element_type=jnp.float32)
+    for t in range(frames):
+        total = both[t * clips : (t + 1) * clips]
+        total = total + both[half_rows + t * clips : half_rows + (t + 1) * clips]
+        total = total + total_first[t] + b_mid_ref[...] * float(rows * widths)
+        live = (edge_ref[3] + t) < len_ref[:, 0:1]
+        pool_ref[t * clips : (t + 1) * clips, :] = jnp.where(live, total, 0.0)
+    act_copy.wait()
+    first_copy.wait()
+
+
+def second_kernel(
+    edge_ref,
+    len_ref,
+    act_hbm,
+    first_hbm,
+    wm_hbm,
+    b_mid_ref,
+    out_ref,
+    act_ref,
+    first_ref,
+    wm_ref,
+    act_sem,
+    first_sem,
+    wm_sem,
+    *,
+    t,
+):
+    rows, widths, clips, chans = first_ref.shape
     cells = rows * widths * clips
-
-    def window(t, tap):
-        dt = tap // 9
-        dr = (tap % 9) // 3
-        dq = tap % 3
-        return act_ref[t + dt, pl.ds(dr, rows), pl.ds(dq, widths)].reshape(cells, chans)
-
-    for t in range(frames):
-        acc_ref[...] = jnp.dot(
-            window(t, 26), wm_ref[26 * chans : 27 * chans, :], preferred_element_type=jnp.float32
-        )
-
-        def pair(p, carry, t=t):
-            both = jnp.concatenate([window(t, 2 * p), window(t, 2 * p + 1)], axis=-1)
-            at = pl.multiple_of(p * 2 * chans, 2 * chans)
-            acc_ref[...] += jnp.dot(
-                both, wm_ref[pl.ds(at, 2 * chans), :], preferred_element_type=jnp.float32
+    starts = list(range(0, 27, CHUNK))
+    act_copies = [
+        pltpu.make_async_copy(act_hbm.at[t + dt], act_ref.at[dt], act_sem.at[dt])
+        for dt in range(TAPS)
+    ]
+    wm_copies = []
+    for i, tap in enumerate(starts):
+        at = pl.ds(tap * chans, (min(tap + CHUNK, 27) - tap) * chans)
+        wm_copies.append(pltpu.make_async_copy(wm_hbm.at[at], wm_ref.at[at], wm_sem.at[i]))
+    first_copy = pltpu.make_async_copy(first_hbm.at[t], first_ref, first_sem)
+    act_copies[0].start()
+    for i, copy in enumerate(wm_copies):
+        copy.start()
+        if i + 1 < TAPS:
+            act_copies[i + 1].start()
+    first_copy.start()
+    total = None
+    for tap in range(0, 27, 2):
+        taps = range(tap, min(tap + 2, 27))
+        for k in taps:
+            if k % 9 == 0:
+                act_copies[k // 9].wait()
+        if tap in starts:
+            wm_copies[starts.index(tap)].wait()
+        parts = [
+            act_ref[k // 9, pl.ds((k % 9) // 3, rows), k % 3 : k % 3 + widths].reshape(cells, chans)
+            for k in taps
+        ]
+        lhs = parts[0] if len(parts) == 1 else jnp.concatenate(parts, axis=-1)
+        weight = wm_ref[tap * chans : (tap + len(parts)) * chans, :]
+        term = jnp.dot(lhs, weight, preferred_element_type=jnp.float32)
+        total = term if total is None else total + term
+    first_copy.wait()
+    live = (edge_ref[3] + t) < len_ref[:, 0:1]
+    for r in range(rows):
+        for q in range(widths):
+            at = (r * widths + q) * clips
+            mixed = (
+                first_ref[r, q].astype(jnp.float32) + total[at : at + clips, :] + b_mid_ref[...]
             )
-            return carry
-
-        lax.fori_loop(0, 13, pair, 0)
-        live = (edge_ref[3] + t) < len_ref[:, 0:1]
-        pooled = jnp.zeros((clips, chans), jnp.float32)
-        for r in range(rows):
-            for q in range(widths):
-                at = (r * widths + q) * clips
-                mixed = (
-                    first_ref[t, r, q].astype(jnp.float32)
-                    + acc_ref[at : at + clips, :]
-                    + b_mid_ref[...]
-                )
-                done = jnp.where(live, mixed, 0.0).astype(jnp.bfloat16)
-                out_ref[t, r, :, q * chans : (q + 1) * chans] = done
-                pooled = pooled + done.astype(jnp.float32)
-        pool_ref[t] = pooled
-
-
-def decode(edges, lens, blocks, w_in, b_in, gain_mid, w_mid, b_mid, frames, rows, widths):
+            done = jnp.where(live, mixed, 0.0).astype(jnp.bfloat16)
+            out_ref[r, :, q * chans : (q + 1) * chans] = done
+
+
+VMEM = pl.BlockSpec(memory_space=pltpu.VMEM)
+SMEM = pl.BlockSpec(memory_space=pltpu.SMEM)
+HBM = pl.BlockSpec(memory_space=pltpu.HBM)
+KERNEL_VMEM = 57 * 1024 * 1024
+CHUNK = 4
+
+
+def first_stage(edges, lens, blocks, w_in, b_in, gain_mid, w_mid, b_mid, frames, rows, widths):
     chans = w_in.shape[1]
     clips = blocks[0].shape[2]
     lanes = blocks[0].shape[3]
     chans_lat = lanes // widths
     frames_act = frames + TAPS - 1
     rows_act = rows + TAPS - 1
-    vmem = pl.BlockSpec(memory_space=pltpu.VMEM)
     kernel = functools.partial(
-        decode_kernel,
+        first_kernel,
         blocks=len(blocks),
         frames=frames,
         rows=rows,
@@ -146,30 +219,29 @@
         clips=clips,
         chans=chans,
     )
-    flops = 2 * frames * rows * widths * clips * chans * 27 * chans
     return pl.pallas_call(
         kernel,
         out_shape=(
-            jax.ShapeDtypeStruct((frames, rows, clips, widths * chans), jnp.bfloat16),
-            jax.ShapeDtypeStruct((frames, clips, chans), jnp.float32),
+            jax.ShapeDtypeStruct((frames_act, rows_act, widths + 2, clips, chans), jnp.bfloat16),
+            jax.ShapeDtypeStruct((frames, rows, widths, clips, chans), jnp.bfloat16),
+            jax.ShapeDtypeStruct((frames * clips, chans), jnp.float32),
         ),
-        in_specs=[pl.BlockSpec(memory_space=pltpu.SMEM), vmem]
-        + [vmem] * len(blocks)
-        + [vmem, vmem, vmem, pl.BlockSpec(memory_space=pl.ANY), vmem],
-        out_specs=(vmem, vmem),
+        in_specs=[SMEM, VMEM]
+        + [VMEM] * len(blocks)
+        + [VMEM, VMEM, VMEM, HBM, VMEM],
+        out_specs=(HBM, HBM, VMEM),
         scratch_shapes=[
             pltpu.VMEM((frames_act * rows_act * clips, 9 * lanes), jnp.bfloat16),
             pltpu.VMEM((9, lanes + 2 * chans_lat, chans), jnp.bfloat16),
+            pltpu.VMEM((2 * frames * clips, 27 * chans), jnp.bfloat16),
             pltpu.VMEM((frames_act, rows_act, widths + 2, clips, chans), jnp.bfloat16),
             pltpu.VMEM((frames, rows, widths, clips, chans), jnp.bfloat16),
-            pltpu.VMEM((rows * widths * clips, chans), jnp.float32),
             pltpu.VMEM(w_mid.shape, jnp.bfloat16),
-            pltpu.SemaphoreType.DMA,
+            pltpu.SemaphoreType.DMA((3,)),
         ],
-        compiler_params=pltpu.CompilerParams(vmem_limit_bytes=40 * 1024 * 1024),
-        cost_estimate=pl.CostEstimate(
-            flops=flops, bytes_accessed=w_mid.size * 2, transcendentals=0
-        ),
+        compiler_params=pltpu.CompilerParams(vmem_limit_bytes=KERNEL_VMEM),
+        cost_estimate=pl.CostEstimate(flops=1 << 32, bytes_accessed=1 << 16, transcendentals=0),
+        name="first_stage",
     )(
         edges,
         lens,
@@ -180,6 +252,28 @@
         w_mid,
         b_mid.reshape(1, -1),
     )
+
+
+def second_stage(edges, lens, act, first, w_mid, b_mid, t):
+    frames, rows, widths, clips, chans = first.shape
+    flops = 2 * rows * widths * clips * chans * 27 * chans
+    return pl.pallas_call(
+        functools.partial(second_kernel, t=t),
+        out_shape=jax.ShapeDtypeStruct((rows, clips, widths * chans), jnp.bfloat16),
+        in_specs=[SMEM, VMEM, HBM, HBM, HBM, VMEM],
+        out_specs=VMEM,
+        scratch_shapes=[
+            pltpu.VMEM((TAPS,) + act.shape[1:], jnp.bfloat16),
+            pltpu.VMEM(first.shape[1:], jnp.bfloat16),
+            pltpu.VMEM(w_mid.shape, jnp.bfloat16),
+            pltpu.SemaphoreType.DMA((TAPS,)),
+            pltpu.SemaphoreType.DMA,
+            pltpu.SemaphoreType.DMA((-(-27 // CHUNK),)),
+        ],
+        compiler_params=pltpu.CompilerParams(vmem_limit_bytes=KERNEL_VMEM),
+        cost_estimate=pl.CostEstimate(flops=flops, bytes_accessed=1 << 20, transcendentals=0),
+        name="second_stage",
+    )(edges, lens, act, first, w_mid, b_mid.reshape(1, -1))
 
 
 def spread(value, axes):
@@ -239,6 +333,7 @@
     got = got.transpose(2, 1, 3, 0, 4, 5).reshape(frames, n_band * rows, clips, lanes)
     got = jnp.pad(got, ((0, 0), (2, 2), (0, 0), (0, 0)))
     own = lax.dynamic_slice_in_dim(got, band * rows, rows + 4, axis=1)
+    own, late_down = lax.optimization_barrier((own, w_down))
     hops = -(-BEHIND // frames)
     blocks = [
         lax.ppermute(own, "stretch", [(i, i + d) for i in range(n_stretch - d)])
@@ -251,20 +346,18 @@
         return lax.dynamic_slice_in_dim(weight, index * units, units, axis=axis)
 
     own_v = jnp.sum(
-        w_down.astype(jnp.float32)
+        late_down.astype(jnp.float32)
         * lax.dynamic_slice_in_dim(w_score, group * w_down.shape[1], w_down.shape[1])[None, :],
         axis=-1,
     )
     depth = w_gate.shape[0]
-    gate_parts, up_parts, v_unit = [None], [None], of_units(own_v, group, 0)
+    gate_parts, up_parts, v_parts = [], [], []
     for d in range(1, n_sample):
         route = [(i, (i + d) % n_sample) for i in range(n_sample)]
         other = (group + d) % n_sample
         gate_parts.append(lax.ppermute(of_units(w_gate, other, 1), "sample", route))
         up_parts.append(lax.ppermute(of_units(w_up, other, 1), "sample", route))
-        v_unit = v_unit + lax.ppermute(of_units(own_v, other, 0), "sample", route)
-    gate_parts[0] = of_units(w_gate, group, 1)
-    up_parts[0] = of_units(w_up, group, 1)
+        v_parts.append(lax.ppermute(of_units(own_v, other, 0), "sample", route))
 
     slot_is = dest_slot[None, :] == jnp.arange(all_clips, dtype=jnp.int32)[:, None]
     len_slot = jnp.sum(jnp.where(slot_is, lengths[None, :], 0), axis=1)
@@ -278,15 +371,23 @@
         ]
     )
     lens = jnp.broadcast_to(my_slots[:, None], (clips, 128))
-    decoded, band_sum = decode(
+    act, first, band_sum = first_stage(
         edges, lens, blocks, w_in, b_in, gain_mid, w_mid, b_mid, frames, rows, widths
     )
-    decoded_out = decoded.transpose(2, 0, 1, 3)
+    band_sum, gate_parts, up_parts, v_parts = lax.optimization_barrier(
+        (band_sum, gate_parts, up_parts, v_parts)
+    )
+    gate_parts = [of_units(w_gate, group, 1)] + gate_parts
+    up_parts = [of_units(w_up, group, 1)] + up_parts
+    v_unit = of_units(own_v, group, 0) + sum(v_parts)
+    decoded = [second_stage(edges, lens, act, first, w_mid, b_mid, t) for t in range(frames)]
 
     band_sum = band_sum.reshape(n_band, frames * clips // n_band, chans)
     parts = lax.all_to_all(band_sum, "band", 0, 0, tiled=True)
     pooled = jnp.sum(parts, axis=0) / (rows * n_band * widths)
+    pooled, decoded[0] = lax.optimization_barrier((pooled, decoded[0]))
     pooled = spread(pooled.astype(jnp.bfloat16), ALL).reshape(-1, chans)
+    decoded_out = jnp.stack(decoded, axis=0).transpose(2, 0, 1, 3)
     tokens = jnp.dot(pooled, w_proj, preferred_element_type=jnp.float32).astype(jnp.bfloat16)
     token_f = tokens.astype(jnp.float32)
     normed = (

time: 90.8 us -> 90.9 us (level)
  waiting for transfers between devices: 16.2 us -> 5.58 us
  Pallas kernels: 25.4 us -> 33.4 us
  starting transfers between devices: 27.1 us -> 32.2 us
  matrix products: 4.24 us -> 3.22 us
    pallas_call x1 -> x3, Pallas kernels: 25.4 us -> 33.4 us  [the longest x2 22.2 us: second_stage(): pl.pallas_call(functools.partial(second_kernel, t=t), out_shape=jax.Shape...]
    all_to_all x2, starting transfers between devices: 5.98 us -> 11.7 us  [spread(): lax.all_to_all(jnp.broadcast_to(value[None], (count,) + value.shape), axe...]
    ppermute x1, waiting for transfers between devices: 3.89 us -> 0.01 us  [body(): v_parts.append(lax.ppermute(of_units(own_v, other, 0), 'sample', route))]
    unnamed x25 -> x33, local copies, waits for them, and re-layouts: 5.73 us -> 2.49 us
    all_to_all x1, waiting for transfers between devices: 2.17 us -> 0.01 us  [body(): parts = lax.all_to_all(band_sum, 'band', 0, 0, tiled=True)]
    ppermute x1, starting transfers between devices: 2.02 us -> 0.01 us  [body(): gate_parts.append(lax.ppermute(of_units(w_gate, other, 1), 'sample', route))]
    ppermute x2, waiting for transfers between devices: 1.8 us -> 0.01 us  [body(): lax.ppermute(own, 'stretch', [(i, i + d) for i in range(n_stretch - d)])]
    reshape x3, local copies, waits for them, and re-layouts: 0.01 us -> 1.72 us  [the longest x1 0.58 us: first_stage(): b_mid.reshape(1, -1)]
  transfers between devices with their start and end apart: 9 -> 9, of which waited for: 6 -> 1; matrix products, arithmetic and copies ran while one was open for 11% -> 9% of each run, Pallas kernels for 28% -> 37%
where the time goes in v2:
time: 90.9 us; the launch traced here: 90.2 us
  Pallas kernels  33.4 us (37%)
  starting transfers between devices  32.2 us (35%)
  local copies, waits for them, and re-layouts  11.7 us (13%)
  waiting for transfers between devices  5.58 us (6%)
  matrix products  3.22 us (4%)
  other arithmetic  3.03 us (3%)
  between operations  1.05 us (1%)
    pallas_call x2, Pallas kernels, second_stage(): pl.pallas_call(functools.partial(second_kernel, t=t), out_shape=jax.Shape...  22.2 us
    all_to_all x2, starting transfers between devices, spread(): lax.all_to_all(jnp.broadcast_to(value[None], (count,) + value.shape), axe...  11.7 us
    pallas_call x1, Pallas kernels, first_stage(): pl.pallas_call(kernel, out_shape=(jax.ShapeDtypeStruct((frames_act, rows_...  11.2 us
    ppermute x2, starting transfers between devices, body(): lax.ppermute(own, 'stretch', [(i, i + d) for i in range(n_stretch - d)])  7.98 us
    all_to_all x2, waiting for transfers between devices, spread(): lax.all_to_all(jnp.broadcast_to(value[None], (count,) + value.shape), axe...  5.56 us
    all_to_all x1, starting transfers between devices, body(): got = lax.all_to_all(outgoing, ('sample', 'band'), 0, 0, tiled=True)  5.17 us
    all_to_all x1, starting transfers between devices, body(): parts = lax.all_to_all(band_sum, 'band', 0, 0, tiled=True)  3.28 us
    dynamic_slice x3, local copies, waits for them, and re-layouts, of_units(): return lax.dynamic_slice_in_dim(weight, index * units, units, axis=axis)  2.67 us
  transfers between devices with their start and end apart: 9, of which 1 were waited for; matrix products, arithmetic and copies ran while one was open for 9% of the time, Pallas kernels for 37%

profile of v2, /device:TPU:0, one launch (start us, length us, event | category | flops | bytes accessed | tf_op | source)
XLA Modules:
  0.0 90.2 jit_solution(10300490070211427766)
XLA Ops:
  0.9 0.9 dynamic_slice.42
  1.8 0.7 dynamic_slice.43
  2.6 0.9 broadcast_select_fusion
  3.7 0.7 broadcast_in_dim.57
  4.3 5.2 %all-to-all-start = ((bf16[8,2,4,8,128]{4,3,2,1,0:T(8,128)(2,1)}), bf16[8,2,4,8,128]{4,3,2,1,0:T(8,128)(2,1)S(1)}, u32[]{:S(2)}, u32[]{:S(2)}) async-start(bf16[8,2,4,8,128]{4,3,2,1,0:T(8,128)(2,1)} %bitcast.9), calls=%async_computation | async-start | bytes 262144 | tf_op jit(solution)/shard_map/all_to_all | solution.py:331
  9.5 1.8 %constant_dynamic-slice_fusion = bf16[768,280]{0,1:T(8,128)(2,1)} fusion(bf16[768,560]{0,1:T(8,128)(2,1)} %param.25, s32[]{:T(128)S(6)} %select_n.79), kind=kLoop, calls=%fused_computation.41 | loop fusion | bytes 860164 | tf_op jit(solution)/shard_map/dynamic_slice | solution.py:346
  11.3 2.0 %collective-permute-start.3 = (bf16[768,280]{0,1:T(8,128)(2,1)}, bf16[768,280]{0,1:T(8,128)(2,1)}, u32[]{:S(2)}, u32[]{:S(2)}) collective-permute-start(bf16[768,280]{0,1:T(8,128)(2,1)} %constant_dynamic-slice_fusion), channel_id=1, source_target_pairs={{0,16},{16,0},{1,17},{17,1},{2,18},{18,2},{3,19},{19,3},{4,20},{20... | collective-permute-start | bytes 1290248 | tf_op jit(solution)/shard_map/ppermute | solution.py:359
  13.3 0.8 constant_dynamic-slice_fusion.1
  14.4 0.6 reshape.136.refs_7_.b_mid_ref
  15.0 0.6 reshape.134.refs_4_
  15.6 0.6 reshape.135.refs_5_
  16.3 0.6 pad_add_fusion.edge_ref
  16.9 3.5 %collective-permute-start.1 = (bf16[2,8,16,128]{3,2,1,0:T(8,128)(2,1)S(1)}, bf16[2,8,16,128]{3,2,1,0:T(8,128)(2,1)S(1)}, u32[]{:S(2)}, u32[]{:S(2)}) collective-permute-start(bf16[2,8,16,128]{3,2,1,0:T(8,128)(2,1)S(1)} %pad_dynamic-slice_fusion.refs_2_), channel_id=1, source_target_pairs={{0,4},{4,8},{8,12},{1,5},{5,9},{9,13},{2,6},{6,10},{10,14},{3,7},{... | collective-permute-start | bytes 196616 | tf_op jit(solution)/shard_map/ppermute | solution.py:339
  20.4 4.5 %collective-permute-start = (bf16[2,8,16,128]{3,2,1,0:T(8,128)(2,1)S(1)}, bf16[2,8,16,128]{3,2,1,0:T(8,128)(2,1)S(1)}, u32[]{:S(2)}, u32[]{:S(2)}) collective-permute-start(bf16[2,8,16,128]{3,2,1,0:T(8,128)(2,1)S(1)} %pad_dynamic-slice_fusion.refs_2_), channel_id=1, source_target_pairs={{0,8},{4,12},{1,9},{5,13},{2,10},{6,14},{3,11},{7,15},{16,24},{20,... | collective-permute-start | bytes 196616 | tf_op jit(solution)/shard_map/ppermute | solution.py:339
  25.3 2.0 %collective-permute-start.4 = (f32[280]{0:T(512)S(1)}, f32[280]{0:T(512)S(1)}, u32[]{:S(2)}, u32[]{:S(2)}) collective-permute-start(f32[280]{0:T(512)S(1)} %dynamic_slice.48), channel_id=1, source_target_pairs={{0,16},{16,0},{1,17},{17,1},{2,18},{18,2},{3,19},{19,3},{4,20},{20... | collective-permute-start | bytes 3368 | tf_op jit(solution)/shard_map/ppermute | solution.py:360
  27.3 0.7 broadcast_in_dim.50.len_ref
  28.0 11.2 %first_stage.1 = (bf16[4,6,10,16,384]{4,3,2,1,0:T(8,128)(2,1)}, bf16[2,4,8,16,384]{4,3,2,1,0:T(8,128)(2,1)}, f32[32,384]{1,0:T(8,128)}) custom-call(s32[4]{0:T(128)} %pad_add_fusion.edge_ref, s32[16,128]{1,0:T(8,128)} %broadcast_in_dim.50.len_ref, bf16[2,8,16,128]{3,2,1,0:T(8,128)(2,1)} %copy-done.13, bf16[2,8,16,128]{3,2,1,0:T(8,128)(2,1)} %copy-done.12, ...), custom_call_target="tpu_custom_call" | custom-call | flops 4294967296 | bytes 65536 | tf_op jit(solution)/shard_map/first_stage/pallas_call | solution.py:222
  39.2 3.3 %all-to-all-start.1 = ((f32[4,8,384]{2,1,0:T(8,128)}), f32[4,8,384]{2,1,0:T(8,128)S(1)}, u32[]{:S(2)}, u32[]{:S(2)}) async-start(f32[4,8,384]{2,1,0:T(8,128)} %bitcast.39), calls=%async_computation.1 | async-start | bytes 98304 | tf_op jit(solution)/shard_map/all_to_all | solution.py:386
  42.5 11.1 %second_stage.2 = bf16[4,16,3072]{2,1,0:T(8,128)(2,1)} custom-call(s32[4]{0:T(128)} %pad_add_fusion.edge_ref, s32[16,128]{1,0:T(8,128)} %broadcast_in_dim.50.len_ref, bf16[4,6,10,16,384]{4,3,2,1,0:T(8,128)(2,1)} %get-tuple-element.17.act_hbm, bf16[2,4,8,16,384]{4,3,2,1,0:T(8,128)(2,1)} %get-tuple-element.18.first_hbm, bf16[10368,384]{1,0:T(8,128)(2,1)} %wm_hbm.3, ...), custom_call_target="tpu_custom_call" | custom-call | flops 4076863488 | bytes 1048576 | tf_op jit(solution)/shard_map/second_stage/pallas_call | solution.py:260
  53.7 0.7 broadcast_in_dim.58
  54.4 6.1 %all-to-all-start.2 = ((bf16[32,8,384]{2,1,0:T(8,128)(2,1)}), bf16[32,8,384]{2,1,0:T(8,128)(2,1)S(1)}, u32[]{:S(2)}, u32[]{:S(2)}) async-start(bf16[32,8,384]{2,1,0:T(8,128)(2,1)} %broadcast_in_dim.58), calls=%async_computation.2 | async-start | bytes 393216 | tf_op jit(solution)/shard_map/all_to_all | solution.py:283
  60.5 11.1 %second_stage.3 = bf16[4,16,3072]{2,1,0:T(8,128)(2,1)} custom-call(s32[4]{0:T(128)} %pad_add_fusion.edge_ref, s32[16,128]{1,0:T(8,128)} %broadcast_in_dim.50.len_ref, bf16[4,6,10,16,384]{4,3,2,1,0:T(8,128)(2,1)} %get-tuple-element.17.act_hbm, bf16[2,4,8,16,384]{4,3,2,1,0:T(8,128)(2,1)} %get-tuple-element.18.first_hbm, bf16[10368,384]{1,0:T(8,128)(2,1)} %wm_hbm.3, ...), custom_call_target="tpu_custom_call" | custom-call | flops 4076863488 | bytes 1048576 | tf_op jit(solution)/shard_map/second_stage/pallas_call | solution.py:260
  71.7 0.7 multiply_reduce_fusion.1
  72.6 0.9 %copy-done.1 = bf16[768,560]{0,1:T(8,128)(2,1)S(1)} copy-done((bf16[768,560]{0,1:T(8,128)(2,1)S(1)}, bf16[768,560]{0,1:T(8,128)(2,1)}, u32[]{:S(2)}) %copy-start.1) | copy-done | bytes 860184
  73.8 0.3 fusion.4
  74.2 0.3 convolution_add_fusion.1
  74.5 1.4 %multiply_reduce_fusion.3 = f32[256]{0:T(256)S(1)} fusion(f32[280]{0:T(512)S(1)} %dynamic-slice_add_fusion, f32[256,280]{0,1:T(8,128)S(1)} %convolution_add_fusion.1, f32[256,280]{0,1:T(8,128)S(1)} %fusion.2, bf16[768,280]{0,1:T(8,128)(2,1)} %collective-permute-done.3, bf16[256,1536]{1,0:T(8,128)(2,1)S(1)} %multiply_convert_fusion, s32[]{:T(128)S(6)} %select_n.85), kind=kOutput, calls=%fused_computation.19 | convolution fusion | flops 110817024 | bytes 1399812 | tf_op jit(solution)/shard_map/dot_general | solution.py:402
  76.2 0.6 broadcast_in_dim.95
  76.8 5.7 %all-to-all-start.3 = ((f32[32,1,32]{2,1,0:T(1,128)}), f32[32,1,32]{2,1,0:T(1,128)S(1)}, u32[]{:S(2)}, u32[]{:S(2)}) async-start(f32[32,1,32]{2,1,0:T(1,128)} %broadcast_in_dim.95), calls=%async_computation.3 | async-start | bytes 32768 | tf_op jit(solution)/shard_map/all_to_all | solution.py:283
  82.6 1.5 %copy.31 = bf16[16,2,4,3072]{3,2,1,0:T(4,128)(2,1)} copy(bf16[16,2,4,3072]{3,0,2,1:T(8,128)(2,1)S(1)} %maximum_bitcast_fusion) | data formatting | bytes 1572864
  84.1 5.6 %all-to-all-done.3 = f32[32,1,32]{2,1,0:T(1,128)S(1)} async-done(((f32[32,1,32]{2,1,0:T(1,128)}), f32[32,1,32]{2,1,0:T(1,128)S(1)}, u32[]{:S(2)}, u32[]{:S(2)}) %all-to-all-start.3) | async-done | bytes 4128 | tf_op jit(solution)/shard_map/all_to_all | solution.py:283
  89.6 0.5 reduce_sum.89
  (68 shorter events, 2.3 us)
Async XLA Ops:
  0.6 71.0 %copy-start = (bf16[384,1536]{1,0:T(8,128)(2,1)S(1)}, bf16[384,1536]{1,0:T(8,128)(2,1)}, u32[]{:S(2)}) copy-start(bf16[384,1536]{1,0:T(8,128)(2,1)} %param.22) | copy-start | bytes 3538948
  0.6 13.5 %copy-start.14 = (s32[32]{0:T(128)S(1)}, s32[32]{0:T(128)}, u32[]{:S(2)}) copy-start(s32[32]{0:T(128)} %param.15) | copy-start | bytes 388
  0.7 13.5 %copy-start.15 = (s32[32]{0:T(128)S(1)}, s32[32]{0:T(128)}, u32[]{:S(2)}) copy-start(s32[32]{0:T(128)} %param.16) | copy-start | bytes 388
  0.7 12.7 %copy-start.2 = (bf16[768,560]{0,1:T(8,128)(2,1)S(1)}, bf16[768,560]{0,1:T(8,128)(2,1)}, u32[]{:S(2)}) copy-start(bf16[768,560]{0,1:T(8,128)(2,1)} %param.24) | copy-start | bytes 2580484
  0.7 13.8 %copy-start.9 = (f32[384]{0:T(512)S(1)}, f32[384]{0:T(512)}, u32[]{:S(2)}) copy-start(f32[384]{0:T(512)} %param.21) | copy-start | bytes 4612
  0.7 14.3 %copy-start.10 = (f32[384]{0:T(512)S(1)}, f32[384]{0:T(512)}, u32[]{:S(2)}) copy-start(f32[384]{0:T(512)} %param.18) | copy-start | bytes 4612
  0.7 14.9 %copy-start.11 = (f32[384]{0:T(512)S(1)}, f32[384]{0:T(512)}, u32[]{:S(2)}) copy-start(f32[384]{0:T(512)} %param.19) | copy-start | bytes 4612
  0.7 15.5 %copy-start.7 = (f32[1536]{0:T(1024)S(1)}, f32[1536]{0:T(1024)}, u32[]{:S(2)}) copy-start(f32[1536]{0:T(1024)} %param.27) | copy-start | bytes 18436
  0.7 24.2 %copy-start.3 = (bf16[560,768]{1,0:T(8,128)(2,1)S(1)}, bf16[560,768]{1,0:T(8,128)(2,1)}, u32[]{:S(2)}) copy-start(bf16[560,768]{1,0:T(8,128)(2,1)} %param.26) | copy-start | bytes 2580484
  4.3 12.5 %all-to-all-start = ((bf16[8,2,4,8,128]{4,3,2,1,0:T(8,128)(2,1)}), bf16[8,2,4,8,128]{4,3,2,1,0:T(8,128)(2,1)S(1)}, u32[]{:S(2)}, u32[]{:S(2)}) async-start(bf16[8,2,4,8,128]{4,3,2,1,0:T(8,128)(2,1)} %bitcast.9), calls=%async_computation | async-start | bytes 262144 | tf_op jit(solution)/shard_map/all_to_all | solution.py:331
  11.3 27.9 %collective-permute-start.3 = (bf16[768,280]{0,1:T(8,128)(2,1)}, bf16[768,280]{0,1:T(8,128)(2,1)}, u32[]{:S(2)}, u32[]{:S(2)}) collective-permute-start(bf16[768,280]{0,1:T(8,128)(2,1)} %constant_dynamic-slice_fusion), channel_id=1, source_target_pairs={{0,16},{16,0},{1,17},{17,1},{2,18},{18,2},{3,19},{19,3},{4,20},{20... | collective-permute-start | bytes 1290248 | tf_op jit(solution)/shard_map/ppermute | solution.py:359
  14.1 25.1 %collective-permute-start.2 = (bf16[768,280]{0,1:T(8,128)(2,1)}, bf16[768,280]{0,1:T(8,128)(2,1)S(1)}, u32[]{:S(2)}, u32[]{:S(2)}) collective-permute-start(bf16[768,280]{0,1:T(8,128)(2,1)} %constant_dynamic-slice_fusion.1), channel_id=1, source_target_pairs={{0,16},{16,0},{1,17},{17,1},{2,18},{18,2},{3,19},{19,3},{4,20},{20... | collective-permute-start | bytes 1290248 | tf_op jit(solution)/shard_map/ppermute | solution.py:358
  16.9 11.1 %copy-start.6 = (bf16[2,8,16,128]{3,2,1,0:T(8,128)(2,1)}, bf16[2,8,16,128]{3,2,1,0:T(8,128)(2,1)S(1)}, u32[]{:S(2)}) copy-start(bf16[2,8,16,128]{3,2,1,0:T(8,128)(2,1)S(1)} %pad_dynamic-slice_fusion.refs_2_) | copy-start | bytes 196612
  16.9 10.4 %collective-permute-start.1 = (bf16[2,8,16,128]{3,2,1,0:T(8,128)(2,1)S(1)}, bf16[2,8,16,128]{3,2,1,0:T(8,128)(2,1)S(1)}, u32[]{:S(2)}, u32[]{:S(2)}) collective-permute-start(bf16[2,8,16,128]{3,2,1,0:T(8,128)(2,1)S(1)} %pad_dynamic-slice_fusion.refs_2_), channel_id=1, source_target_pairs={{0,4},{4,8},{8,12},{1,5},{5,9},{9,13},{2,6},{6,10},{10,14},{3,7},{... | collective-permute-start | bytes 196616 | tf_op jit(solution)/shard_map/ppermute | solution.py:339
  20.4 6.9 %collective-permute-start = (bf16[2,8,16,128]{3,2,1,0:T(8,128)(2,1)S(1)}, bf16[2,8,16,128]{3,2,1,0:T(8,128)(2,1)S(1)}, u32[]{:S(2)}, u32[]{:S(2)}) collective-permute-start(bf16[2,8,16,128]{3,2,1,0:T(8,128)(2,1)S(1)} %pad_dynamic-slice_fusion.refs_2_), channel_id=1, source_target_pairs={{0,8},{4,12},{1,9},{5,13},{2,10},{6,14},{3,11},{7,15},{16,24},{20,... | collective-permute-start | bytes 196616 | tf_op jit(solution)/shard_map/ppermute | solution.py:339
  25.3 13.9 %collective-permute-start.4 = (f32[280]{0:T(512)S(1)}, f32[280]{0:T(512)S(1)}, u32[]{:S(2)}, u32[]{:S(2)}) collective-permute-start(f32[280]{0:T(512)S(1)} %dynamic_slice.48), channel_id=1, source_target_pairs={{0,16},{16,0},{1,17},{17,1},{2,18},{18,2},{3,19},{19,3},{4,20},{20... | collective-permute-start | bytes 3368 | tf_op jit(solution)/shard_map/ppermute | solution.py:360
  27.3 0.7 copy-start.12
  27.3 0.7 copy-start.13
  39.2 14.4 %all-to-all-start.1 = ((f32[4,8,384]{2,1,0:T(8,128)}), f32[4,8,384]{2,1,0:T(8,128)S(1)}, u32[]{:S(2)}, u32[]{:S(2)}) async-start(f32[4,8,384]{2,1,0:T(8,128)} %bitcast.39), calls=%async_computation.1 | async-start | bytes 98304 | tf_op jit(solution)/shard_map/all_to_all | solution.py:386
  54.4 17.3 %all-to-all-start.2 = ((bf16[32,8,384]{2,1,0:T(8,128)(2,1)}), bf16[32,8,384]{2,1,0:T(8,128)(2,1)S(1)}, u32[]{:S(2)}, u32[]{:S(2)}) async-start(bf16[32,8,384]{2,1,0:T(8,128)(2,1)} %broadcast_in_dim.58), calls=%async_computation.2 | async-start | bytes 393216 | tf_op jit(solution)/shard_map/all_to_all | solution.py:283
  71.6 0.8 copy-start.8
  72.4 1.2 %copy-start.1 = (bf16[768,560]{0,1:T(8,128)(2,1)S(1)}, bf16[768,560]{0,1:T(8,128)(2,1)}, u32[]{:S(2)}) copy-start(bf16[768,560]{0,1:T(8,128)(2,1)} %param.25) | copy-start | bytes 2580484
  74.2 8.3 %copy-start.4 = (bf16[4,16,3072]{2,1,0:T(8,128)(2,1)S(1)}, bf16[4,16,3072]{2,1,0:T(8,128)(2,1)}, u32[]{:S(2)}) copy-start(bf16[4,16,3072]{2,1,0:T(8,128)(2,1)} %second_stage.2) | copy-start | bytes 1179652
  74.2 8.3 %copy-start.5 = (bf16[4,16,3072]{2,1,0:T(8,128)(2,1)S(1)}, bf16[4,16,3072]{2,1,0:T(8,128)(2,1)}, u32[]{:S(2)}) copy-start(bf16[4,16,3072]{2,1,0:T(8,128)(2,1)} %second_stage.3) | copy-start | bytes 1179652
  76.8 12.8 %all-to-all-start.3 = ((f32[32,1,32]{2,1,0:T(1,128)}), f32[32,1,32]{2,1,0:T(1,128)S(1)}, u32[]{:S(2)}, u32[]{:S(2)}) async-start(f32[32,1,32]{2,1,0:T(1,128)} %broadcast_in_dim.95), calls=%async_computation.3 | async-start | bytes 32768 | tf_op jit(solution)/shard_map/all_to_all | solution.py:283

commit v3 on v1

v3 whole, which is shorter than its diff:
```python
import functools

import jax
import jax.numpy as jnp
from jax import lax
from jax.experimental import pallas as pl
from jax.experimental.pallas import tpu as pltpu
from jax.sharding import PartitionSpec as P

ALL = ("sample", "stretch", "band")
TAPS = 3
BEHIND = 2 * (TAPS - 1)


def decode_kernel(
    scalar_ref,
    lat_ref,
    w_in_ref,
    b_in_ref,
    gain_ref,
    w_mid_hbm,
    b_mid_ref,
    out_ref,
    pool_ref,
    x1_ref,
    wt_ref,
    act_ref,
    first_ref,
    wm_ref,
    sem,
    *,
    frames,
    rows,
    widths,
):
    clips, lanes = lat_ref.shape[2:]
    chans = w_in_ref.shape[1]
    chans_lat = w_in_ref.shape[0] // 27
    frames_act = frames + TAPS - 1
    rows_act = rows + TAPS - 1
    per_frame = rows_act * clips
    weights_copy = pltpu.make_async_copy(w_mid_hbm, wm_ref, sem)
    weights_copy.start()
    b_in = b_in_ref[...].reshape(1, chans)
    gain = gain_ref[...].reshape(1, chans)
    b_mid = b_mid_ref[...].reshape(1, chans)

    for j in range(9):
        dt, dr = divmod(j, 3)
        for f in range(frames_act):
            x1_ref[f * per_frame : (f + 1) * per_frame, j * lanes : (j + 1) * lanes] = lat_ref[
                f + dt, dr : dr + rows_act
            ].reshape(per_frame, lanes)
    wt_ref[...] = jnp.zeros_like(wt_ref)
    act_ref[:, :, 0] = jnp.zeros((frames_act, rows_act, clips, chans), jnp.bfloat16)
    act_ref[:, :, widths + 1] = jnp.zeros((frames_act, rows_act, clips, chans), jnp.bfloat16)

    def column(q, carry):
        here = pl.multiple_of(q * chans_lat, chans_lat)
        before = pl.multiple_of(jnp.maximum(q - 1, 0) * chans_lat, chans_lat)
        for j in range(9):
            wt_ref[j, pl.ds(before, chans_lat), :] = jnp.zeros((chans_lat, chans), jnp.bfloat16)
            wt_ref[j, pl.ds(here, 3 * chans_lat), :] = w_in_ref[
                j * 3 * chans_lat : (j + 1) * 3 * chans_lat, :
            ]
        weight = wt_ref[:, chans_lat : chans_lat + lanes, :].reshape(9 * lanes, chans)
        total = jnp.dot(x1_ref[...], weight, preferred_element_type=jnp.float32)
        first = (total + b_in).astype(jnp.bfloat16)
        values = first.astype(jnp.float32)
        square = jnp.sum(values * values, axis=-1, keepdims=True) * (1.0 / chans)
        half = values * lax.rsqrt(square + 1e-06) * (gain * 0.5)
        act = (half + half * jnp.tanh(half)).astype(jnp.bfloat16)
        act_ref[:, :, q + 1] = act.reshape(frames_act, rows_act, clips, chans)
        first_ref[:, :, q] = first.reshape(frames_act, rows_act, clips, chans)[
            TAPS - 1 :, 1 : 1 + rows
        ]
        return carry

    lax.fori_loop(0, widths, column, 0)

    @pl.when(scalar_ref[0] == 1)
    def _():
        act_ref[:, 0] = jnp.zeros((frames_act, widths + 2, clips, chans), jnp.bfloat16)

    @pl.when(scalar_ref[1] == 1)
    def _():
        act_ref[:, rows_act - 1] = jnp.zeros((frames_act, widths + 2, clips, chans), jnp.bfloat16)

    @pl.when(scalar_ref[2] == 1)
    def _():
        act_ref[0 : TAPS - 1] = jnp.zeros(
            (TAPS - 1, rows_act, widths + 2, clips, chans), jnp.bfloat16
        )

    weights_copy.wait()
    cells = widths * clips
    clip_ids = lax.broadcasted_iota(jnp.int32, (clips, chans), 0)
    lens = jnp.zeros((clips, chans), jnp.int32)
    for c in range(clips):
        lens = jnp.where(clip_ids == c, scalar_ref[4 + c], lens)
    pool_ref[...] = jnp.zeros_like(pool_ref)

    def line(r, carry):
        totals = [None] * frames
        for f in range(frames_act):
            outs = [t for t in range(frames) if 0 <= f - t < TAPS]
            for j in range(0, 9, 2):
                taps = range(j, min(j + 2, 9))
                lhs = [
                    act_ref[f, r + k // 3, k % 3 : k % 3 + widths].reshape(cells, chans)
                    for k in taps
                ]
                lhs = lhs[0] if len(lhs) == 1 else jnp.concatenate(lhs, axis=-1)
                weights = []
                for t in outs:
                    at = (f - t) * 9 + j
                    weights.append(wm_ref[at * chans : (at + len(taps)) * chans, :])
                weight = weights[0] if len(outs) == 1 else jnp.concatenate(weights, axis=-1)
                term = jnp.dot(lhs, weight, preferred_element_type=jnp.float32)
                for i, t in enumerate(outs):
                    part = term[:, i * chans : (i + 1) * chans]
                    totals[t] = part if totals[t] is None else totals[t] + part
        for t in range(frames):
            live = (scalar_ref[3] + t) < lens
            pooled = pool_ref[t]
            for q in range(widths):
                mixed = (
                    first_ref[t, r, q].astype(jnp.float32)
                    + totals[t][q * clips : (q + 1) * clips, :]
                    + b_mid
                )
                done = jnp.where(live, mixed, 0.0).astype(jnp.bfloat16)
                out_ref[t, r, :, q * chans : (q + 1) * chans] = done
                pooled = pooled + done.astype(jnp.float32)
            pool_ref[t] = pooled
        return carry

    lax.fori_loop(0, rows, line, 0)


VMEM = pl.BlockSpec(memory_space=pltpu.VMEM)
SMEM = pl.BlockSpec(memory_space=pltpu.SMEM)
HBM = pl.BlockSpec(memory_space=pltpu.HBM)
KERNEL_VMEM = 57 * 1024 * 1024


def decode(scalars, cells, w_in, b_in, gain_mid, w_mid, b_mid, frames, rows, widths):
    chans = w_in.shape[1]
    clips, lanes = cells.shape[2:]
    chans_lat = lanes // widths
    frames_act = frames + TAPS - 1
    rows_act = rows + TAPS - 1
    flops = 2 * frames * rows * widths * clips * chans * 27 * chans
    return pl.pallas_call(
        functools.partial(decode_kernel, frames=frames, rows=rows, widths=widths),
        out_shape=(
            jax.ShapeDtypeStruct((frames, rows, clips, widths * chans), jnp.bfloat16),
            jax.ShapeDtypeStruct((frames, clips, chans), jnp.float32),
        ),
        in_specs=[SMEM, VMEM, VMEM, VMEM, VMEM, HBM, VMEM],
        out_specs=(VMEM, VMEM),
        scratch_shapes=[
            pltpu.VMEM((frames_act * rows_act * clips, 9 * lanes), jnp.bfloat16),
            pltpu.VMEM((9, lanes + 2 * chans_lat, chans), jnp.bfloat16),
            pltpu.VMEM((frames_act, rows_act, widths + 2, clips, chans), jnp.bfloat16),
            pltpu.VMEM((frames, rows, widths, clips, chans), jnp.bfloat16),
            pltpu.VMEM(w_mid.shape, jnp.bfloat16),
            pltpu.SemaphoreType.DMA,
        ],
        compiler_params=pltpu.CompilerParams(vmem_limit_bytes=KERNEL_VMEM),
        cost_estimate=pl.CostEstimate(flops=flops, bytes_accessed=1 << 16, transcendentals=0),
        name="decode",
    )(scalars, cells, w_in, b_in, gain_mid, w_mid, b_mid)


def spread(value, axes):
    count = 1
    for axis in axes:
        count *= lax.axis_size(axis)
    return lax.all_to_all(
        jnp.broadcast_to(value[None], (count,) + value.shape), axes, 0, 0, tiled=True
    )


def body(
    latents,
    lengths,
    dest_slot,
    w_in,
    b_in,
    gain_mid,
    w_mid,
    b_mid,
    w_proj,
    gain_tok,
    w_gate,
    w_up,
    w_down,
    w_score,
):
    clips, frames, rows, lanes = latents.shape
    n_sample, n_stretch, n_band = (lax.axis_size(axis) for axis in ALL)
    chans_lat = w_in.shape[0] // 27
    chans = w_in.shape[1]
    widths = lanes // chans_lat
    sends = clips // n_sample
    group = lax.axis_index("sample")
    stretch = lax.axis_index("stretch")
    band = lax.axis_index("band")
    all_clips = dest_slot.shape[0]
    frame0 = stretch * frames

    hops = -(-BEHIND // frames)
    series = [
        lax.ppermute(latents, "stretch", [(i, i + d) for i in range(n_stretch - d)])
        for d in range(hops, 0, -1)
    ] + [latents]
    series = jnp.concatenate(series, axis=1)[:, hops * frames - BEHIND :]
    all_frames = frames + BEHIND
    is_group = jnp.arange(n_sample, dtype=jnp.int32)[:, None] == group
    my_dest = jnp.sum(jnp.where(is_group, dest_slot.reshape(n_sample, clips), 0), axis=0)
    my_len = jnp.sum(jnp.where(is_group, lengths.reshape(n_sample, clips), 0), axis=0)
    target = jnp.arange(n_sample, dtype=jnp.int32)[:, None] * clips + group * sends
    target = (target + jnp.arange(sends, dtype=jnp.int32)[None, :]).reshape(-1)
    select = (target[:, None] == my_dest[None, :]).astype(jnp.bfloat16)
    frame_ids = frame0 - BEHIND + jnp.arange(all_frames, dtype=jnp.int32)
    live = frame_ids[None, :] < my_len[:, None]
    masked = jnp.where(live[:, :, None, None], series, jnp.zeros((), jnp.bfloat16))
    routed = jnp.einsum(
        "kc,ctrl->trkl", select, masked, preferred_element_type=jnp.float32
    ).astype(jnp.bfloat16)
    routed = routed.reshape(all_frames, rows, n_sample, sends, lanes).transpose(2, 0, 1, 3, 4)
    outgoing = jnp.broadcast_to(
        routed[:, None], (n_sample, n_band, all_frames, rows, sends, lanes)
    ).reshape(n_sample * n_band, all_frames, rows, sends, lanes)
    got = lax.all_to_all(outgoing, ("sample", "band"), 0, 0, tiled=True)
    got = got.reshape(n_sample, n_band, all_frames, rows, sends, lanes)
    got = got.transpose(2, 1, 3, 0, 4, 5).reshape(all_frames, n_band * rows, clips, lanes)
    got = jnp.pad(got, ((0, 0), (2, 2), (0, 0), (0, 0)))
    cells = lax.dynamic_slice_in_dim(got, band * rows, rows + 4, axis=1)

    units = w_gate.shape[1] // n_sample

    def of_units(weight, index, axis):
        return lax.dynamic_slice_in_dim(weight, index * units, units, axis=axis)

    own_v = jnp.sum(
        w_down.astype(jnp.float32)
        * lax.dynamic_slice_in_dim(w_score, group * w_down.shape[1], w_down.shape[1])[None, :],
        axis=-1,
    )
    depth = w_gate.shape[0]
    gate_parts, up_parts, v_parts = [], [], []
    for d in range(1, n_sample):
        route = [(i, (i + d) % n_sample) for i in range(n_sample)]
        other = (group + d) % n_sample
        gate_parts.append(lax.ppermute(of_units(w_gate, other, 1), "sample", route))
        up_parts.append(lax.ppermute(of_units(w_up, other, 1), "sample", route))
        v_parts.append(lax.ppermute(of_units(own_v, other, 0), "sample", route))

    slot_is = dest_slot[None, :] == jnp.arange(all_clips, dtype=jnp.int32)[:, None]
    len_slot = jnp.sum(jnp.where(slot_is, lengths[None, :], 0), axis=1)
    my_slots = lax.dynamic_slice_in_dim(len_slot, group * clips, clips)
    scalars = jnp.concatenate(
        [
            jnp.stack([band == 0, band == n_band - 1, stretch == 0]).astype(jnp.int32),
            frame0[None].astype(jnp.int32),
            my_slots,
        ]
    )
    decoded, band_sum = decode(
        scalars, cells, w_in, b_in, gain_mid, w_mid, b_mid, frames, rows, widths
    )
    band_sum, gate_parts, up_parts, v_parts = lax.optimization_barrier(
        (band_sum, gate_parts, up_parts, v_parts)
    )
    gate_parts = [of_units(w_gate, group, 1)] + gate_parts
    up_parts = [of_units(w_up, group, 1)] + up_parts
    v_unit = of_units(own_v, group, 0) + sum(v_parts)
    decoded_out = decoded.transpose(2, 0, 1, 3)

    band_sum = band_sum.reshape(n_band, frames * clips // n_band, chans)
    parts = lax.all_to_all(band_sum, "band", 0, 0, tiled=True)
    pooled = jnp.sum(parts, axis=0) / (rows * n_band * widths)
    pooled = spread(pooled.astype(jnp.bfloat16), ALL).reshape(-1, chans)
    tokens = jnp.dot(pooled, w_proj, preferred_element_type=jnp.float32).astype(jnp.bfloat16)
    token_f = tokens.astype(jnp.float32)
    normed = (
        token_f * lax.rsqrt(jnp.mean(token_f * token_f, axis=-1, keepdims=True) + 1e-06) * gain_tok
    ).astype(jnp.bfloat16)

    def product(parts):
        total = None
        for d in range(n_sample):
            source = (group - d) % n_sample
            rows_here = lax.dynamic_slice_in_dim(normed, source * depth, depth, axis=1)
            term = jnp.dot(rows_here, parts[d], preferred_element_type=jnp.float32)
            total = term if total is None else total + term
        return total

    hidden = (jax.nn.silu(product(gate_parts)) * product(up_parts)).astype(jnp.bfloat16)
    branch = jnp.sum(hidden.astype(jnp.float32) * v_unit[None, :], axis=-1)
    at_home = jnp.sum(token_f * w_score, axis=-1)
    first_device = (group == 0) & (stretch == 0) & (band == 0)
    partial = branch + jnp.where(first_device, at_home, 0.0)
    partial = partial.reshape(n_sample, n_stretch * frames, clips)
    lens_all = len_slot.reshape(n_sample, 1, clips)
    counted = jnp.arange(n_stretch * frames, dtype=jnp.int32)[None, :, None] < lens_all
    slot_part = jnp.sum(jnp.where(counted, partial, 0.0), axis=1).reshape(-1)
    slot_part = slot_part / len_slot.astype(jnp.float32)
    clip_part = jnp.sum(jnp.where(slot_is, slot_part[:, None], 0.0), axis=0)
    scores = jnp.sum(spread(clip_part, ALL), axis=0)
    return (decoded_out, scores)


def solution(mesh):
    in_specs = (
        P("sample", "stretch", "band", None),
        P(),
        P(),
        P(),
        P(),
        P(),
        P(),
        P(),
        P(),
        P(),
        P("sample", ("stretch", "band")),
        P("sample", ("stretch", "band")),
        P(("stretch", "band"), "sample"),
        P(),
    )
    out_specs = (P("sample", "stretch", "band", None), P())
    return jax.shard_map(body, mesh=mesh, in_specs=in_specs, out_specs=out_specs, check_vma=False)
```

time: 90.8 us -> 92 us (1.013)
  waiting for transfers between devices: 16.2 us -> 26.2 us
  blocking collectives: 0 us -> 7.29 us
  Pallas kernels: 25.4 us -> 19.8 us
  starting transfers between devices: 27.1 us -> 22.5 us
  local copies, waits for them, and re-layouts: 12.6 us -> 8.98 us
  other arithmetic: 3.58 us -> 2.44 us
  matrix products: 4.24 us -> 3.26 us
    all_to_all x1, waiting for transfers between devices: 1.13 us -> 11.9 us  [body(): got = lax.all_to_all(outgoing, ('sample', 'band'), 0, 0, tiled=True)]
    all_to_all x0 -> x1, blocking collectives: none -> 7.29 us  [body(): parts = lax.all_to_all(band_sum, 'band', 0, 0, tiled=True)]
    all_to_all x2, waiting for transfers between devices: 7.21 us -> 14.3 us  [spread(): lax.all_to_all(jnp.broadcast_to(value[None], (count,) + value.shape), axe...]
    ppermute x3, waiting for transfers between devices: 5.69 us -> 0.01 us  [the longest x2 0.01 us: body(): lax.ppermute(latents, 'stretch', [(i, i + d) for i in range(n_stretch - d)])]
    pallas_call x1, Pallas kernels: 25.4 us -> 19.8 us  [decode(): pl.pallas_call(functools.partial(decode_kernel, frames=frames, rows=rows,...]
    all_to_all x1 -> x0, starting transfers between devices: 3.28 us -> none  [body(): parts = lax.all_to_all(band_sum, 'band', 0, 0, tiled=True)]
    unnamed x25 -> x21, local copies, waits for them, and re-layouts: 5.73 us -> 2.46 us
    all_to_all x1 -> x0, waiting for transfers between devices: 2.17 us -> none  [body(): parts = lax.all_to_all(band_sum, 'band', 0, 0, tiled=True)]
  transfers between devices with their start and end apart: 9 -> 8, of which waited for: 6 -> 3; matrix products, arithmetic and copies ran while one was open for 11% -> 9% of each run, Pallas kernels for 28% -> 22%
where the time goes in v3:
time: 92 us; the launch traced here: 91.4 us
  waiting for transfers between devices  26.2 us (28%)
  starting transfers between devices  22.5 us (24%)
  Pallas kernels  19.8 us (22%)
  local copies, waits for them, and re-layouts  8.98 us (10%)
  blocking collectives  7.29 us (8%)
  matrix products  3.26 us (4%)
  other arithmetic  2.44 us (3%)
  between operations  0.97 us (1%)
    pallas_call x1, Pallas kernels, decode(): pl.pallas_call(functools.partial(decode_kernel, frames=frames, rows=rows,...  19.8 us
    all_to_all x2, waiting for transfers between devices, spread(): lax.all_to_all(jnp.broadcast_to(value[None], (count,) + value.shape), axe...  14.3 us
    all_to_all x1, waiting for transfers between devices, body(): got = lax.all_to_all(outgoing, ('sample', 'band'), 0, 0, tiled=True)  11.9 us
    ppermute x2, starting transfers between devices, body(): lax.ppermute(latents, 'stretch', [(i, i + d) for i in range(n_stretch - d)])  9.56 us
    all_to_all x1, blocking collectives, body(): parts = lax.all_to_all(band_sum, 'band', 0, 0, tiled=True)  7.29 us
    all_to_all x2, starting transfers between devices, spread(): lax.all_to_all(jnp.broadcast_to(value[None], (count,) + value.shape), axe...  5.14 us
    all_to_all x1, starting transfers between devices, body(): got = lax.all_to_all(outgoing, ('sample', 'band'), 0, 0, tiled=True)  3.72 us
    dynamic_slice x3, local copies, waits for them, and re-layouts, of_units(): return lax.dynamic_slice_in_dim(weight, index * units, units, axis=axis)  2.92 us
  transfers between devices with their start and end apart: 8, of which 3 were waited for; matrix products, arithmetic and copies ran while one was open for 9% of the time, Pallas kernels for 22%

profile of v3, /device:TPU:0, one launch (start us, length us, event | category | flops | bytes accessed | tf_op | source)
XLA Modules:
  0.0 91.4 jit_solution(3924340327123662077)
XLA Ops:
  0.7 5.1 %collective-permute-start.1 = (bf16[16,2,4,128]{3,2,1,0:T(4,128)(2,1)}, bf16[16,2,4,128]{3,2,1,0:T(4,128)(2,1)S(1)}, u32[]{:S(2)}, u32[]{:S(2)}) collective-permute-start(bf16[16,2,4,128]{3,2,1,0:T(4,128)(2,1)} %param.14), channel_id=1, source_target_pairs={{0,4},{4,8},{8,12},{1,5},{5,9},{9,13},{2,6},{6,10},{10,14},{3,7},{... | collective-permute-start | bytes 98312 | tf_op jit(solution)/shard_map/ppermute | solution.py:215
  5.8 4.5 %collective-permute-start = (bf16[16,2,4,128]{3,2,1,0:T(4,128)(2,1)}, bf16[16,2,4,128]{3,2,1,0:T(4,128)(2,1)S(1)}, u32[]{:S(2)}, u32[]{:S(2)}) collective-permute-start(bf16[16,2,4,128]{3,2,1,0:T(4,128)(2,1)} %param.14), channel_id=1, source_target_pairs={{0,8},{4,12},{1,9},{5,13},{2,10},{6,14},{3,11},{7,15},{16,24},{20,... | collective-permute-start | bytes 98312 | tf_op jit(solution)/shard_map/ppermute | solution.py:215
  10.3 1.0 %constant_dynamic-slice_fusion.1 = bf16[768,280]{0,1:T(8,128)(2,1)S(1)} fusion(bf16[768,560]{0,1:T(8,128)(2,1)} %param.24, s32[]{:T(128)S(6)} %select_n.86), kind=kLoop, calls=%fused_computation.42 | loop fusion | bytes 860164 | tf_op jit(solution)/shard_map/dynamic_slice | solution.py:245
  11.3 1.6 %collective-permute-start.2 = (bf16[768,280]{0,1:T(8,128)(2,1)S(1)}, bf16[768,280]{0,1:T(8,128)(2,1)S(1)}, u32[]{:S(2)}, u32[]{:S(2)}) collective-permute-start(bf16[768,280]{0,1:T(8,128)(2,1)S(1)} %constant_dynamic-slice_fusion.1), channel_id=1, source_target_pairs={{0,16},{16,0},{1,17},{17,1},{2,18},{18,2},{3,19},{19,3},{4,20},{20... | collective-permute-start | bytes 1290248 | tf_op jit(solution)/shard_map/ppermute | solution.py:257
  12.9 1.8 %constant_dynamic-slice_fusion = bf16[768,280]{0,1:T(8,128)(2,1)} fusion(bf16[768,560]{0,1:T(8,128)(2,1)} %param.25, s32[]{:T(128)S(6)} %select_n.86), kind=kLoop, calls=%fused_computation.41 | loop fusion | bytes 860164 | tf_op jit(solution)/shard_map/dynamic_slice | solution.py:245
  14.7 0.5 collective-permute-start.3
  15.8 0.2 maximum_select_fusion
  16.0 0.2 fusion.1
  16.3 0.8 broadcast_in_dim.105
  17.1 3.7 %all-to-all-start = ((bf16[8,6,4,8,128]{4,3,2,1,0:T(8,128)(2,1)}), bf16[8,6,4,8,128]{4,3,2,1,0:T(8,128)(2,1)S(1)}, u32[]{:S(2)}, u32[]{:S(2)}) async-start(bf16[8,6,4,8,128]{4,3,2,1,0:T(8,128)(2,1)} %bitcast.9), calls=%async_computation | async-start | bytes 786432 | tf_op jit(solution)/shard_map/all_to_all | solution.py:236
  20.8 0.3 multiply_reduce_fusion
  21.1 2.0 %collective-permute-start.4 = (f32[280]{0:T(512)S(1)}, f32[280]{0:T(512)S(1)}, u32[]{:S(2)}, u32[]{:S(2)}) collective-permute-start(f32[280]{0:T(512)S(1)} %dynamic_slice.40), channel_id=1, source_target_pairs={{0,16},{16,0},{1,17},{17,1},{2,18},{18,2},{3,19},{19,3},{4,20},{20... | collective-permute-start | bytes 3368 | tf_op jit(solution)/shard_map/ppermute | solution.py:259
  23.4 0.6 pad_add_fusion.scalar_ref
  24.0 11.9 %all-to-all-done = bf16[8,6,4,8,128]{4,3,2,1,0:T(8,128)(2,1)S(1)} async-done(((bf16[8,6,4,8,128]{4,3,2,1,0:T(8,128)(2,1)}), bf16[8,6,4,8,128]{4,3,2,1,0:T(8,128)(2,1)S(1)}, u32[]{:S(2)}, u32[]{:S(2)}) %all-to-all-start) | async-done | bytes 393248 | tf_op jit(solution)/shard_map/all_to_all | solution.py:236
  36.0 0.7 pad_dynamic-slice_fusion.lat_ref
  36.8 19.8 %decode.1 = (bf16[2,4,16,3072]{3,2,1,0:T(8,128)(2,1)}, f32[2,16,384]{2,1,0:T(8,128)}) custom-call(s32[20]{0:T(128)} %pad_add_fusion.scalar_ref, bf16[6,8,16,128]{3,2,1,0:T(8,128)(2,1)} %pad_dynamic-slice_fusion.lat_ref, bf16[432,384]{1,0:T(8,128)(2,1)} %w_in_ref.1, f32[384]{0:T(512)} %b_in_ref.1, f32[384]{0:T(512)} %gain_ref.1, ...), custom_call_target="tpu_custom_call" | custom-call | flops 8153726976 | bytes 65536 | tf_op jit(solution)/shard_map/decode/pallas_call | solution.py:154
  56.6 7.3 %all_to_all.21 = f32[4,8,384]{2,1,0:T(8,128)S(1)} all-to-all(f32[4,8,384]{2,1,0:T(8,128)} %bitcast.35), channel_id=1, replica_groups=mesh['sample'=2,'stretch'=4,'band'=4] {'band'}, dimensions={0} | all-to-all | bytes 98304 | tf_op jit(solution)/shard_map/all_to_all | solution.py:283
  63.9 0.7 broadcast_in_dim.106
  64.6 2.6 %all-to-all-start.2 = ((bf16[32,8,384]{2,1,0:T(8,128)(2,1)}), bf16[32,8,384]{2,1,0:T(8,128)(2,1)S(1)}, u32[]{:S(2)}, u32[]{:S(2)}) async-start(bf16[32,8,384]{2,1,0:T(8,128)(2,1)} %broadcast_in_dim.106), calls=%async_computation.2 | async-start | bytes 393216 | tf_op jit(solution)/shard_map/all_to_all | solution.py:180
  67.3 8.7 %all-to-all-done.2 = bf16[32,8,384]{2,1,0:T(8,128)(2,1)S(1)} async-done(((bf16[32,8,384]{2,1,0:T(8,128)(2,1)}), bf16[32,8,384]{2,1,0:T(8,128)(2,1)S(1)}, u32[]{:S(2)}, u32[]{:S(2)}) %all-to-all-start.2) | async-done | bytes 196640 | tf_op jit(solution)/shard_map/all_to_all | solution.py:180
  76.0 0.7 multiply_reduce_fusion.1
  76.8 0.2 multiply_convert_fusion
  77.0 0.9 %copy-done.1 = bf16[768,560]{0,1:T(8,128)(2,1)S(1)} copy-done((bf16[768,560]{0,1:T(8,128)(2,1)S(1)}, bf16[768,560]{0,1:T(8,128)(2,1)}, u32[]{:S(2)}) %copy-start.1) | copy-done | bytes 860184
  77.9 0.3 fusion.4
  78.2 0.3 fusion.2
  78.6 0.3 convolution_add_fusion.1
  78.9 1.4 %multiply_reduce_fusion.3 = f32[256]{0:T(256)S(1)} fusion(f32[280]{0:T(512)S(1)} %dynamic-slice_add_fusion, f32[256,280]{0,1:T(8,128)S(1)} %convolution_add_fusion.1, f32[256,280]{0,1:T(8,128)S(1)} %fusion.2, bf16[768,280]{0,1:T(8,128)(2,1)} %collective-permute-done.3, bf16[256,1536]{1,0:T(8,128)(2,1)S(1)} %multiply_convert_fusion, s32[]{:T(128)S(6)} %select_n.92), kind=kOutput, calls=%fused_computation.19 | convolution fusion | flops 110817024 | bytes 1399812 | tf_op jit(solution)/shard_map/dot_general | solution.py:297
  80.6 0.6 broadcast_in_dim.111
  81.2 2.6 %all-to-all-start.3 = ((f32[32,1,32]{2,1,0:T(1,128)}), f32[32,1,32]{2,1,0:T(1,128)S(1)}, u32[]{:S(2)}, u32[]{:S(2)}) async-start(f32[32,1,32]{2,1,0:T(1,128)} %broadcast_in_dim.111), calls=%async_computation.3 | async-start | bytes 32768 | tf_op jit(solution)/shard_map/all_to_all | solution.py:180
  83.8 1.5 %copy.31 = bf16[16,2,4,3072]{3,2,1,0:T(4,128)(2,1)} copy(bf16[16,2,4,3072]{3,0,2,1:T(8,128)(2,1)S(1)} %bitcast.33) | data formatting | bytes 1572864
  85.3 5.6 %all-to-all-done.3 = f32[32,1,32]{2,1,0:T(1,128)S(1)} async-done(((f32[32,1,32]{2,1,0:T(1,128)}), f32[32,1,32]{2,1,0:T(1,128)S(1)}, u32[]{:S(2)}, u32[]{:S(2)}) %all-to-all-start.3) | async-done | bytes 4128 | tf_op jit(solution)/shard_map/all_to_all | solution.py:180
  90.9 0.5 reduce_sum.109
  (51 shorter events, 1.6 us)
Async XLA Ops:
  0.6 75.4 %copy-start = (bf16[384,1536]{1,0:T(8,128)(2,1)S(1)}, bf16[384,1536]{1,0:T(8,128)(2,1)}, u32[]{:S(2)}) copy-start(bf16[384,1536]{1,0:T(8,128)(2,1)} %param.22) | copy-start | bytes 3538948
  0.6 15.2 %copy-start.5 = (bf16[16,2,4,128]{3,2,1,0:T(4,128)(2,1)S(1)}, bf16[16,2,4,128]{3,2,1,0:T(4,128)(2,1)}, u32[]{:S(2)}) copy-start(bf16[16,2,4,128]{3,2,1,0:T(4,128)(2,1)} %param.14) | copy-start | bytes 98308
  0.7 14.6 %copy-start.9 = (s32[32]{0:T(128)S(1)}, s32[32]{0:T(128)}, u32[]{:S(2)}) copy-start(s32[32]{0:T(128)} %param.16) | copy-start | bytes 388
  0.7 14.7 %copy-start.8 = (s32[32]{0:T(128)S(1)}, s32[32]{0:T(128)}, u32[]{:S(2)}) copy-start(s32[32]{0:T(128)} %param.15) | copy-start | bytes 388
  0.7 15.1 %copy-start.6 = (f32[1536]{0:T(1024)S(1)}, f32[1536]{0:T(1024)}, u32[]{:S(2)}) copy-start(f32[1536]{0:T(1024)} %param.27) | copy-start | bytes 18436
  0.7 15.1 %collective-permute-start.1 = (bf16[16,2,4,128]{3,2,1,0:T(4,128)(2,1)}, bf16[16,2,4,128]{3,2,1,0:T(4,128)(2,1)S(1)}, u32[]{:S(2)}, u32[]{:S(2)}) collective-permute-start(bf16[16,2,4,128]{3,2,1,0:T(4,128)(2,1)} %param.14), channel_id=1, source_target_pairs={{0,4},{4,8},{8,12},{1,5},{5,9},{9,13},{2,6},{6,10},{10,14},{3,7},{... | collective-permute-start | bytes 98312 | tf_op jit(solution)/shard_map/ppermute | solution.py:215
  5.8 10.1 %collective-permute-start = (bf16[16,2,4,128]{3,2,1,0:T(4,128)(2,1)}, bf16[16,2,4,128]{3,2,1,0:T(4,128)(2,1)S(1)}, u32[]{:S(2)}, u32[]{:S(2)}) collective-permute-start(bf16[16,2,4,128]{3,2,1,0:T(4,128)(2,1)} %param.14), channel_id=1, source_target_pairs={{0,8},{4,12},{1,9},{5,13},{2,10},{6,14},{3,11},{7,15},{16,24},{20,... | collective-permute-start | bytes 98312 | tf_op jit(solution)/shard_map/ppermute | solution.py:215
  11.3 9.5 %copy-start.3 = (bf16[560,768]{1,0:T(8,128)(2,1)S(1)}, bf16[560,768]{1,0:T(8,128)(2,1)}, u32[]{:S(2)}) copy-start(bf16[560,768]{1,0:T(8,128)(2,1)} %param.26) | copy-start | bytes 2580484
  11.3 45.2 %collective-permute-start.2 = (bf16[768,280]{0,1:T(8,128)(2,1)S(1)}, bf16[768,280]{0,1:T(8,128)(2,1)S(1)}, u32[]{:S(2)}, u32[]{:S(2)}) collective-permute-start(bf16[768,280]{0,1:T(8,128)(2,1)S(1)} %constant_dynamic-slice_fusion.1), channel_id=1, source_target_pairs={{0,16},{16,0},{1,17},{17,1},{2,18},{18,2},{3,19},{19,3},{4,20},{20... | collective-permute-start | bytes 1290248 | tf_op jit(solution)/shard_map/ppermute | solution.py:257
  14.7 41.8 %collective-permute-start.3 = (bf16[768,280]{0,1:T(8,128)(2,1)}, bf16[768,280]{0,1:T(8,128)(2,1)}, u32[]{:S(2)}, u32[]{:S(2)}) collective-permute-start(bf16[768,280]{0,1:T(8,128)(2,1)} %constant_dynamic-slice_fusion), channel_id=1, source_target_pairs={{0,16},{16,0},{1,17},{17,1},{2,18},{18,2},{3,19},{19,3},{4,20},{20... | collective-permute-start | bytes 1290248 | tf_op jit(solution)/shard_map/ppermute | solution.py:258
  17.1 18.9 %all-to-all-start = ((bf16[8,6,4,8,128]{4,3,2,1,0:T(8,128)(2,1)}), bf16[8,6,4,8,128]{4,3,2,1,0:T(8,128)(2,1)S(1)}, u32[]{:S(2)}, u32[]{:S(2)}) async-start(bf16[8,6,4,8,128]{4,3,2,1,0:T(8,128)(2,1)} %bitcast.9), calls=%async_computation | async-start | bytes 786432 | tf_op jit(solution)/shard_map/all_to_all | solution.py:236
  21.1 35.4 %collective-permute-start.4 = (f32[280]{0:T(512)S(1)}, f32[280]{0:T(512)S(1)}, u32[]{:S(2)}, u32[]{:S(2)}) collective-permute-start(f32[280]{0:T(512)S(1)} %dynamic_slice.40), channel_id=1, source_target_pairs={{0,16},{16,0},{1,17},{17,1},{2,18},{18,2},{3,19},{19,3},{4,20},{20... | collective-permute-start | bytes 3368 | tf_op jit(solution)/shard_map/ppermute | solution.py:259
  64.6 11.5 %all-to-all-start.2 = ((bf16[32,8,384]{2,1,0:T(8,128)(2,1)}), bf16[32,8,384]{2,1,0:T(8,128)(2,1)S(1)}, u32[]{:S(2)}, u32[]{:S(2)}) async-start(bf16[32,8,384]{2,1,0:T(8,128)(2,1)} %broadcast_in_dim.106), calls=%async_computation.2 | async-start | bytes 393216 | tf_op jit(solution)/shard_map/all_to_all | solution.py:180
  67.1 9.6 %copy-start.7 = (f32[1536]{0:T(1024)S(1)}, f32[1536]{0:T(1024)}, u32[]{:S(2)}) copy-start(f32[1536]{0:T(1024)} %param.23) | copy-start | bytes 18436
  76.7 1.2 %copy-start.1 = (bf16[768,560]{0,1:T(8,128)(2,1)S(1)}, bf16[768,560]{0,1:T(8,128)(2,1)}, u32[]{:S(2)}) copy-start(bf16[768,560]{0,1:T(8,128)(2,1)} %param.24) | copy-start | bytes 2580484
  76.8 1.5 %copy-start.2 = (bf16[768,560]{0,1:T(8,128)(2,1)S(1)}, bf16[768,560]{0,1:T(8,128)(2,1)}, u32[]{:S(2)}) copy-start(bf16[768,560]{0,1:T(8,128)(2,1)} %param.25) | copy-start | bytes 2580484
  78.5 5.2 %copy-start.4 = (bf16[2,4,16,3072]{3,2,1,0:T(8,128)(2,1)S(1)}, bf16[2,4,16,3072]{3,2,1,0:T(8,128)(2,1)}, u32[]{:S(2)}) copy-start(bf16[2,4,16,3072]{3,2,1,0:T(8,128)(2,1)} %get-tuple-element.8) | copy-start | bytes 2359300
  81.2 9.7 %all-to-all-start.3 = ((f32[32,1,32]{2,1,0:T(1,128)}), f32[32,1,32]{2,1,0:T(1,128)S(1)}, u32[]{:S(2)}, u32[]{:S(2)}) async-start(f32[32,1,32]{2,1,0:T(1,128)} %broadcast_in_dim.111), calls=%async_computation.3 | async-start | bytes 32768 | tf_op jit(solution)/shard_map/all_to_all | solution.py:180

commit v4 on v3

--- a/solution.py
+++ b/solution.py
@@ -52,18 +52,16 @@
                 f + dt, dr : dr + rows_act
             ].reshape(per_frame, lanes)
     wt_ref[...] = jnp.zeros_like(wt_ref)
+    for q in range(widths):
+        for j in range(9):
+            wt_ref[q, j, q * chans_lat : (q + 3) * chans_lat, :] = w_in_ref[
+                j * 3 * chans_lat : (j + 1) * 3 * chans_lat, :
+            ]
     act_ref[:, :, 0] = jnp.zeros((frames_act, rows_act, clips, chans), jnp.bfloat16)
     act_ref[:, :, widths + 1] = jnp.zeros((frames_act, rows_act, clips, chans), jnp.bfloat16)
 
     def column(q, carry):
-        here = pl.multiple_of(q * chans_lat, chans_lat)
-        before = pl.multiple_of(jnp.maximum(q - 1, 0) * chans_lat, chans_lat)
-        for j in range(9):
-            wt_ref[j, pl.ds(before, chans_lat), :] = jnp.zeros((chans_lat, chans), jnp.bfloat16)
-            wt_ref[j, pl.ds(here, 3 * chans_lat), :] = w_in_ref[
-                j * 3 * chans_lat : (j + 1) * 3 * chans_lat, :
-            ]
-        weight = wt_ref[:, chans_lat : chans_lat + lanes, :].reshape(9 * lanes, chans)
+        weight = wt_ref[q, :, chans_lat : chans_lat + lanes, :].reshape(9 * lanes, chans)
         total = jnp.dot(x1_ref[...], weight, preferred_element_type=jnp.float32)
         first = (total + b_in).astype(jnp.bfloat16)
         values = first.astype(jnp.float32)
@@ -76,7 +74,7 @@
         ]
         return carry
 
-    lax.fori_loop(0, widths, column, 0)
+    lax.fori_loop(0, widths, column, 0, unroll=True)
 
     @pl.when(scalar_ref[0] == 1)
     def _():
@@ -135,7 +133,7 @@
             pool_ref[t] = pooled
         return carry
 
-    lax.fori_loop(0, rows, line, 0)
+    lax.fori_loop(0, rows, line, 0, unroll=2)
 
 
 VMEM = pl.BlockSpec(memory_space=pltpu.VMEM)
@@ -161,7 +159,7 @@
         out_specs=(VMEM, VMEM),
         scratch_shapes=[
             pltpu.VMEM((frames_act * rows_act * clips, 9 * lanes), jnp.bfloat16),
-            pltpu.VMEM((9, lanes + 2 * chans_lat, chans), jnp.bfloat16),
+            pltpu.VMEM((widths, 9, lanes + 2 * chans_lat, chans), jnp.bfloat16),
             pltpu.VMEM((frames_act, rows_act, widths + 2, clips, chans), jnp.bfloat16),
             pltpu.VMEM((frames, rows, widths, clips, chans), jnp.bfloat16),
             pltpu.VMEM(w_mid.shape, jnp.bfloat16),
@@ -217,9 +215,10 @@
     ] + [latents]
     series = jnp.concatenate(series, axis=1)[:, hops * frames - BEHIND :]
     all_frames = frames + BEHIND
-    is_group = jnp.arange(n_sample, dtype=jnp.int32)[:, None] == group
-    my_dest = jnp.sum(jnp.where(is_group, dest_slot.reshape(n_sample, clips), 0), axis=0)
-    my_len = jnp.sum(jnp.where(is_group, lengths.reshape(n_sample, clips), 0), axis=0)
+    ids = jnp.arange(all_clips, dtype=jnp.int32)
+    mine = ids[None, :] == (group * clips + jnp.arange(clips, dtype=jnp.int32))[:, None]
+    my_dest = jnp.sum(jnp.where(mine, dest_slot[None, :], 0), axis=1)
+    my_len = jnp.sum(jnp.where(mine, lengths[None, :], 0), axis=1)
     target = jnp.arange(n_sample, dtype=jnp.int32)[:, None] * clips + group * sends
     target = (target + jnp.arange(sends, dtype=jnp.int32)[None, :]).reshape(-1)
     select = (target[:, None] == my_dest[None, :]).astype(jnp.bfloat16)
@@ -233,30 +232,33 @@
     outgoing = jnp.broadcast_to(
         routed[:, None], (n_sample, n_band, all_frames, rows, sends, lanes)
     ).reshape(n_sample * n_band, all_frames, rows, sends, lanes)
+    units = w_gate.shape[1] // n_sample
+
+    def of_units(weight, index, axis):
+        return lax.dynamic_slice_in_dim(weight, index * units, units, axis=axis)
+
+    others = [(group + d) % n_sample for d in range(1, n_sample)]
+    outbound = [
+        jnp.concatenate([of_units(w_gate.T, i, 0), of_units(w_up.T, i, 0)], axis=0) for i in others
+    ]
+    outgoing, outbound = lax.optimization_barrier((outgoing, outbound))
     got = lax.all_to_all(outgoing, ("sample", "band"), 0, 0, tiled=True)
     got = got.reshape(n_sample, n_band, all_frames, rows, sends, lanes)
     got = got.transpose(2, 1, 3, 0, 4, 5).reshape(all_frames, n_band * rows, clips, lanes)
     got = jnp.pad(got, ((0, 0), (2, 2), (0, 0), (0, 0)))
     cells = lax.dynamic_slice_in_dim(got, band * rows, rows + 4, axis=1)
 
-    units = w_gate.shape[1] // n_sample
-
-    def of_units(weight, index, axis):
-        return lax.dynamic_slice_in_dim(weight, index * units, units, axis=axis)
-
     own_v = jnp.sum(
         w_down.astype(jnp.float32)
         * lax.dynamic_slice_in_dim(w_score, group * w_down.shape[1], w_down.shape[1])[None, :],
         axis=-1,
     )
     depth = w_gate.shape[0]
-    gate_parts, up_parts, v_parts = [], [], []
+    arrived, v_parts = [], []
     for d in range(1, n_sample):
         route = [(i, (i + d) % n_sample) for i in range(n_sample)]
-        other = (group + d) % n_sample
-        gate_parts.append(lax.ppermute(of_units(w_gate, other, 1), "sample", route))
-        up_parts.append(lax.ppermute(of_units(w_up, other, 1), "sample", route))
-        v_parts.append(lax.ppermute(of_units(own_v, other, 0), "sample", route))
+        arrived.append(lax.ppermute(outbound[d - 1], "sample", route))
+        v_parts.append(lax.ppermute(of_units(own_v, others[d - 1], 0), "sample", route))
 
     slot_is = dest_slot[None, :] == jnp.arange(all_clips, dtype=jnp.int32)[:, None]
     len_slot = jnp.sum(jnp.where(slot_is, lengths[None, :], 0), axis=1)
@@ -271,17 +273,16 @@
     decoded, band_sum = decode(
         scalars, cells, w_in, b_in, gain_mid, w_mid, b_mid, frames, rows, widths
     )
-    band_sum, gate_parts, up_parts, v_parts = lax.optimization_barrier(
-        (band_sum, gate_parts, up_parts, v_parts)
-    )
-    gate_parts = [of_units(w_gate, group, 1)] + gate_parts
-    up_parts = [of_units(w_up, group, 1)] + up_parts
-    v_unit = of_units(own_v, group, 0) + sum(v_parts)
     decoded_out = decoded.transpose(2, 0, 1, 3)
 
+    band_sum, v_parts = lax.optimization_barrier((band_sum, v_parts))
     band_sum = band_sum.reshape(n_band, frames * clips // n_band, chans)
     parts = lax.all_to_all(band_sum, "band", 0, 0, tiled=True)
     pooled = jnp.sum(parts, axis=0) / (rows * n_band * widths)
+    pooled, arrived = lax.optimization_barrier((pooled, arrived))
+    gate_parts = [of_units(w_gate, group, 1)] + [w[:units].T for w in arrived]
+    up_parts = [of_units(w_up, group, 1)] + [w[units:].T for w in arrived]
+    v_unit = of_units(own_v, group, 0) + sum(v_parts)
     pooled = spread(pooled.astype(jnp.bfloat16), ALL).reshape(-1, chans)
     tokens = jnp.dot(pooled, w_proj, preferred_element_type=jnp.float32).astype(jnp.bfloat16)
     token_f = tokens.astype(jnp.float32)

time: 92 us -> 77.7 us (0.84)
  waiting for transfers between devices: 26.2 us -> 18.8 us
  Pallas kernels: 19.8 us -> 16.8 us
  local copies, waits for them, and re-layouts: 8.98 us -> 7.18 us
  starting transfers between devices: 22.5 us -> 20.7 us
  matrix products: 3.26 us -> 2.24 us
    all_to_all x1, waiting for transfers between devices: 11.9 us -> 4.66 us  [body(): got = lax.all_to_all(outgoing, ('sample', 'band'), 0, 0, tiled=True)]
    pallas_call x1, Pallas kernels: 19.8 us -> 16.8 us  [decode(): pl.pallas_call(functools.partial(decode_kernel, frames=frames, rows=rows,...]
    ppermute x3 -> x2, starting transfers between devices: 4.11 us -> 2.06 us  [the longest x1 2.02 us: body(): lax.ppermute(of_units(own_v, others[d - 1], 0), 'sample', route)]
    dynamic_slice x3 -> x2, local copies, waits for them, and re-layouts: 2.92 us -> 1.3 us  [of_units(): return lax.dynamic_slice_in_dim(weight, index * units, units, axis=axis)]
    dot_general x4, matrix products: 2.33 us -> 1.33 us  [product(): term = jnp.dot(rows_here, parts[d], preferred_element_type=jnp.float32)]
  transfers between devices with their start and end apart: 8 -> 7, of which waited for: 3 -> 3; matrix products, arithmetic and copies ran while one was open for 9% -> 8% of each run, Pallas kernels for 22% -> 22%
where the time goes in v4:
time: 77.7 us; the launch traced here: 77.3 us
  starting transfers between devices  20.7 us (27%)
  waiting for transfers between devices  18.8 us (24%)
  Pallas kernels  16.8 us (22%)
  blocking collectives  7.29 us (9%)
  local copies, waits for them, and re-layouts  7.18 us (9%)
  other arithmetic  3.27 us (4%)
  matrix products  2.24 us (3%)
  between operations  0.97 us (1%)
    pallas_call x1, Pallas kernels, decode(): pl.pallas_call(functools.partial(decode_kernel, frames=frames, rows=rows,...  16.8 us
    all_to_all x2, waiting for transfers between devices, spread(): lax.all_to_all(jnp.broadcast_to(value[None], (count,) + value.shape), axe...  14.1 us
    ppermute x2, starting transfers between devices, body(): lax.ppermute(latents, 'stretch', [(i, i + d) for i in range(n_stretch - d)])  9.56 us
    all_to_all x1, blocking collectives, body(): parts = lax.all_to_all(band_sum, 'band', 0, 0, tiled=True)  7.29 us
    all_to_all x2, starting transfers between devices, spread(): lax.all_to_all(jnp.broadcast_to(value[None], (count,) + value.shape), axe...  5.32 us
    all_to_all x1, waiting for transfers between devices, body(): got = lax.all_to_all(outgoing, ('sample', 'band'), 0, 0, tiled=True)  4.66 us
    all_to_all x1, starting transfers between devices, body(): got = lax.all_to_all(outgoing, ('sample', 'band'), 0, 0, tiled=True)  3.72 us
    unnamed x21, local copies, waits for them, and re-layouts  2.46 us
  transfers between devices with their start and end apart: 7, of which 3 were waited for; matrix products, arithmetic and copies ran while one was open for 8% of the time, Pallas kernels for 22%

profile of v4, /device:TPU:0, one launch (start us, length us, event | category | flops | bytes accessed | tf_op | source)
XLA Modules:
  0.0 77.3 jit_solution(8786556664513813349)
XLA Ops:
  0.6 6.1 %collective-permute-start = (bf16[16,2,4,128]{3,2,1,0:T(4,128)(2,1)}, bf16[16,2,4,128]{3,2,1,0:T(4,128)(2,1)S(1)}, u32[]{:S(2)}, u32[]{:S(2)}) collective-permute-start(bf16[16,2,4,128]{3,2,1,0:T(4,128)(2,1)} %param.14), channel_id=1, source_target_pairs={{0,8},{4,12},{1,9},{5,13},{2,10},{6,14},{3,11},{7,15},{16,24},{20,... | collective-permute-start | bytes 98312 | tf_op jit(solution)/shard_map/ppermute | solution.py:213
  6.7 3.5 %collective-permute-start.1 = (bf16[16,2,4,128]{3,2,1,0:T(4,128)(2,1)}, bf16[16,2,4,128]{3,2,1,0:T(4,128)(2,1)S(1)}, u32[]{:S(2)}, u32[]{:S(2)}) collective-permute-start(bf16[16,2,4,128]{3,2,1,0:T(4,128)(2,1)} %param.14), channel_id=1, source_target_pairs={{0,4},{4,8},{8,12},{1,5},{5,9},{9,13},{2,6},{6,10},{10,14},{3,7},{... | collective-permute-start | bytes 98312 | tf_op jit(solution)/shard_map/ppermute | solution.py:213
  10.4 0.9 %select_reduce_fusion.3 = (s32[16]{0:T(128)S(1)}, s32[16]{0:T(128)S(1)}) fusion(s32[32]{0:T(128)} %param.16, s32[16]{0:T(128)S(1)} %iota_add_fusion.1, s32[32]{0:T(128)} %param.15), kind=kLoop, calls=%fused_computation.37 | loop fusion | flops 2528 | bytes 448 | tf_op jit(solution)/shard_map/reduce_sum | solution.py:220
  11.3 1.2 %dynamic-slice_bitcast_fusion = (bf16[280,768]{1,0:T(8,128)(2,1)S(1)}, bf16[280,768]{1,0:T(8,128)(2,1)S(1)}) fusion(bf16[768,560]{0,1:T(8,128)(2,1)} %param.25, s32[]{:T(128)S(6)} %select_n.85, bf16[768,560]{0,1:T(8,128)(2,1)} %param.24), kind=kLoop, calls=%fused_computation.23 | loop fusion | bytes 1720324 | tf_op jit(solution)/shard_map/dynamic_slice | solution.py:238
  12.8 0.2 maximum_select_fusion
  13.0 0.2 fusion.6
  13.2 0.8 %broadcast_in_dim.111 = bf16[2,4,6,4,8,128]{5,4,3,2,1,0:T(8,128)(2,1)} broadcast(bf16[2,6,4,8,128]{4,3,2,1,0:T(8,128)(2,1)S(1)} %copy.28), dimensions={0,2,3,4,5} | broadcast | bytes 491520 | tf_op jit(solution)/shard_map/broadcast_in_dim | solution.py:232
  14.0 3.7 %all-to-all-start = ((bf16[8,6,4,8,128]{4,3,2,1,0:T(8,128)(2,1)}), bf16[8,6,4,8,128]{4,3,2,1,0:T(8,128)(2,1)S(1)}, u32[]{:S(2)}, u32[]{:S(2)}) async-start(bf16[8,6,4,8,128]{4,3,2,1,0:T(8,128)(2,1)} %bitcast.9), calls=%async_computation | async-start | bytes 786432 | tf_op jit(solution)/shard_map/all_to_all | solution.py:245
  17.8 0.3 multiply_reduce_fusion
  18.1 2.0 %collective-permute-start.2 = (f32[280]{0:T(512)S(1)}, f32[280]{0:T(512)S(1)}, u32[]{:S(2)}, u32[]{:S(2)}) collective-permute-start(f32[280]{0:T(512)S(1)} %dynamic_slice.40), channel_id=1, source_target_pairs={{0,16},{16,0},{1,17},{17,1},{2,18},{18,2},{3,19},{19,3},{4,20},{20... | collective-permute-start | bytes 3368 | tf_op jit(solution)/shard_map/ppermute | solution.py:261
  20.1 0.1 select_reduce_fusion.1
  20.4 0.6 pad_add_fusion.scalar_ref
  21.1 4.7 %all-to-all-done = bf16[8,6,4,8,128]{4,3,2,1,0:T(8,128)(2,1)S(1)} async-done(((bf16[8,6,4,8,128]{4,3,2,1,0:T(8,128)(2,1)}), bf16[8,6,4,8,128]{4,3,2,1,0:T(8,128)(2,1)S(1)}, u32[]{:S(2)}, u32[]{:S(2)}) %all-to-all-start) | async-done | bytes 393248 | tf_op jit(solution)/shard_map/all_to_all | solution.py:245
  25.7 0.1 copy.29
  25.8 0.7 pad_dynamic-slice_fusion.lat_ref
  26.5 16.8 %decode.1 = (bf16[2,4,16,3072]{3,2,1,0:T(8,128)(2,1)}, f32[2,16,384]{2,1,0:T(8,128)}) custom-call(s32[20]{0:T(128)} %pad_add_fusion.scalar_ref, bf16[6,8,16,128]{3,2,1,0:T(8,128)(2,1)} %pad_dynamic-slice_fusion.lat_ref, bf16[432,384]{1,0:T(8,128)(2,1)} %w_in_ref.1, f32[384]{0:T(512)} %b_in_ref.1, f32[384]{0:T(512)} %gain_ref.1, ...), custom_call_target="tpu_custom_call" | custom-call | flops 8153726976 | bytes 65536 | tf_op jit(solution)/shard_map/decode/pallas_call | solution.py:152
  43.4 7.3 %all_to_all.21 = f32[4,8,384]{2,1,0:T(8,128)S(1)} all-to-all(f32[4,8,384]{2,1,0:T(8,128)} %bitcast.37), channel_id=1, replica_groups=mesh['sample'=2,'stretch'=4,'band'=4] {'band'}, dimensions={0} | all-to-all | bytes 98304 | tf_op jit(solution)/shard_map/all_to_all | solution.py:280
  50.7 0.7 broadcast_in_dim.112
  51.4 2.8 %all-to-all-start.2 = ((bf16[32,8,384]{2,1,0:T(8,128)(2,1)}), bf16[32,8,384]{2,1,0:T(8,128)(2,1)S(1)}, u32[]{:S(2)}, u32[]{:S(2)}) async-start(bf16[32,8,384]{2,1,0:T(8,128)(2,1)} %broadcast_in_dim.112), calls=%async_computation.2 | async-start | bytes 393216 | tf_op jit(solution)/shard_map/all_to_all | solution.py:178
  54.4 8.5 %all-to-all-done.2 = bf16[32,8,384]{2,1,0:T(8,128)(2,1)S(1)} async-done(((bf16[32,8,384]{2,1,0:T(8,128)(2,1)}), bf16[32,8,384]{2,1,0:T(8,128)(2,1)S(1)}, u32[]{:S(2)}, u32[]{:S(2)}) %all-to-all-start.2) | async-done | bytes 196640 | tf_op jit(solution)/shard_map/all_to_all | solution.py:178
  62.8 0.7 multiply_reduce_fusion.1
  63.6 0.2 multiply_convert_fusion
  63.8 0.9 %copy-done.1 = bf16[768,560]{0,1:T(8,128)(2,1)S(1)} copy-done((bf16[768,560]{0,1:T(8,128)(2,1)S(1)}, bf16[768,560]{0,1:T(8,128)(2,1)}, u32[]{:S(2)}) %copy-start.1) | copy-done | bytes 860184
  64.7 0.3 fusion.8
  65.0 0.3 fusion.11
  65.4 0.3 convolution_add_fusion.1
  65.7 0.4 fusion.5
  66.4 0.6 broadcast_in_dim.117
  67.0 2.6 %all-to-all-start.3 = ((f32[32,1,32]{2,1,0:T(1,128)}), f32[32,1,32]{2,1,0:T(1,128)S(1)}, u32[]{:S(2)}, u32[]{:S(2)}) async-start(f32[32,1,32]{2,1,0:T(1,128)} %broadcast_in_dim.117), calls=%async_computation.3 | async-start | bytes 32768 | tf_op jit(solution)/shard_map/all_to_all | solution.py:178
  69.6 1.5 %copy.31 = bf16[16,2,4,3072]{3,2,1,0:T(4,128)(2,1)} copy(bf16[16,2,4,3072]{3,0,2,1:T(8,128)(2,1)S(1)} %bitcast.35) | data formatting | bytes 1572864
  71.1 5.6 %all-to-all-done.3 = f32[32,1,32]{2,1,0:T(1,128)S(1)} async-done(((f32[32,1,32]{2,1,0:T(1,128)}), f32[32,1,32]{2,1,0:T(1,128)S(1)}, u32[]{:S(2)}, u32[]{:S(2)}) %all-to-all-start.3) | async-done | bytes 4128 | tf_op jit(solution)/shard_map/all_to_all | solution.py:178
  76.7 0.5 reduce_sum.109
  (47 shorter events, 1.2 us)
Async XLA Ops:
  0.6 62.2 %copy-start = (bf16[384,1536]{1,0:T(8,128)(2,1)S(1)}, bf16[384,1536]{1,0:T(8,128)(2,1)}, u32[]{:S(2)}) copy-start(bf16[384,1536]{1,0:T(8,128)(2,1)} %param.22) | copy-start | bytes 3538948
  0.6 12.1 %collective-permute-start = (bf16[16,2,4,128]{3,2,1,0:T(4,128)(2,1)}, bf16[16,2,4,128]{3,2,1,0:T(4,128)(2,1)S(1)}, u32[]{:S(2)}, u32[]{:S(2)}) collective-permute-start(bf16[16,2,4,128]{3,2,1,0:T(4,128)(2,1)} %param.14), channel_id=1, source_target_pairs={{0,8},{4,12},{1,9},{5,13},{2,10},{6,14},{3,11},{7,15},{16,24},{20,... | collective-permute-start | bytes 98312 | tf_op jit(solution)/shard_map/ppermute | solution.py:213
  6.7 6.1 %collective-permute-start.1 = (bf16[16,2,4,128]{3,2,1,0:T(4,128)(2,1)}, bf16[16,2,4,128]{3,2,1,0:T(4,128)(2,1)S(1)}, u32[]{:S(2)}, u32[]{:S(2)}) collective-permute-start(bf16[16,2,4,128]{3,2,1,0:T(4,128)(2,1)} %param.14), channel_id=1, source_target_pairs={{0,4},{4,8},{8,12},{1,5},{5,9},{9,13},{2,6},{6,10},{10,14},{3,7},{... | collective-permute-start | bytes 98312 | tf_op jit(solution)/shard_map/ppermute | solution.py:213
  11.3 1.4 %copy-start.6 = (f32[1536]{0:T(1024)S(1)}, f32[1536]{0:T(1024)}, u32[]{:S(2)}) copy-start(f32[1536]{0:T(1024)} %param.27) | copy-start | bytes 18436
  11.3 1.5 %copy-start.5 = (bf16[16,2,4,128]{3,2,1,0:T(4,128)(2,1)S(1)}, bf16[16,2,4,128]{3,2,1,0:T(4,128)(2,1)}, u32[]{:S(2)}) copy-start(bf16[16,2,4,128]{3,2,1,0:T(4,128)(2,1)} %param.14) | copy-start | bytes 98308
  12.5 5.2 %copy-start.3 = (bf16[560,768]{1,0:T(8,128)(2,1)S(1)}, bf16[560,768]{1,0:T(8,128)(2,1)}, u32[]{:S(2)}) copy-start(bf16[560,768]{1,0:T(8,128)(2,1)} %param.26) | copy-start | bytes 2580484
  12.6 7.5 %copy-start.8 = (s32[32]{0:T(128)S(1)}, s32[32]{0:T(128)}, u32[]{:S(2)}) copy-start(s32[32]{0:T(128)} %param.15) | copy-start | bytes 388
  12.6 7.5 %copy-start.9 = (s32[32]{0:T(128)S(1)}, s32[32]{0:T(128)}, u32[]{:S(2)}) copy-start(s32[32]{0:T(128)} %param.16) | copy-start | bytes 388
  14.0 11.7 %all-to-all-start = ((bf16[8,6,4,8,128]{4,3,2,1,0:T(8,128)(2,1)}), bf16[8,6,4,8,128]{4,3,2,1,0:T(8,128)(2,1)S(1)}, u32[]{:S(2)}, u32[]{:S(2)}) async-start(bf16[8,6,4,8,128]{4,3,2,1,0:T(8,128)(2,1)} %bitcast.9), calls=%async_computation | async-start | bytes 786432 | tf_op jit(solution)/shard_map/all_to_all | solution.py:245
  18.1 25.3 %collective-permute-start.2 = (f32[280]{0:T(512)S(1)}, f32[280]{0:T(512)S(1)}, u32[]{:S(2)}, u32[]{:S(2)}) collective-permute-start(f32[280]{0:T(512)S(1)} %dynamic_slice.40), channel_id=1, source_target_pairs={{0,16},{16,0},{1,17},{17,1},{2,18},{18,2},{3,19},{19,3},{4,20},{20... | collective-permute-start | bytes 3368 | tf_op jit(solution)/shard_map/ppermute | solution.py:261
  21.0 29.7 %collective-permute-start.3 = (bf16[560,768]{1,0:T(8,128)(2,1)S(1)}, bf16[560,768]{1,0:T(8,128)(2,1)S(1)}, u32[]{:S(2)}, u32[]{:S(2)}) collective-permute-start(bf16[560,768]{1,0:T(8,128)(2,1)S(1)} %pad_maximum_fusion), channel_id=1, source_target_pairs={{0,16},{16,0},{1,17},{17,1},{2,18},{18,2},{3,19},{19,3},{4,20},{20... | collective-permute-start | bytes 2580488 | tf_op jit(solution)/shard_map/ppermute | solution.py:260
  51.4 11.5 %all-to-all-start.2 = ((bf16[32,8,384]{2,1,0:T(8,128)(2,1)}), bf16[32,8,384]{2,1,0:T(8,128)(2,1)S(1)}, u32[]{:S(2)}, u32[]{:S(2)}) async-start(bf16[32,8,384]{2,1,0:T(8,128)(2,1)} %broadcast_in_dim.112), calls=%async_computation.2 | async-start | bytes 393216 | tf_op jit(solution)/shard_map/all_to_all | solution.py:178
  54.1 9.4 %copy-start.7 = (f32[1536]{0:T(1024)S(1)}, f32[1536]{0:T(1024)}, u32[]{:S(2)}) copy-start(f32[1536]{0:T(1024)} %param.23) | copy-start | bytes 18436
  63.5 1.2 %copy-start.1 = (bf16[768,560]{0,1:T(8,128)(2,1)S(1)}, bf16[768,560]{0,1:T(8,128)(2,1)}, u32[]{:S(2)}) copy-start(bf16[768,560]{0,1:T(8,128)(2,1)} %param.25) | copy-start | bytes 2580484
  63.6 1.5 %copy-start.2 = (bf16[768,560]{0,1:T(8,128)(2,1)S(1)}, bf16[768,560]{0,1:T(8,128)(2,1)}, u32[]{:S(2)}) copy-start(bf16[768,560]{0,1:T(8,128)(2,1)} %param.24) | copy-start | bytes 2580484
  65.7 3.9 %copy-start.4 = (bf16[2,4,16,3072]{3,2,1,0:T(8,128)(2,1)S(1)}, bf16[2,4,16,3072]{3,2,1,0:T(8,128)(2,1)}, u32[]{:S(2)}) copy-start(bf16[2,4,16,3072]{3,2,1,0:T(8,128)(2,1)} %get-tuple-element.11) | copy-start | bytes 2359300
  67.0 9.7 %all-to-all-start.3 = ((f32[32,1,32]{2,1,0:T(1,128)}), f32[32,1,32]{2,1,0:T(1,128)S(1)}, u32[]{:S(2)}, u32[]{:S(2)}) async-start(f32[32,1,32]{2,1,0:T(1,128)} %broadcast_in_dim.117), calls=%async_computation.3 | async-start | bytes 32768 | tf_op jit(solution)/shard_map/all_to_all | solution.py:178

commit v5 on v4

--- a/solution.py
+++ b/solution.py
@@ -10,6 +10,7 @@
 ALL = ("sample", "stretch", "band")
 TAPS = 3
 BEHIND = 2 * (TAPS - 1)
+STEP = 2
 
 
 def decode_kernel(
@@ -52,16 +53,17 @@
                 f + dt, dr : dr + rows_act
             ].reshape(per_frame, lanes)
     wt_ref[...] = jnp.zeros_like(wt_ref)
-    for q in range(widths):
-        for j in range(9):
-            wt_ref[q, j, q * chans_lat : (q + 3) * chans_lat, :] = w_in_ref[
-                j * 3 * chans_lat : (j + 1) * 3 * chans_lat, :
-            ]
+    middle = lanes - chans_lat
+    for j in range(9):
+        wt_ref[j, middle : middle + 3 * chans_lat, :] = w_in_ref[
+            j * 3 * chans_lat : (j + 1) * 3 * chans_lat, :
+        ]
     act_ref[:, :, 0] = jnp.zeros((frames_act, rows_act, clips, chans), jnp.bfloat16)
     act_ref[:, :, widths + 1] = jnp.zeros((frames_act, rows_act, clips, chans), jnp.bfloat16)
 
     def column(q, carry):
-        weight = wt_ref[q, :, chans_lat : chans_lat + lanes, :].reshape(9 * lanes, chans)
+        at = pl.multiple_of(lanes - q * chans_lat, chans_lat)
+        weight = wt_ref[:, pl.ds(at, lanes), :].reshape(9 * lanes, chans)
         total = jnp.dot(x1_ref[...], weight, preferred_element_type=jnp.float32)
         first = (total + b_in).astype(jnp.bfloat16)
         values = first.astype(jnp.float32)
@@ -91,7 +93,7 @@
         )
 
     weights_copy.wait()
-    cells = widths * clips
+    cells = STEP * widths * clips
     clip_ids = lax.broadcasted_iota(jnp.int32, (clips, chans), 0)
     lens = jnp.zeros((clips, chans), jnp.int32)
     for c in range(clips):
@@ -102,10 +104,12 @@
         totals = [None] * frames
         for f in range(frames_act):
             outs = [t for t in range(frames) if 0 <= f - t < TAPS]
-            for j in range(0, 9, 2):
-                taps = range(j, min(j + 2, 9))
+            for j in range(0, 9, 9):
+                taps = range(j, min(j + 9, 9))
                 lhs = [
-                    act_ref[f, r + k // 3, k % 3 : k % 3 + widths].reshape(cells, chans)
+                    act_ref[
+                        f, pl.ds(r * STEP + k // 3, STEP), k % 3 : k % 3 + widths
+                    ].reshape(cells, chans)
                     for k in taps
                 ]
                 lhs = lhs[0] if len(lhs) == 1 else jnp.concatenate(lhs, axis=-1)
@@ -121,19 +125,20 @@
         for t in range(frames):
             live = (scalar_ref[3] + t) < lens
             pooled = pool_ref[t]
-            for q in range(widths):
+            for i in range(STEP * widths):
+                line_at, q = divmod(i, widths)
                 mixed = (
-                    first_ref[t, r, q].astype(jnp.float32)
-                    + totals[t][q * clips : (q + 1) * clips, :]
+                    first_ref[t, r * STEP + line_at, q].astype(jnp.float32)
+                    + totals[t][i * clips : (i + 1) * clips, :]
                     + b_mid
                 )
                 done = jnp.where(live, mixed, 0.0).astype(jnp.bfloat16)
-                out_ref[t, r, :, q * chans : (q + 1) * chans] = done
+                out_ref[t, r * STEP + line_at, :, q * chans : (q + 1) * chans] = done
                 pooled = pooled + done.astype(jnp.float32)
             pool_ref[t] = pooled
         return carry
 
-    lax.fori_loop(0, rows, line, 0, unroll=2)
+    lax.fori_loop(0, rows // STEP, line, 0)
 
 
 VMEM = pl.BlockSpec(memory_space=pltpu.VMEM)
@@ -159,7 +164,7 @@
         out_specs=(VMEM, VMEM),
         scratch_shapes=[
             pltpu.VMEM((frames_act * rows_act * clips, 9 * lanes), jnp.bfloat16),
-            pltpu.VMEM((widths, 9, lanes + 2 * chans_lat, chans), jnp.bfloat16),
+            pltpu.VMEM((9, 2 * lanes, chans), jnp.bfloat16),
             pltpu.VMEM((frames_act, rows_act, widths + 2, clips, chans), jnp.bfloat16),
             pltpu.VMEM((frames, rows, widths, clips, chans), jnp.bfloat16),
             pltpu.VMEM(w_mid.shape, jnp.bfloat16),

time: 77.7 us -> 77.3 us (level)
  transfers between devices with their start and end apart: 7 -> 7, of which waited for: 3 -> 3; matrix products, arithmetic and copies ran while one was open for 8% -> 8% of each run, Pallas kernels for 22% -> 21%
where the time goes in v5:
time: 77.3 us; the launch traced here: 76.9 us
  starting transfers between devices  20.5 us (27%)
  waiting for transfers between devices  19 us (25%)
  Pallas kernels  16.4 us (21%)
  blocking collectives  7.29 us (9%)
  local copies, waits for them, and re-layouts  7.18 us (9%)
  other arithmetic  3.27 us (4%)
  matrix products  2.24 us (3%)
  between operations  0.97 us (1%)
    pallas_call x1, Pallas kernels, decode(): pl.pallas_call(functools.partial(decode_kernel, frames=frames, rows=rows,...  16.4 us
    all_to_all x2, waiting for transfers between devices, spread(): lax.all_to_all(jnp.broadcast_to(value[None], (count,) + value.shape), axe...  14.3 us
    ppermute x2, starting transfers between devices, body(): lax.ppermute(latents, 'stretch', [(i, i + d) for i in range(n_stretch - d)])  9.56 us
    all_to_all x1, blocking collectives, body(): parts = lax.all_to_all(band_sum, 'band', 0, 0, tiled=True)  7.29 us
    all_to_all x2, starting transfers between devices, spread(): lax.all_to_all(jnp.broadcast_to(value[None], (count,) + value.shape), axe...  5.14 us
    all_to_all x1, waiting for transfers between devices, body(): got = lax.all_to_all(outgoing, ('sample', 'band'), 0, 0, tiled=True)  4.66 us
    all_to_all x1, starting transfers between devices, body(): got = lax.all_to_all(outgoing, ('sample', 'band'), 0, 0, tiled=True)  3.72 us
    unnamed x21, local copies, waits for them, and re-layouts  2.46 us
  transfers between devices with their start and end apart: 7, of which 3 were waited for; matrix products, arithmetic and copies ran while one was open for 8% of the time, Pallas kernels for 21%

profile of v5, /device:TPU:0, one launch (start us, length us, event | category | flops | bytes accessed | tf_op | source)
XLA Modules:
  0.0 76.9 jit_solution(9297429728786550291)
XLA Ops:
  0.6 6.1 %collective-permute-start = (bf16[16,2,4,128]{3,2,1,0:T(4,128)(2,1)}, bf16[16,2,4,128]{3,2,1,0:T(4,128)(2,1)S(1)}, u32[]{:S(2)}, u32[]{:S(2)}) collective-permute-start(bf16[16,2,4,128]{3,2,1,0:T(4,128)(2,1)} %param.14), channel_id=1, source_target_pairs={{0,8},{4,12},{1,9},{5,13},{2,10},{6,14},{3,11},{7,15},{16,24},{20,... | collective-permute-start | bytes 98312 | tf_op jit(solution)/shard_map/ppermute | solution.py:218
  6.7 3.5 %collective-permute-start.1 = (bf16[16,2,4,128]{3,2,1,0:T(4,128)(2,1)}, bf16[16,2,4,128]{3,2,1,0:T(4,128)(2,1)S(1)}, u32[]{:S(2)}, u32[]{:S(2)}) collective-permute-start(bf16[16,2,4,128]{3,2,1,0:T(4,128)(2,1)} %param.14), channel_id=1, source_target_pairs={{0,4},{4,8},{8,12},{1,5},{5,9},{9,13},{2,6},{6,10},{10,14},{3,7},{... | collective-permute-start | bytes 98312 | tf_op jit(solution)/shard_map/ppermute | solution.py:218
  10.4 0.9 %select_reduce_fusion.3 = (s32[16]{0:T(128)S(1)}, s32[16]{0:T(128)S(1)}) fusion(s32[32]{0:T(128)} %param.16, s32[16]{0:T(128)S(1)} %iota_add_fusion.1, s32[32]{0:T(128)} %param.15), kind=kLoop, calls=%fused_computation.37 | loop fusion | flops 2528 | bytes 448 | tf_op jit(solution)/shard_map/reduce_sum | solution.py:225
  11.3 1.2 %dynamic-slice_bitcast_fusion = (bf16[280,768]{1,0:T(8,128)(2,1)S(1)}, bf16[280,768]{1,0:T(8,128)(2,1)S(1)}) fusion(bf16[768,560]{0,1:T(8,128)(2,1)} %param.25, s32[]{:T(128)S(6)} %select_n.85, bf16[768,560]{0,1:T(8,128)(2,1)} %param.24), kind=kLoop, calls=%fused_computation.23 | loop fusion | bytes 1720324 | tf_op jit(solution)/shard_map/dynamic_slice | solution.py:243
  12.8 0.2 maximum_select_fusion
  13.0 0.2 fusion.6
  13.2 0.8 %broadcast_in_dim.111 = bf16[2,4,6,4,8,128]{5,4,3,2,1,0:T(8,128)(2,1)} broadcast(bf16[2,6,4,8,128]{4,3,2,1,0:T(8,128)(2,1)S(1)} %copy.28), dimensions={0,2,3,4,5} | broadcast | bytes 491520 | tf_op jit(solution)/shard_map/broadcast_in_dim | solution.py:237
  14.0 3.7 %all-to-all-start = ((bf16[8,6,4,8,128]{4,3,2,1,0:T(8,128)(2,1)}), bf16[8,6,4,8,128]{4,3,2,1,0:T(8,128)(2,1)S(1)}, u32[]{:S(2)}, u32[]{:S(2)}) async-start(bf16[8,6,4,8,128]{4,3,2,1,0:T(8,128)(2,1)} %bitcast.9), calls=%async_computation | async-start | bytes 786432 | tf_op jit(solution)/shard_map/all_to_all | solution.py:250
  17.8 0.3 multiply_reduce_fusion
  18.1 2.0 %collective-permute-start.2 = (f32[280]{0:T(512)S(1)}, f32[280]{0:T(512)S(1)}, u32[]{:S(2)}, u32[]{:S(2)}) collective-permute-start(f32[280]{0:T(512)S(1)} %dynamic_slice.40), channel_id=1, source_target_pairs={{0,16},{16,0},{1,17},{17,1},{2,18},{18,2},{3,19},{19,3},{4,20},{20... | collective-permute-start | bytes 3368 | tf_op jit(solution)/shard_map/ppermute | solution.py:266
  20.1 0.1 select_reduce_fusion.1
  20.4 0.6 pad_add_fusion.scalar_ref
  21.1 4.7 %all-to-all-done = bf16[8,6,4,8,128]{4,3,2,1,0:T(8,128)(2,1)S(1)} async-done(((bf16[8,6,4,8,128]{4,3,2,1,0:T(8,128)(2,1)}), bf16[8,6,4,8,128]{4,3,2,1,0:T(8,128)(2,1)S(1)}, u32[]{:S(2)}, u32[]{:S(2)}) %all-to-all-start) | async-done | bytes 393248 | tf_op jit(solution)/shard_map/all_to_all | solution.py:250
  25.7 0.1 copy.29
  25.8 0.7 pad_dynamic-slice_fusion.lat_ref
  26.5 16.4 %decode.1 = (bf16[2,4,16,3072]{3,2,1,0:T(8,128)(2,1)}, f32[2,16,384]{2,1,0:T(8,128)}) custom-call(s32[20]{0:T(128)} %pad_add_fusion.scalar_ref, bf16[6,8,16,128]{3,2,1,0:T(8,128)(2,1)} %pad_dynamic-slice_fusion.lat_ref, bf16[432,384]{1,0:T(8,128)(2,1)} %w_in_ref.1, f32[384]{0:T(512)} %b_in_ref.1, f32[384]{0:T(512)} %gain_ref.1, ...), custom_call_target="tpu_custom_call" | custom-call | flops 8153726976 | bytes 65536 | tf_op jit(solution)/shard_map/decode/pallas_call | solution.py:157
  43.0 7.3 %all_to_all.21 = f32[4,8,384]{2,1,0:T(8,128)S(1)} all-to-all(f32[4,8,384]{2,1,0:T(8,128)} %bitcast.37), channel_id=1, replica_groups=mesh['sample'=2,'stretch'=4,'band'=4] {'band'}, dimensions={0} | all-to-all | bytes 98304 | tf_op jit(solution)/shard_map/all_to_all | solution.py:285
  50.3 0.7 broadcast_in_dim.112
  51.0 2.6 %all-to-all-start.2 = ((bf16[32,8,384]{2,1,0:T(8,128)(2,1)}), bf16[32,8,384]{2,1,0:T(8,128)(2,1)S(1)}, u32[]{:S(2)}, u32[]{:S(2)}) async-start(bf16[32,8,384]{2,1,0:T(8,128)(2,1)} %broadcast_in_dim.112), calls=%async_computation.2 | async-start | bytes 393216 | tf_op jit(solution)/shard_map/all_to_all | solution.py:183
  53.8 8.7 %all-to-all-done.2 = bf16[32,8,384]{2,1,0:T(8,128)(2,1)S(1)} async-done(((bf16[32,8,384]{2,1,0:T(8,128)(2,1)}), bf16[32,8,384]{2,1,0:T(8,128)(2,1)S(1)}, u32[]{:S(2)}, u32[]{:S(2)}) %all-to-all-start.2) | async-done | bytes 196640 | tf_op jit(solution)/shard_map/all_to_all | solution.py:183
  62.5 0.7 multiply_reduce_fusion.1
  63.2 0.2 multiply_convert_fusion
  63.4 0.9 %copy-done.1 = bf16[768,560]{0,1:T(8,128)(2,1)S(1)} copy-done((bf16[768,560]{0,1:T(8,128)(2,1)S(1)}, bf16[768,560]{0,1:T(8,128)(2,1)}, u32[]{:S(2)}) %copy-start.1) | copy-done | bytes 860184
  64.3 0.3 fusion.8
  64.6 0.3 fusion.11
  65.0 0.3 convolution_add_fusion.1
  65.3 0.4 fusion.5
  66.0 0.6 broadcast_in_dim.117
  66.6 2.6 %all-to-all-start.3 = ((f32[32,1,32]{2,1,0:T(1,128)}), f32[32,1,32]{2,1,0:T(1,128)S(1)}, u32[]{:S(2)}, u32[]{:S(2)}) async-start(f32[32,1,32]{2,1,0:T(1,128)} %broadcast_in_dim.117), calls=%async_computation.3 | async-start | bytes 32768 | tf_op jit(solution)/shard_map/all_to_all | solution.py:183
  69.2 1.5 %copy.31 = bf16[16,2,4,3072]{3,2,1,0:T(4,128)(2,1)} copy(bf16[16,2,4,3072]{3,0,2,1:T(8,128)(2,1)S(1)} %bitcast.35) | data formatting | bytes 1572864
  70.7 5.6 %all-to-all-done.3 = f32[32,1,32]{2,1,0:T(1,128)S(1)} async-done(((f32[32,1,32]{2,1,0:T(1,128)}), f32[32,1,32]{2,1,0:T(1,128)S(1)}, u32[]{:S(2)}, u32[]{:S(2)}) %all-to-all-start.3) | async-done | bytes 4128 | tf_op jit(solution)/shard_map/all_to_all | solution.py:183
  76.3 0.5 reduce_sum.109
  (47 shorter events, 1.2 us)
Async XLA Ops:
  0.6 61.8 %copy-start = (bf16[384,1536]{1,0:T(8,128)(2,1)S(1)}, bf16[384,1536]{1,0:T(8,128)(2,1)}, u32[]{:S(2)}) copy-start(bf16[384,1536]{1,0:T(8,128)(2,1)} %param.22) | copy-start | bytes 3538948
  0.6 12.1 %collective-permute-start = (bf16[16,2,4,128]{3,2,1,0:T(4,128)(2,1)}, bf16[16,2,4,128]{3,2,1,0:T(4,128)(2,1)S(1)}, u32[]{:S(2)}, u32[]{:S(2)}) collective-permute-start(bf16[16,2,4,128]{3,2,1,0:T(4,128)(2,1)} %param.14), channel_id=1, source_target_pairs={{0,8},{4,12},{1,9},{5,13},{2,10},{6,14},{3,11},{7,15},{16,24},{20,... | collective-permute-start | bytes 98312 | tf_op jit(solution)/shard_map/ppermute | solution.py:218
  6.7 6.1 %collective-permute-start.1 = (bf16[16,2,4,128]{3,2,1,0:T(4,128)(2,1)}, bf16[16,2,4,128]{3,2,1,0:T(4,128)(2,1)S(1)}, u32[]{:S(2)}, u32[]{:S(2)}) collective-permute-start(bf16[16,2,4,128]{3,2,1,0:T(4,128)(2,1)} %param.14), channel_id=1, source_target_pairs={{0,4},{4,8},{8,12},{1,5},{5,9},{9,13},{2,6},{6,10},{10,14},{3,7},{... | collective-permute-start | bytes 98312 | tf_op jit(solution)/shard_map/ppermute | solution.py:218
  11.3 1.4 %copy-start.6 = (f32[1536]{0:T(1024)S(1)}, f32[1536]{0:T(1024)}, u32[]{:S(2)}) copy-start(f32[1536]{0:T(1024)} %param.27) | copy-start | bytes 18436
  11.3 1.5 %copy-start.5 = (bf16[16,2,4,128]{3,2,1,0:T(4,128)(2,1)S(1)}, bf16[16,2,4,128]{3,2,1,0:T(4,128)(2,1)}, u32[]{:S(2)}) copy-start(bf16[16,2,4,128]{3,2,1,0:T(4,128)(2,1)} %param.14) | copy-start | bytes 98308
  12.5 5.2 %copy-start.3 = (bf16[560,768]{1,0:T(8,128)(2,1)S(1)}, bf16[560,768]{1,0:T(8,128)(2,1)}, u32[]{:S(2)}) copy-start(bf16[560,768]{1,0:T(8,128)(2,1)} %param.26) | copy-start | bytes 2580484
  12.6 7.5 %copy-start.8 = (s32[32]{0:T(128)S(1)}, s32[32]{0:T(128)}, u32[]{:S(2)}) copy-start(s32[32]{0:T(128)} %param.15) | copy-start | bytes 388
  12.6 7.5 %copy-start.9 = (s32[32]{0:T(128)S(1)}, s32[32]{0:T(128)}, u32[]{:S(2)}) copy-start(s32[32]{0:T(128)} %param.16) | copy-start | bytes 388
  14.0 11.7 %all-to-all-start = ((bf16[8,6,4,8,128]{4,3,2,1,0:T(8,128)(2,1)}), bf16[8,6,4,8,128]{4,3,2,1,0:T(8,128)(2,1)S(1)}, u32[]{:S(2)}, u32[]{:S(2)}) async-start(bf16[8,6,4,8,128]{4,3,2,1,0:T(8,128)(2,1)} %bitcast.9), calls=%async_computation | async-start | bytes 786432 | tf_op jit(solution)/shard_map/all_to_all | solution.py:250
  18.1 24.9 %collective-permute-start.2 = (f32[280]{0:T(512)S(1)}, f32[280]{0:T(512)S(1)}, u32[]{:S(2)}, u32[]{:S(2)}) collective-permute-start(f32[280]{0:T(512)S(1)} %dynamic_slice.40), channel_id=1, source_target_pairs={{0,16},{16,0},{1,17},{17,1},{2,18},{18,2},{3,19},{19,3},{4,20},{20... | collective-permute-start | bytes 3368 | tf_op jit(solution)/shard_map/ppermute | solution.py:266
  21.0 29.3 %collective-permute-start.3 = (bf16[560,768]{1,0:T(8,128)(2,1)S(1)}, bf16[560,768]{1,0:T(8,128)(2,1)S(1)}, u32[]{:S(2)}, u32[]{:S(2)}) collective-permute-start(bf16[560,768]{1,0:T(8,128)(2,1)S(1)} %pad_maximum_fusion), channel_id=1, source_target_pairs={{0,16},{16,0},{1,17},{17,1},{2,18},{18,2},{3,19},{19,3},{4,20},{20... | collective-permute-start | bytes 2580488 | tf_op jit(solution)/shard_map/ppermute | solution.py:265
  51.0 11.5 %all-to-all-start.2 = ((bf16[32,8,384]{2,1,0:T(8,128)(2,1)}), bf16[32,8,384]{2,1,0:T(8,128)(2,1)S(1)}, u32[]{:S(2)}, u32[]{:S(2)}) async-start(bf16[32,8,384]{2,1,0:T(8,128)(2,1)} %broadcast_in_dim.112), calls=%async_computation.2 | async-start | bytes 393216 | tf_op jit(solution)/shard_map/all_to_all | solution.py:183
  53.6 9.6 %copy-start.7 = (f32[1536]{0:T(1024)S(1)}, f32[1536]{0:T(1024)}, u32[]{:S(2)}) copy-start(f32[1536]{0:T(1024)} %param.23) | copy-start | bytes 18436
  63.2 1.2 %copy-start.1 = (bf16[768,560]{0,1:T(8,128)(2,1)S(1)}, bf16[768,560]{0,1:T(8,128)(2,1)}, u32[]{:S(2)}) copy-start(bf16[768,560]{0,1:T(8,128)(2,1)} %param.25) | copy-start | bytes 2580484
  63.2 1.5 %copy-start.2 = (bf16[768,560]{0,1:T(8,128)(2,1)S(1)}, bf16[768,560]{0,1:T(8,128)(2,1)}, u32[]{:S(2)}) copy-start(bf16[768,560]{0,1:T(8,128)(2,1)} %param.24) | copy-start | bytes 2580484
  65.3 3.9 %copy-start.4 = (bf16[2,4,16,3072]{3,2,1,0:T(8,128)(2,1)S(1)}, bf16[2,4,16,3072]{3,2,1,0:T(8,128)(2,1)}, u32[]{:S(2)}) copy-start(bf16[2,4,16,3072]{3,2,1,0:T(8,128)(2,1)} %get-tuple-element.11) | copy-start | bytes 2359300
  66.6 9.7 %all-to-all-start.3 = ((f32[32,1,32]{2,1,0:T(1,128)}), f32[32,1,32]{2,1,0:T(1,128)S(1)}, u32[]{:S(2)}, u32[]{:S(2)}) async-start(f32[32,1,32]{2,1,0:T(1,128)} %broadcast_in_dim.117), calls=%async_computation.3 | async-start | bytes 32768 | tf_op jit(solution)/shard_map/all_to_all | solution.py:183
